TPU v7x, 32 devices: a whole 2x2x4 slice. The times are simulated.
32 devices in a mesh: head: 4 (over y, core), blk: 8 (over z, x).
Axes of the slice: x: 2, y: 2, z: 4, core: 2. Of those that a mesh axis runs over, the one named last changes fastest.
Arguments:
- tokens: bfloat16 [4096, 768], P(('head', 'blk')), may hold values from -6 to 6
- prev_logits: float32 [4096, 12], P(('head', 'blk')), may hold values from -4 to 4
- norm_gains: bfloat16 [2, 2, 768], P(None, None, ('head', 'blk')), may hold values from 0.5 to 1.5
- attn_in_weight: bfloat16 [2, 768, 2304], P(None, ('head', 'blk')), may hold values from -0.21875 to 0.21875
- attn_out_weight: bfloat16 [2, 768, 768], P(None, ('head', 'blk')), may hold values from -0.75 to 0.75
- router_weight: bfloat16 [2, 768, 12], P(None, ('head', 'blk')), may hold values from -0.14941406 to 0.14941406
- const_mix: bfloat16 [2, 768, 4], P(None, ('head', 'blk')), may hold values from -0.21875 to 0.21875
- const_values: bfloat16 [2, 2, 768], P(None, None, ('head', 'blk')), may hold values from -6 to 6
- expert_gate: bfloat16 [2, 8, 768, 2048], P(None, 'head', 'blk'), may hold values from -0.21875 to 0.21875
- expert_up: bfloat16 [2, 8, 768, 2048], P(None, 'head', 'blk'), may hold values from -0.21875 to 0.21875
- expert_down: bfloat16 [2, 8, 768, 2048], P(None, 'head', 'blk'), may hold values from -0.25 to 0.25
- routes: int32 [2, 4096, 2], P(None, ('head', 'blk')), may hold values from 0 to 11, all different within a row
- order: int32 [2, 4096, 2], P(None, ('head', 'blk')), may hold values from 0 to 255, as said below
- cotangent: bfloat16 [4096, 768], P(('head', 'blk')), may hold values from -6 to 6
Outputs:
- output: bfloat16 [4096, 768], P(('head', 'blk'))
- input_grad: float32 [4096, 768], P(('head', 'blk'))
- logits_grad: float32 [4096, 12], P(('head', 'blk'))
- gains_grad: float32 [2, 2, 768], P(None, None, ('head', 'blk'))
- attn_in_grad: float32 [2, 768, 2304], P(None, ('head', 'blk'))
- attn_out_grad: float32 [2, 768, 768], P(None, ('head', 'blk'))
- router_grad: float32 [2, 768, 12], P(None, ('head', 'blk'))
- mix_grad: float32 [2, 768, 4], P(None, ('head', 'blk'))
- values_grad: float32 [2, 2, 768], P(None, None, ('head', 'blk'))
- gate_grad: float32 [2, 8, 768, 2048], P(None, 'head', 'blk')
- up_grad: float32 [2, 8, 768, 2048], P(None, 'head', 'blk')
- down_grad: float32 [2, 8, 768, 2048], P(None, 'head', 'blk')
Inputs may be any that keep to these rules, and one draw needn't show every extreme that they name: `routes`: each token names two different experts; ids 8, 9, 10 and 11 are the zero, copy and two constant experts. `order`: within each layer and each aligned block of 128 tokens, the 256 entries are each of 0 to 255 once.
All inputs are finite; a program needn't handle non-finite values.
Results may differ from a plain program's by a relative error of at most 0.039.
Values may be sent and summed in bfloat16 or wider, within the bound.
A program may use at most 320 MiB of HBM per device.

v0:
```python
from functools import partial

import jax
import jax.numpy as jnp
from jax import lax
from jax.sharding import PartitionSpec as P

HEADS = 12
HD = 64
NF = 8
TOP = 2
LAYERS = 2
NE = 12
CAP = 26


EPSILON = 1e-05
HIGH = lax.Precision.HIGHEST
NEGATIVE = -1e30
SCORE_FORM = {True: "sqhd,skhd->hsqk", False: "qhd,khd->hqk"}
FORWARD_OUT = {True: "hsqk,skhd->hsqd", False: "hqk,khd->hqd"}
TO_QUERIES = {True: "hsqk,skhd->sqhd", False: "hqk,khd->qhd"}
TO_KEYS = {True: "hsqk,sqhd->skhd", False: "hqk,qhd->khd"}


def rms_norm(values, gain):
    return values * lax.rsqrt(jnp.mean(values * values, axis=-1, keepdims=True) + EPSILON) * gain


def rotary_tables(positions):
    freqs = 10000.0 ** (-jnp.arange(0, HD, 2, dtype=jnp.float32) / HD)
    angles = positions[:, None] * freqs[None, :]
    return (jnp.cos(angles)[:, None, :], jnp.sin(angles)[:, None, :])


def rotate(values, cosine, sine):
    half = HD // 2
    first = values[..., :half]
    second = values[..., half:]
    return jnp.concatenate(
        [first * cosine - second * sine, second * cosine + first * sine], axis=-1
    )


def swiglu(gate, upper):
    return jax.nn.silu(gate) * upper


def over_rows(update, carry, pieces, rows):
    count = pieces[0].shape[0]
    blocks = count // rows
    stacked = tuple((piece.reshape((blocks, rows) + piece.shape[1:]) for piece in pieces))

    def step(state, entry):
        number, parts = entry
        return (update(state, parts, number * rows), None)

    carry, _ = lax.scan(step, carry, (jnp.arange(blocks, dtype=jnp.int32), stacked))
    return carry


def piece_layout(start, count, local_rows, group_rows):
    index = start + jnp.arange(count, dtype=jnp.int32)
    return (index % group_rows // local_rows, index // group_rows * local_rows + index % local_rows)


def pair_mask(query_pos, key_pos, local_rows):
    allowed = key_pos[None, :local_rows] <= query_pos[:local_rows, None]
    return allowed[None, None]


def split_sets(values, sets):
    return values.reshape((sets, values.shape[0] // sets) + values.shape[1:])


def split_stat(stat, sets):
    return stat.reshape((stat.shape[0], sets, stat.shape[1] // sets) + stat.shape[2:])


def attend_block(
    carry,
    pieces,
    start,
    head_q,
    query_seq,
    query_pos,
    blk_index,
    local_rows,
    group_rows,
    scale,
    skip_masked,
):
    piece_keys, piece_values = pieces
    count = piece_keys.shape[0]
    heads = head_q.shape[1]
    sets = group_rows // local_rows
    grouped = count == group_rows
    key_seq, key_pos = piece_layout(start, count, local_rows, group_rows)
    mask = pair_mask(query_pos, key_pos, local_rows)
    query_part = split_sets(head_q, sets)
    key_part = split_sets(piece_keys.reshape(count, heads, HD), sets)
    value_part = split_sets(piece_values.reshape(count, heads, HD), sets)
    peak = split_stat(carry[0], sets)
    total = split_stat(carry[1], sets)
    weighted = split_stat(carry[2], sets)
    scores = (
        jnp.einsum(SCORE_FORM[grouped], query_part, key_part, preferred_element_type=jnp.float32)
        * scale
    )
    scores = jnp.where(mask, scores, NEGATIVE)
    new_peak = jnp.maximum(peak, jnp.max(scores, axis=-1))
    block_weights = jnp.where(mask, jnp.exp(scores - new_peak[..., None]), 0.0)
    factor = jnp.exp(peak - new_peak)
    total = total * factor + jnp.sum(block_weights, axis=-1)
    weighted = weighted * factor[..., None] + jnp.einsum(
        FORWARD_OUT[grouped],
        block_weights.astype(jnp.bfloat16),
        value_part,
        preferred_element_type=jnp.float32,
    )
    return (
        new_peak.reshape(heads, group_rows),
        total.reshape(heads, group_rows),
        weighted.reshape(heads, group_rows, HD),
    )


def grad_block(
    carry,
    pieces,
    start,
    local_parts,
    query_seq,
    query_pos,
    blk_index,
    local_rows,
    group_rows,
    scale,
    skip_masked,
):
    piece_keys, piece_values, piece_queries, piece_outgrad, piece_logsum, piece_delta = pieces
    local_queries, local_keys, local_values, local_outgrad, local_logsum, local_delta = local_parts
    count = piece_keys.shape[0]
    heads = local_queries.shape[1]
    sets = group_rows // local_rows
    grouped = count == group_rows
    piece_seq, piece_pos = piece_layout(start, count, local_rows, group_rows)

    def shaped(values):
        return split_sets(values.reshape(count, heads, HD), sets)

    def row_stat(stat):
        return split_stat(stat.T, sets)

    key_block = shaped(piece_keys)
    value_block = shaped(piece_values)
    query_block = shaped(piece_queries)
    outgrad_block = shaped(piece_outgrad)
    own_queries = split_sets(local_queries, sets)
    own_keys = split_sets(local_keys, sets)
    own_values = split_sets(local_values, sets)
    own_outgrad = split_sets(local_outgrad, sets)
    query_grad, key_grad, value_grad = carry
    mask = pair_mask(query_pos, piece_pos, local_rows)
    scores = (
        jnp.einsum(SCORE_FORM[grouped], own_queries, key_block, preferred_element_type=jnp.float32)
        * scale
    )
    block_weights = jnp.where(mask, jnp.exp(scores - row_stat(local_logsum)[..., None]), 0.0)
    weight_grad = jnp.einsum(
        SCORE_FORM[grouped], own_outgrad, value_block, preferred_element_type=jnp.float32
    )
    score_grad = (block_weights * (weight_grad - row_stat(local_delta)[..., None])).astype(
        jnp.bfloat16
    )
    added = jnp.einsum(
        TO_QUERIES[grouped], score_grad, key_block, preferred_element_type=jnp.float32
    )
    query_grad = query_grad + scale * added.reshape(group_rows, heads, HD)
    towards_key_grad = key_grad
    towards_value_grad = value_grad
    mask = pair_mask(piece_pos, query_pos, local_rows)
    scores = (
        jnp.einsum(SCORE_FORM[grouped], query_block, own_keys, preferred_element_type=jnp.float32)
        * scale
    )
    block_weights = jnp.where(mask, jnp.exp(scores - row_stat(piece_logsum)[..., None]), 0.0)
    weight_grad = jnp.einsum(
        SCORE_FORM[grouped], outgrad_block, own_values, preferred_element_type=jnp.float32
    )
    score_grad = (block_weights * (weight_grad - row_stat(piece_delta)[..., None])).astype(
        jnp.bfloat16
    )
    value_add = jnp.einsum(
        TO_KEYS[grouped],
        block_weights.astype(jnp.bfloat16),
        outgrad_block,
        preferred_element_type=jnp.float32,
    )
    key_add = jnp.einsum(
        TO_KEYS[grouped], score_grad, query_block, preferred_element_type=jnp.float32
    )
    key_grad = towards_key_grad + scale * key_add.reshape(group_rows, heads, HD)
    value_grad = towards_value_grad + value_add.reshape(group_rows, heads, HD)
    return (query_grad, key_grad, value_grad)


def mixture(normed, logits, mix_weight, const_vals, slot_values, layer_routes, pair_select):
    picks = (layer_routes[:, :, None] == jnp.arange(NE, dtype=jnp.int32)).astype(jnp.float32)
    chosen = jnp.sum(picks * logits[:, None, :], axis=-1)
    gates = jax.nn.softmax(chosen, axis=-1)
    combine = jnp.einsum("stj,tj->ts", pair_select, gates, precision=HIGH)
    mixed = jnp.dot(combine, slot_values, precision=HIGH)
    copy_weight = jnp.sum(gates * picks[:, :, NF + 1], axis=-1)
    mixed = mixed + copy_weight[:, None] * normed
    for index in range(2):
        weight = jnp.sum(gates * picks[:, :, NF + 2 + index], axis=-1)
        shares = jax.nn.softmax(
            jnp.dot(normed, mix_weight[:, 2 * index : 2 * index + 2], precision=HIGH), axis=-1
        )
        const_out = shares[:, 0:1] * normed + shares[:, 1:2] * const_vals[index][None, :]
        mixed = mixed + weight[:, None] * const_out
    return mixed


def reduce_grads(
    in_grad, out_grad, router_grad, mix_grad, gain_grad, const_grad, gate_grad, up_grad, down_grad
):
    summed = (
        lax.psum_scatter(in_grad, ("head", "blk"), scatter_dimension=1, tiled=True),
        lax.psum_scatter(out_grad, ("head", "blk"), scatter_dimension=1, tiled=True),
        lax.psum_scatter(router_grad, ("head", "blk"), scatter_dimension=1, tiled=True),
        lax.psum_scatter(mix_grad, ("head", "blk"), scatter_dimension=1, tiled=True),
        lax.psum_scatter(gain_grad, ("head", "blk"), scatter_dimension=2, tiled=True),
        lax.psum_scatter(const_grad, ("head", "blk"), scatter_dimension=2, tiled=True),
    )
    expert_sums = (
        lax.psum_scatter(
            gate_grad.astype(jnp.bfloat16), "blk", scatter_dimension=2, tiled=True
        ).astype(jnp.float32),
        lax.psum_scatter(
            up_grad.astype(jnp.bfloat16), "blk", scatter_dimension=2, tiled=True
        ).astype(jnp.float32),
        lax.psum_scatter(
            down_grad.astype(jnp.bfloat16), "blk", scatter_dimension=2, tiled=True
        ).astype(jnp.float32),
    )
    return tuple(summed) + tuple(expert_sums)


def local(
    tokens,
    prev_logits,
    norm_gains,
    attn_in_weight,
    attn_out_weight,
    router_weight,
    const_mix,
    const_values,
    expert_gate,
    expert_up,
    expert_down,
    routes,
    order,
    cotangent,
):
    head_count = lax.axis_size("head")
    blk_index = lax.axis_index("blk")
    local_rows = tokens.shape[0]
    width = tokens.shape[1]
    group_rows = head_count * local_rows
    group_width = width // head_count
    group_heads = group_width // HD
    local_experts = expert_gate.shape[1]
    slot_count = NF * CAP
    scale = HD ** (-0.5)
    skip_masked = False
    token_pos = blk_index * local_rows + jnp.arange(local_rows, dtype=jnp.int32)
    cosine, sine = rotary_tables(token_pos.astype(jnp.float32))
    group_index = jnp.arange(group_rows, dtype=jnp.int32)
    query_seq = group_index // local_rows
    query_pos = blk_index * local_rows + group_index % local_rows

    def rotate_here(values):
        return rotate(values, cosine, sine)

    state = tokens.astype(jnp.float32)
    carried_logits = prev_logits
    saved = []
    for layer in range(LAYERS):
        in_weight, out_weight, router, mix_weight, gains, values_const = (
            lax.all_gather(attn_in_weight[layer], ("head", "blk"), axis=0, tiled=True),
            lax.all_gather(attn_out_weight[layer], ("head", "blk"), axis=0, tiled=True),
            lax.all_gather(router_weight[layer], ("head", "blk"), axis=0, tiled=True),
            lax.all_gather(const_mix[layer], ("head", "blk"), axis=0, tiled=True),
            lax.all_gather(norm_gains[layer], ("head", "blk"), axis=1, tiled=True),
            lax.all_gather(const_values[layer], ("head", "blk"), axis=1, tiled=True),
        )
        gate_weight, up_weight, down_weight = (
            lax.all_gather(expert_gate[layer], "blk", axis=1, tiled=True),
            lax.all_gather(expert_up[layer], "blk", axis=1, tiled=True),
            lax.all_gather(expert_down[layer], "blk", axis=1, tiled=True),
        )
        state_in = state
        normed = rms_norm(state, gains[0].astype(jnp.float32))
        normed_low = normed.astype(jnp.bfloat16)
        projected = jnp.dot(normed_low, in_weight, preferred_element_type=jnp.float32)
        queries = rotate_here(projected[:, :width].reshape(local_rows, HEADS, HD))
        keys = rotate_here(projected[:, width : 2 * width].reshape(local_rows, HEADS, HD))
        values = projected[:, 2 * width :]
        send_queries = queries.reshape(local_rows, head_count, group_width).astype(jnp.bfloat16)
        send_keys = keys.reshape(local_rows, head_count, group_width).astype(jnp.bfloat16)
        send_values = values.reshape(local_rows, head_count, group_width).astype(jnp.bfloat16)
        got_queries, got_keys, got_values = (
            lax.all_to_all(send_queries, "head", split_axis=1, concat_axis=0, tiled=True),
            lax.all_to_all(send_keys, "head", split_axis=1, concat_axis=0, tiled=True),
            lax.all_to_all(send_values, "head", split_axis=1, concat_axis=0, tiled=True),
        )
        got_queries = got_queries.reshape(group_rows, group_width)
        got_keys = got_keys.reshape(group_rows, group_width)
        got_values = got_values.reshape(group_rows, group_width)
        head_q = got_queries.reshape(group_rows, group_heads, HD)
        attend_update = partial(
            attend_block,
            head_q=head_q,
            query_seq=query_seq,
            query_pos=query_pos,
            blk_index=blk_index,
            local_rows=local_rows,
            group_rows=group_rows,
            scale=scale,
            skip_masked=skip_masked,
        )

        def attend_fold(carry, pieces, start, attend_update=attend_update):
            return over_rows(attend_update, carry, pieces, group_rows)

        start_state = (
            jnp.full((group_heads, group_rows), NEGATIVE, jnp.float32),
            jnp.zeros((group_heads, group_rows), jnp.float32),
            jnp.zeros((group_heads, group_rows, HD), jnp.float32),
        )
        peak, total, weighted = attend_fold(
            start_state,
            (
                lax.all_gather(got_keys, "blk", axis=0, tiled=True),
                lax.all_gather(got_values, "blk", axis=0, tiled=True),
            ),
            jnp.int32(0),
        )
        attended = weighted / total[:, :, None]
        log_total = peak + jnp.log(total)
        attended_rows = jnp.transpose(attended, (1, 0, 2))
        attended_low = attended_rows.reshape(group_rows, 1, group_width).astype(jnp.bfloat16)
        returned = lax.all_to_all(
            attended_low, "head", split_axis=0, concat_axis=1, tiled=True
        ).reshape(local_rows, width)
        middle = state + jnp.dot(returned, out_weight, preferred_element_type=jnp.float32)
        normed_two = rms_norm(middle, gains[1].astype(jnp.float32))
        normed_two_low = normed_two.astype(jnp.bfloat16)
        logits = (
            jnp.dot(normed_two_low, router, preferred_element_type=jnp.float32) + carried_logits
        )
        layer_routes = routes[layer]
        route_ids = layer_routes.reshape(-1)
        ranks = order[layer].reshape(-1)
        same = (route_ids[:, None] == route_ids[None, :]) & (ranks[None, :] < ranks[:, None])
        slot = jnp.sum(same.astype(jnp.int32), axis=1)
        kept = (route_ids < NF) & (slot < CAP)
        target = jnp.where(kept, route_ids * CAP + slot, -1)
        chosen_slots = (target[None, :] == jnp.arange(slot_count, dtype=jnp.int32)[:, None]).astype(
            jnp.float32
        )
        pair_select = chosen_slots.reshape(slot_count, local_rows, TOP)
        token_select = jnp.sum(pair_select, axis=2).astype(jnp.bfloat16)
        outgoing = jnp.dot(token_select, normed_two_low, preferred_element_type=jnp.float32).astype(
            jnp.bfloat16
        )
        outgoing = outgoing.reshape(head_count, local_experts, CAP, width)
        incoming = lax.all_to_all(outgoing, "head", split_axis=0, concat_axis=0, tiled=True)
        gate_pre = jnp.einsum(
            "sxcd,xdf->sxcf", incoming, gate_weight, preferred_element_type=jnp.float32
        )
        up_pre = jnp.einsum(
            "sxcd,xdf->sxcf", incoming, up_weight, preferred_element_type=jnp.float32
        )
        hidden = swiglu(gate_pre, up_pre).astype(jnp.bfloat16)
        produced = jnp.einsum(
            "sxcf,xdf->sxcd", hidden, down_weight, preferred_element_type=jnp.float32
        ).astype(jnp.bfloat16)
        results = lax.all_to_all(produced, "head", split_axis=0, concat_axis=0, tiled=True).reshape(
            slot_count, width
        )
        mixed = mixture(
            normed_two,
            logits,
            mix_weight.astype(jnp.float32),
            values_const.astype(jnp.float32),
            results.astype(jnp.float32),
            layer_routes,
            pair_select,
        )
        state = middle + mixed
        carried_logits = logits
        saved.append(
            (
                state_in,
                normed_low,
                in_weight,
                out_weight,
                router,
                mix_weight,
                gains,
                values_const,
                gate_weight,
                up_weight,
                down_weight,
                got_queries,
                got_keys,
                got_values,
                attended_rows,
                log_total,
                returned,
                middle,
                normed_two,
                normed_two_low,
                logits,
                layer_routes,
                pair_select,
                token_select,
                incoming,
                gate_pre,
                up_pre,
                results,
            )
        )
    grad_state = cotangent.astype(jnp.float32)
    grad_logits = jnp.zeros_like(prev_logits)
    layer_grads = []
    for layer in reversed(range(LAYERS)):
        (
            state_in,
            normed_low,
            in_weight,
            out_weight,
            router,
            mix_weight,
            gains,
            values_const,
            gate_weight,
            up_weight,
            down_weight,
            got_queries,
            got_keys,
            got_values,
            attended_rows,
            log_total,
            returned,
            middle,
            normed_two,
            normed_two_low,
            logits,
            layer_routes,
            pair_select,
            token_select,
            incoming,
            gate_pre,
            up_pre,
            results,
        ) = saved[layer]
        mix_part = partial(mixture, layer_routes=layer_routes, pair_select=pair_select)
        _, mix_pull = jax.vjp(
            mix_part,
            normed_two,
            logits,
            mix_weight.astype(jnp.float32),
            values_const.astype(jnp.float32),
            results.astype(jnp.float32),
        )
        normed_grad, logit_part, mix_grad, const_grad, slot_grad = mix_pull(grad_state)
        grad_logits = logit_part + grad_logits
        router_grad = jnp.dot(normed_two_low.astype(jnp.float32).T, grad_logits, precision=HIGH)
        normed_grad = normed_grad + jnp.dot(
            grad_logits, router.astype(jnp.float32).T, precision=HIGH
        )
        slot_low = slot_grad.astype(jnp.bfloat16).reshape(head_count, local_experts, CAP, width)
        slot_back = lax.all_to_all(slot_low, "head", split_axis=0, concat_axis=0, tiled=True)
        hidden_grad = jnp.einsum(
            "sxcd,xdf->sxcf", slot_back, down_weight, preferred_element_type=jnp.float32
        )
        _, swiglu_pull = jax.vjp(swiglu, gate_pre, up_pre)
        gate_part, up_part = swiglu_pull(hidden_grad)
        gate_low = gate_part.astype(jnp.bfloat16)
        up_low = up_part.astype(jnp.bfloat16)
        hidden = swiglu(gate_pre, up_pre).astype(jnp.bfloat16)
        down_grad = jnp.einsum(
            "sxcd,sxcf->xdf", slot_back, hidden, preferred_element_type=jnp.float32
        )
        gate_grad = jnp.einsum(
            "sxcd,sxcf->xdf", incoming, gate_low, preferred_element_type=jnp.float32
        )
        up_grad = jnp.einsum("sxcd,sxcf->xdf", incoming, up_low, preferred_element_type=jnp.float32)
        input_part = jnp.einsum(
            "sxcf,xdf->sxcd", gate_low, gate_weight, preferred_element_type=jnp.float32
        )
        input_part = input_part + jnp.einsum(
            "sxcf,xdf->sxcd", up_low, up_weight, preferred_element_type=jnp.float32
        )
        returned_grad = lax.all_to_all(
            input_part.astype(jnp.bfloat16), "head", split_axis=0, concat_axis=0, tiled=True
        ).reshape(slot_count, width)
        normed_grad = normed_grad + jnp.dot(
            token_select.T, returned_grad, preferred_element_type=jnp.float32
        )
        _, norm_pull = jax.vjp(rms_norm, middle, gains[1].astype(jnp.float32))
        middle_grad, gain_two = norm_pull(normed_grad)
        middle_grad = middle_grad + grad_state
        branch_grad = middle_grad.astype(jnp.bfloat16)
        out_grad = jnp.dot(returned.T, branch_grad, preferred_element_type=jnp.float32)
        attended_grad = jnp.dot(
            branch_grad, out_weight.T, preferred_element_type=jnp.float32
        ).astype(jnp.bfloat16)
        attended_grad = attended_grad.reshape(local_rows, head_count, group_width)
        head_grad = lax.all_to_all(
            attended_grad, "head", split_axis=1, concat_axis=0, tiled=True
        ).reshape(group_rows, group_width)
        head_grad_rows = head_grad.reshape(group_rows, group_heads, HD)
        delta_rows = jnp.sum(head_grad_rows.astype(jnp.float32) * attended_rows, axis=-1)
        logsum_rows = log_total.T
        local_parts = (
            got_queries.reshape(group_rows, group_heads, HD),
            got_keys.reshape(group_rows, group_heads, HD),
            got_values.reshape(group_rows, group_heads, HD),
            head_grad_rows,
            logsum_rows,
            delta_rows,
        )
        grad_update = partial(
            grad_block,
            local_parts=local_parts,
            query_seq=query_seq,
            query_pos=query_pos,
            blk_index=blk_index,
            local_rows=local_rows,
            group_rows=group_rows,
            scale=scale,
            skip_masked=skip_masked,
        )

        def grad_fold_rows(carry, pieces, start, grad_update=grad_update):
            return over_rows(grad_update, carry, pieces, group_rows)

        zero_grads = (
            jnp.zeros((group_rows, group_heads, HD), jnp.float32),
            jnp.zeros((group_rows, group_heads, HD), jnp.float32),
            jnp.zeros((group_rows, group_heads, HD), jnp.float32),
        )
        query_grad, key_grad, value_grad = grad_fold_rows(
            zero_grads,
            (
                lax.all_gather(got_keys, "blk", axis=0, tiled=True),
                lax.all_gather(got_values, "blk", axis=0, tiled=True),
                lax.all_gather(got_queries, "blk", axis=0, tiled=True),
                lax.all_gather(head_grad, "blk", axis=0, tiled=True),
                lax.all_gather(logsum_rows.astype(jnp.bfloat16), "blk", axis=0, tiled=True).astype(
                    jnp.float32
                ),
                lax.all_gather(delta_rows.astype(jnp.bfloat16), "blk", axis=0, tiled=True).astype(
                    jnp.float32
                ),
            ),
            jnp.int32(0),
        )
        back_queries, back_keys, back_values = (
            lax.all_to_all(
                query_grad.reshape(group_rows, 1, group_width).astype(jnp.bfloat16),
                "head",
                split_axis=0,
                concat_axis=1,
                tiled=True,
            ),
            lax.all_to_all(
                key_grad.reshape(group_rows, 1, group_width).astype(jnp.bfloat16),
                "head",
                split_axis=0,
                concat_axis=1,
                tiled=True,
            ),
            lax.all_to_all(
                value_grad.reshape(group_rows, 1, group_width).astype(jnp.bfloat16),
                "head",
                split_axis=0,
                concat_axis=1,
                tiled=True,
            ),
        )
        back_queries = back_queries.reshape(local_rows, HEADS, HD).astype(jnp.float32)
        back_keys = back_keys.reshape(local_rows, HEADS, HD).astype(jnp.float32)
        _, rotate_pull = jax.vjp(rotate_here, back_queries)
        query_lin = rotate_pull(back_queries)[0]
        key_lin = rotate_pull(back_keys)[0]
        projected_grad = jnp.concatenate(
            [
                query_lin.reshape(local_rows, width),
                key_lin.reshape(local_rows, width),
                back_values.reshape(local_rows, width).astype(jnp.float32),
            ],
            axis=1,
        ).astype(jnp.bfloat16)
        in_grad = jnp.dot(normed_low.T, projected_grad, preferred_element_type=jnp.float32)
        first_normed_grad = jnp.dot(projected_grad, in_weight.T, preferred_element_type=jnp.float32)
        _, first_pull = jax.vjp(rms_norm, state_in, gains[0].astype(jnp.float32))
        state_grad, gain_one = first_pull(first_normed_grad)
        grad_state = middle_grad + state_grad
        gain_grad = jnp.stack([gain_one, gain_two])
        entry = (
            in_grad[None],
            out_grad[None],
            router_grad[None],
            mix_grad[None],
            gain_grad[None],
            const_grad[None],
            gate_grad[None],
            up_grad[None],
            down_grad[None],
        )
        entry = reduce_grads(
            entry[0], entry[1], entry[2], entry[3], entry[4], entry[5], entry[6], entry[7], entry[8]
        )
        layer_grads.append(entry)
    ordered = layer_grads[::-1]
    reduced = tuple(
        (jnp.concatenate([grads[index] for grads in ordered], axis=0) for index in range(9))
    )
    return (
        state.astype(jnp.bfloat16),
        grad_state,
        grad_logits,
        reduced[4],
        reduced[0],
        reduced[1],
        reduced[2],
        reduced[3],
        reduced[5],
        reduced[6],
        reduced[7],
        reduced[8],
    )


def solution(mesh):
    placed = (
        P(("head", "blk"), None),
        P(("head", "blk"), None),
        P(None, None, ("head", "blk")),
        P(None, ("head", "blk"), None),
        P(None, ("head", "blk"), None),
        P(None, ("head", "blk"), None),
        P(None, ("head", "blk"), None),
        P(None, None, ("head", "blk")),
        P(None, "head", "blk", None),
        P(None, "head", "blk", None),
        P(None, "head", "blk", None),
        P(None, ("head", "blk"), None),
        P(None, ("head", "blk"), None),
        P(("head", "blk"), None),
    )
    return jax.shard_map(
        local,
        mesh=mesh,
        in_specs=placed,
        out_specs=(
            P(("head", "blk"), None),
            P(("head", "blk"), None),
            P(("head", "blk"), None),
            P(None, None, ("head", "blk")),
            P(None, ("head", "blk"), None),
            P(None, ("head", "blk"), None),
            P(None, ("head", "blk"), None),
            P(None, ("head", "blk"), None),
            P(None, None, ("head", "blk")),
            P(None, "head", "blk", None),
            P(None, "head", "blk", None),
            P(None, "head", "blk", None),
        ),
        check_vma=False,
    )
```

profile of v0, /device:TPU:8, one launch (start us, length us, event | category | flops | bytes accessed | tf_op | source)
XLA Modules:
  0.0 2967.6 jit_solution(2617642169777728144)
XLA Ops:
  9.8 68.5 %all-gather = bf16[1,2,768]{1,0,2:T(2,128)(2,1)S(1)} all-gather(bf16[1,2,24]{1,0,2:T(2,128)(2,1)S(1)} %copy.963), channel_id=2, replica_groups=mesh['head'=4,'blk'=8] {'head','blk'}, dimensions={2}, use_global_device_ids=true | all-gather | bytes 3168 | tf_op jit(solution)/shard_map/all_gather | solution.py:296
  118.9 66.9 %all-gather.9 = bf16[1,2,768]{1,0,2:T(2,128)(2,1)S(1)} all-gather(bf16[1,2,24]{1,0,2:T(2,128)(2,1)S(1)} %copy.968), channel_id=11, replica_groups=mesh['head'=4,'blk'=8] {'head','blk'}, dimensions={2}, use_global_device_ids=true | all-gather | bytes 3168 | tf_op jit(solution)/shard_map/all_gather | solution.py:296
  195.2 68.5 %all-gather.8 = bf16[1,2,768]{1,0,2:T(2,128)(2,1)S(1)} all-gather(bf16[1,2,24]{1,0,2:T(2,128)(2,1)S(1)} %copy.967), channel_id=10, replica_groups=mesh['head'=4,'blk'=8] {'head','blk'}, dimensions={2}, use_global_device_ids=true | all-gather | bytes 3168 | tf_op jit(solution)/shard_map/all_gather | solution.py:297
  271.1 69.8 %while.72 = (s32[]{:T(128)}, f32[3,512]{1,0:T(4,128)}, f32[3,512]{1,0:T(4,128)}, f32[3,512,64]{1,2,0:T(8,128)S(1)}, s32[8]{0:T(128)}, /*index=5*/s32[512]{0:T(51...) while((s32[]{:T(128)}, f32[3,512]{1,0:T(4,128)}, ...), condition=%wide.wide.region_4.5_spmd.clone, body=%wide.wide.region_1.4_spmd.clone.sunk | while | flops 52338180 | bytes 6356220 | solution.py:58
  352.7 69.6 %all-gather.7 = bf16[1,768,4]{2,0,1:T(2,128)(2,1)S(1)} all-gather(bf16[1,24,4]{2,0,1:T(2,128)(2,1)S(1)} %copy.966), channel_id=9, replica_groups=mesh['head'=4,'blk'=8] {'head','blk'}, dimensions={1}, use_global_device_ids=true | all-gather | bytes 6336 | tf_op jit(solution)/shard_map/all_gather | solution.py:295
  422.6 70.8 %all-gather.3 = bf16[1,768,12]{2,0,1:T(2,128)(2,1)S(1)} all-gather(bf16[1,24,12]{2,0,1:T(2,128)(2,1)S(1)} %copy.965), channel_id=5, replica_groups=mesh['head'=4,'blk'=8] {'head','blk'}, dimensions={1}, use_global_device_ids=true | all-gather | bytes 19008 | tf_op jit(solution)/shard_map/all_gather | solution.py:294
  519.7 33.4 %all-gather.61.cloned.1.call-done = bf16[1,2,768,2048]{3,2,1,0:T(8,128)(2,1)} async-done(((bf16[1,2,96,2048]{3,2,1,0:T(8,128)(2,1)}), bf16[1,2,768,2048]{3,2,1,0:T(8,128)(2,1)}) %all-gather.61.cloned.1.call-update) | async-done | bytes 6291472 | tf_op jit(solution)/shard_map/all_gather | solution.py:302
  571.5 44.6 %all-gather.63.cloned.1.call-done = bf16[1,768,2304]{2,1,0:T(8,128)(2,1)} async-done(((bf16[1,24,2304]{2,1,0:T(8,128)(2,1)}), bf16[1,768,2304]{2,1,0:T(8,128)(2,1)}) %all-gather.63.cloned.1.call-update) | async-done | bytes 3538960 | tf_op jit(solution)/shard_map/all_gather | solution.py:292
  621.0 7.9 all_to_all.270
  643.0 66.1 %all-gather.17 = bf16[1,2,768]{1,0,2:T(2,128)(2,1)S(1)} all-gather(bf16[1,2,24]{1,0,2:T(2,128)(2,1)S(1)} %copy.972), channel_id=19, replica_groups=mesh['head'=4,'blk'=8] {'head','blk'}, dimensions={2}, use_global_device_ids=true | all-gather | bytes 3168 | tf_op jit(solution)/shard_map/all_gather | solution.py:297
  725.4 46.0 %while.73 = (s32[]{:T(128)}, f32[3,512]{1,0:T(4,128)}, f32[3,512]{1,0:T(4,128)}, f32[3,512,64]{1,2,0:T(8,128)S(1)}, s32[8]{0:T(128)S(1)}, /*index=5*/s32[512]{0:...) while((s32[]{:T(128)}, f32[3,512]{1,0:T(4,128)}, ...), condition=%wide.wide.region_22.23_spmd.clone, body=%wide.wide.region_19.22_spmd.clone.sunk | while | flops 52338180 | bytes 6380824 | solution.py:58
  782.5 70.1 %all-gather.12 = bf16[1,768,12]{2,0,1:T(2,128)(2,1)S(1)} all-gather(bf16[1,24,12]{2,0,1:T(2,128)(2,1)S(1)} %copy.970), channel_id=14, replica_groups=mesh['head'=4,'blk'=8] {'head','blk'}, dimensions={1}, use_global_device_ids=true | all-gather | bytes 19008 | tf_op jit(solution)/shard_map/all_gather | solution.py:294
  853.0 70.2 %all-gather.16 = bf16[1,768,4]{2,0,1:T(2,128)(2,1)S(1)} all-gather(bf16[1,24,4]{2,0,1:T(2,128)(2,1)S(1)} %copy.971), channel_id=18, replica_groups=mesh['head'=4,'blk'=8] {'head','blk'}, dimensions={1}, use_global_device_ids=true | all-gather | bytes 6336 | tf_op jit(solution)/shard_map/all_gather | solution.py:295
  949.1 36.0 %all-gather.71.cloned.1.call-done = bf16[1,2,768,2048]{3,2,1,0:T(8,128)(2,1)} async-done(((bf16[1,2,96,2048]{3,2,1,0:T(8,128)(2,1)}), bf16[1,2,768,2048]{3,2,1,0:T(8,128)(2,1)}) %all-gather.71.cloned.1.call-update) | async-done | bytes 6291472 | tf_op jit(solution)/shard_map/all_gather | solution.py:302
  990.4 94.1 %all-gather.67.cloned.1.call-done = bf16[1,2,768,2048]{3,2,1,0:T(8,128)(2,1)} async-done(((bf16[1,2,96,2048]{3,2,1,0:T(8,128)(2,1)}), bf16[1,2,768,2048]{3,2,1,0:T(8,128)(2,1)}) %all-gather.67.cloned.1.call-update) | async-done | bytes 6291472 | tf_op jit(solution)/shard_map/all_gather | solution.py:300
  1137.2 29.1 all_gather.117
  1170.7 30.8 %all_gather.119 = bf16[4096,3]{0,1:T(4,128)(2,1)S(1)} all-gather(bf16[512,3]{0,1:T(4,128)(2,1)S(1)} %convert_element_type.533), channel_id=1, replica_groups=mesh['head'=4,'blk'=8] {'blk'}, dimensions={0}, use_global_device_ids=true | all-gather | bytes 27648 | tf_op jit(solution)/shard_map/all_gather | solution.py:568
  1205.6 123.0 %while.74 = (s32[]{:T(128)}, f32[512,3,64]{0,2,1:T(8,128)}, f32[512,3,64]{0,2,1:T(8,128)S(1)}, f32[512,3,64]{0,2,1:T(8,128)}, bf16[8,512,192]{1,2,0:T(8,128)(2,1...) while((s32[]{:T(128)}, f32[512,3,64]{0,2,1:T(8,128)}, ...), condition=%wide.wide.region_50.51_spmd.clone, body=%wide.wide.region_49.50_spmd.clone.sunk | while | flops 179549184 | bytes 18834776 | solution.py:58
  1424.6 30.7 %all_gather.121 = bf16[4096,3]{0,1:T(4,128)(2,1)S(1)} all-gather(bf16[512,3]{0,1:T(4,128)(2,1)S(1)} %get-tuple-element.1458), channel_id=1, replica_groups=mesh['head'=4,'blk'=8] {'blk'}, dimensions={0}, use_global_device_ids=true | all-gather | bytes 27648 | tf_op jit(solution)/shard_map/all_gather | solution.py:565
  1465.2 30.9 %all_gather.123 = bf16[4096,3]{0,1:T(4,128)(2,1)S(1)} all-gather(bf16[512,3]{0,1:T(4,128)(2,1)S(1)} %convert_element_type.562), channel_id=1, replica_groups=mesh['head'=4,'blk'=8] {'blk'}, dimensions={0}, use_global_device_ids=true | all-gather | bytes 27648 | tf_op jit(solution)/shard_map/all_gather | solution.py:568
  1500.8 114.7 %while.75 = (s32[]{:T(128)}, f32[512,3,64]{0,2,1:T(8,128)}, f32[512,3,64]{0,2,1:T(8,128)S(1)}, f32[512,3,64]{0,2,1:T(8,128)S(1)}, bf16[8,512,192]{1,2,0:T(8,128)...) while((s32[]{:T(128)}, f32[512,3,64]{0,2,1:T(8,128)}, ...), condition=%wide.wide.region_66.67_spmd.clone, body=%wide.wide.region_65.66_spmd.clone.sunk | while | flops 179549184 | bytes 18834776 | solution.py:58
  1701.5 75.1 %all-reduce.35.cloned.1.call-done = (f32[1,2,768]{2,1,0:T(2,128)}, f32[1,2,768]{2,1,0:T(2,128)}, f32[1,768,12]{1,2,0:T(8,128)}, f32[1,768,12]{1,2,0:T(8,128)}, f...) async-done(((f32[1,2,768]{2,1,0:T(2,128)}, f32[1,2,768]{2,1,0:T(2,128)}, f32[1,768,12]{1,2,0:T(8,128)}, ...) | async-done | bytes 122896
  1785.0 96.0 %reduce-scatter.25.cloned.1.call-done = f32[1,24,768]{2,1,0:T(8,128)} async-done(((f32[1,768,768]{2,1,0:T(8,128)}), f32[1,24,768]{2,1,0:T(8,128)}) %reduce-scatter.25.cloned.1.call-update) | async-done | bytes 73744 | tf_op jit(solution)/shard_map/reduce_scatter | solution.py:231
  1881.0 104.8 %reduce-scatter.23.cloned.1.call-done = f32[1,24,768]{2,1,0:T(8,128)} async-done(((f32[1,768,768]{2,1,0:T(8,128)}), f32[1,24,768]{2,1,0:T(8,128)}) %reduce-scatter.23.cloned.1.call-update) | async-done | bytes 73744 | tf_op jit(solution)/shard_map/reduce_scatter | solution.py:231
  1987.4 118.4 %reduce-scatter.37.cloned.1.call-done = bf16[1,2,96,2048]{3,2,1,0:T(8,128)(2,1)} async-done(((bf16[1,2,768,2048]{3,2,1,0:T(8,128)(2,1)}), bf16[1,2,96,2048]{3,2,1,0:T(8,128)(2,1)}) %reduce-scatter.37.cloned.1.call-update) | async-done | bytes 786448 | tf_op jit(solution)/shard_map/reduce_scatter | solution.py:244
  2105.8 120.7 %reduce-scatter.35.cloned.1.call-done = bf16[1,2,96,2048]{3,2,1,0:T(8,128)(2,1)} async-done(((bf16[1,2,768,2048]{3,2,1,0:T(8,128)(2,1)}), bf16[1,2,96,2048]{3,2,1,0:T(8,128)(2,1)}) %reduce-scatter.35.cloned.1.call-update) | async-done | bytes 786448 | tf_op jit(solution)/shard_map/reduce_scatter | solution.py:244
  2229.7 117.4 %reduce-scatter.33.cloned.1.call-done = bf16[1,2,96,2048]{3,2,1,0:T(8,128)(2,1)} async-done(((bf16[1,2,768,2048]{3,2,1,0:T(8,128)(2,1)}), bf16[1,2,96,2048]{3,2,1,0:T(8,128)(2,1)}) %reduce-scatter.33.cloned.1.call-update) | async-done | bytes 786448 | tf_op jit(solution)/shard_map/reduce_scatter | solution.py:241
  2347.1 120.7 %reduce-scatter.31.cloned.1.call-done = bf16[1,2,96,2048]{3,2,1,0:T(8,128)(2,1)} async-done(((bf16[1,2,768,2048]{3,2,1,0:T(8,128)(2,1)}), bf16[1,2,96,2048]{3,2,1,0:T(8,128)(2,1)}) %reduce-scatter.31.cloned.1.call-update) | async-done | bytes 786448 | tf_op jit(solution)/shard_map/reduce_scatter | solution.py:241
  2471.1 117.4 %reduce-scatter.29.cloned.1.call-done = bf16[1,2,96,2048]{3,2,1,0:T(8,128)(2,1)} async-done(((bf16[1,2,768,2048]{3,2,1,0:T(8,128)(2,1)}), bf16[1,2,96,2048]{3,2,1,0:T(8,128)(2,1)}) %reduce-scatter.29.cloned.1.call-update) | async-done | bytes 786448 | tf_op jit(solution)/shard_map/reduce_scatter | solution.py:238
  2588.5 120.6 %reduce-scatter.27.cloned.1.call-done = bf16[1,2,96,2048]{3,2,1,0:T(8,128)(2,1)} async-done(((bf16[1,2,768,2048]{3,2,1,0:T(8,128)(2,1)}), bf16[1,2,96,2048]{3,2,1,0:T(8,128)(2,1)}) %reduce-scatter.27.cloned.1.call-update) | async-done | bytes 786448 | tf_op jit(solution)/shard_map/reduce_scatter | solution.py:238
  2712.3 121.4 %reduce-scatter.21.cloned.1.call-done = f32[1,24,2304]{2,1,0:T(8,128)} async-done(((f32[1,768,2304]{2,1,0:T(8,128)}), f32[1,24,2304]{2,1,0:T(8,128)}) %reduce-scatter.21.cloned.1.call-update) | async-done | bytes 221200 | tf_op jit(solution)/shard_map/reduce_scatter | solution.py:230
  2833.6 125.1 %reduce-scatter.19.cloned.1.call-done = f32[1,24,2304]{2,1,0:T(8,128)} async-done(((f32[1,768,2304]{2,1,0:T(8,128)}), f32[1,24,2304]{2,1,0:T(8,128)}) %reduce-scatter.19.cloned.1.call-update) | async-done | bytes 221200 | tf_op jit(solution)/shard_map/reduce_scatter | solution.py:230
  (1906 shorter events, 797.5 us)
Async XLA Ops:
  7.2 77.0 %all-gather.53.cloned.1.call-start = ((), (), s32[]{:S(2)}) async-start(), calls=%async_computation.52 | async-start | bytes 3649536 | tf_op jit(solution)/shard_map/all_gather | solution.py:292
  8.9 257.3 %all-gather.37.cloned.1.call-start = ((), (), s32[]{:S(2)}) async-start(), calls=%async_computation.34 | async-start | bytes 1769472 | tf_op jit(solution)/shard_map/all_gather | solution.py:346
  96.4 171.4 %all-gather.39.cloned.1.call-start = ((), (), s32[]{:S(2)}) async-start(), calls=%async_computation.35 | async-start | bytes 1769472 | tf_op jit(solution)/shard_map/all_gather | solution.py:347
  105.3 389.9 %all-gather.55.cloned.1.call-start = ((), (), s32[]{:S(2)}) async-start(), calls=%async_computation.53 | async-start | bytes 1216512 | tf_op jit(solution)/shard_map/all_gather | solution.py:293
  106.0 403.0 %all-gather.57.cloned.1.call-start = ((), (), s32[]{:S(2)}) async-start(), calls=%async_computation.54 | async-start | bytes 7077888 | tf_op jit(solution)/shard_map/all_gather | solution.py:300
  108.8 404.4 %all-gather.59.cloned.1.call-start = ((), (), s32[]{:S(2)}) async-start(), calls=%async_computation.55 | async-start | bytes 7077888 | tf_op jit(solution)/shard_map/all_gather | solution.py:301
  110.2 443.0 %all-gather.61.cloned.1.call-start = ((), (), s32[]{:S(2)}) async-start(), calls=%async_computation.56 | async-start | bytes 7077888 | tf_op jit(solution)/shard_map/all_gather | solution.py:302
  113.0 503.1 %all-gather.63.cloned.1.call-start = ((), (), s32[]{:S(2)}) async-start(), calls=%async_computation.57 | async-start | bytes 3649536 | tf_op jit(solution)/shard_map/all_gather | solution.py:292
  186.6 78.9 %all-to-all-start.1 = ((bf16[128,4,192]{0,2,1:T(8,128)(2,1)}), bf16[128,4,192]{0,2,1:T(8,128)(2,1)S(1)}, u32[]{:S(2)}, u32[]{:S(2)}) async-start(bf16[128,4,192]{0,2,1:T(8,128)(2,1)} %bitcast.10), calls=%async_computation.1 | async-start | bytes 393216 | tf_op jit(solution)/shard_map/all_to_all | solution.py:315
  344.3 150.1 %all-to-all-start.3 = ((bf16[4,2,12288]{2,1,0:T(2,128)(2,1)}), bf16[4,2,12288]{2,1,0:T(2,128)(2,1)S(1)}, u32[]{:S(2)}, u32[]{:S(2)}) async-start(bf16[4,2,12288]{2,1,0:T(2,128)(2,1)} %reshape.1317), calls=%async_computation.3 | async-start | bytes 393216 | tf_op jit(solution)/shard_map/all_to_all | solution.py:355
  563.2 156.7 %all-gather.41.cloned.1.call-start = ((), (), s32[]{:S(2)}) async-start(), calls=%async_computation.36 | async-start | bytes 1769472 | tf_op jit(solution)/shard_map/all_gather | solution.py:346
  629.8 92.9 %all-gather.43.cloned.1.call-start = ((), (), s32[]{:S(2)}) async-start(), calls=%async_computation.37 | async-start | bytes 1769472 | tf_op jit(solution)/shard_map/all_gather | solution.py:347
  638.6 286.7 %all-gather.65.cloned.1.call-start = ((), (), s32[]{:S(2)}) async-start(), calls=%async_computation.58 | async-start | bytes 1216512 | tf_op jit(solution)/shard_map/all_gather | solution.py:293
  639.4 304.6 %all-gather.69.cloned.1.call-start = ((), (), s32[]{:S(2)}) async-start(), calls=%async_computation.60 | async-start | bytes 7077888 | tf_op jit(solution)/shard_map/all_gather | solution.py:301
  640.0 345.2 %all-gather.71.cloned.1.call-start = ((), (), s32[]{:S(2)}) async-start(), calls=%async_computation.61 | async-start | bytes 7077888 | tf_op jit(solution)/shard_map/all_gather | solution.py:302
  640.7 443.7 %all-gather.67.cloned.1.call-start = ((), (), s32[]{:S(2)}) async-start(), calls=%async_computation.59 | async-start | bytes 7077888 | tf_op jit(solution)/shard_map/all_gather | solution.py:300
  774.1 150.4 %all-to-all-start.9 = ((bf16[4,2,12288]{2,1,0:T(2,128)(2,1)}), bf16[4,2,12288]{2,1,0:T(2,128)(2,1)S(1)}, u32[]{:S(2)}, u32[]{:S(2)}) async-start(bf16[4,2,12288]{2,1,0:T(2,128)(2,1)} %reshape.1319), calls=%async_computation.9 | async-start | bytes 393216 | tf_op jit(solution)/shard_map/all_to_all | solution.py:355
  777.5 390.0 %all-gather.45.cloned.1.call-start = ((), (), s32[]{:S(2)}) async-start(), calls=%async_computation.38 | async-start | bytes 1769472 | tf_op jit(solution)/shard_map/all_gather | solution.py:563
  1114.4 88.6 %all-gather.47.cloned.1.call-start = ((), (), s32[]{:S(2)}) async-start(), calls=%async_computation.39 | async-start | bytes 1769472 | tf_op jit(solution)/shard_map/all_gather | solution.py:564
  1134.1 321.9 %all-gather.49.cloned.1.call-start = ((), (), s32[]{:S(2)}) async-start(), calls=%async_computation.40 | async-start | bytes 1769472 | tf_op jit(solution)/shard_map/all_gather | solution.py:563
  1400.5 97.0 %all-gather.51.cloned.1.call-start = ((), (), s32[]{:S(2)}) async-start(), calls=%async_computation.41 | async-start | bytes 1769472 | tf_op jit(solution)/shard_map/all_gather | solution.py:564
  1639.1 137.5 %all-reduce.35.cloned.1.call-start = ((), (), s32[]{:S(2)}) async-start(), calls=%async_computation.62 | async-start | bytes 294912
  1650.5 230.5 %reduce-scatter.25.cloned.1.call-start = ((), (), s32[]{:S(2)}) async-start(), calls=%async_computation.45 | async-start | bytes 2433024 | tf_op jit(solution)/shard_map/reduce_scatter | solution.py:231
  1652.5 333.3 %reduce-scatter.23.cloned.1.call-start = ((), (), s32[]{:S(2)}) async-start(), calls=%async_computation.44 | async-start | bytes 2433024 | tf_op jit(solution)/shard_map/reduce_scatter | solution.py:231
  1654.5 451.4 %reduce-scatter.37.cloned.1.call-start = ((), (), s32[]{:S(2)}) async-start(), calls=%async_computation.51 | async-start | bytes 7077888 | tf_op jit(solution)/shard_map/reduce_scatter | solution.py:244
  1659.1 567.4 %reduce-scatter.35.cloned.1.call-start = ((), (), s32[]{:S(2)}) async-start(), calls=%async_computation.50 | async-start | bytes 7077888 | tf_op jit(solution)/shard_map/reduce_scatter | solution.py:244
  1665.7 681.4 %reduce-scatter.33.cloned.1.call-start = ((), (), s32[]{:S(2)}) async-start(), calls=%async_computation.49 | async-start | bytes 7077888 | tf_op jit(solution)/shard_map/reduce_scatter | solution.py:241
  1671.6 796.3 %reduce-scatter.31.cloned.1.call-start = ((), (), s32[]{:S(2)}) async-start(), calls=%async_computation.48 | async-start | bytes 7077888 | tf_op jit(solution)/shard_map/reduce_scatter | solution.py:241
  1677.5 911.0 %reduce-scatter.29.cloned.1.call-start = ((), (), s32[]{:S(2)}) async-start(), calls=%async_computation.47 | async-start | bytes 7077888 | tf_op jit(solution)/shard_map/reduce_scatter | solution.py:238
  1683.2 1025.8 %reduce-scatter.27.cloned.1.call-start = ((), (), s32[]{:S(2)}) async-start(), calls=%async_computation.46 | async-start | bytes 7077888 | tf_op jit(solution)/shard_map/reduce_scatter | solution.py:238
  1689.0 1144.6 %reduce-scatter.21.cloned.1.call-start = ((), (), s32[]{:S(2)}) async-start(), calls=%async_computation.43 | async-start | bytes 7299072 | tf_op jit(solution)/shard_map/reduce_scatter | solution.py:230
  1694.3 1264.5 %reduce-scatter.19.cloned.1.call-start = ((), (), s32[]{:S(2)}) async-start(), calls=%async_computation.42 | async-start | bytes 7299072 | tf_op jit(solution)/shard_map/reduce_scatter | solution.py:230
  (380 other events, 6362.2 us)
Sparse Core Ops, SparseCore 0:
  11.6 62.5 all-gather.52
  96.5 44.1 all-gather.36
  142.8 45.2 all-gather.38
  191.0 53.1 all-gather.54
  246.8 98.2 all-gather.56
  347.8 104.2 all-gather.58
  454.2 98.9 all-gather.60
  556.7 59.2 all-gather.62
  629.9 44.6 all-gather.40
  677.1 44.1 all-gather.42
  724.3 52.9 all-gather.64
  779.9 104.1 all-gather.68
  886.3 98.7 all-gather.70
  987.2 97.1 all-gather.66
  1086.3 43.4 all-gather.44
  1134.2 42.6 all-gather.46
  1178.8 43.5 all-gather.48
  1421.6 43.7 all-gather.50
  1650.6 125.9 all-reduce.34
  1782.3 98.6 reduce-scatter.24
  1887.7 97.9 reduce-scatter.22
  1989.4 116.3 reduce-scatter.36
  2109.4 117.0 reduce-scatter.34
  2229.9 117.1 reduce-scatter.32
  2350.7 117.1 reduce-scatter.30
  2471.3 117.1 reduce-scatter.28
  2591.9 117.0 reduce-scatter.26
  2714.7 118.9 reduce-scatter.20
  2840.3 118.4 reduce-scatter.18
where the time goes:
time: 2990 us; the launch traced here: 2970 us
  waiting for transfers between devices  1500 us (50%)
  blocking collectives  719 us (24%)
  local copies, waits for them, and re-layouts  275 us (9%)
  matrix products  251 us (8%)
  other arithmetic  115 us (4%)
  starting transfers between devices  65.5 us (2%)
    reduce_scatter x2, waiting for transfers between devices, reduce_grads(): lax.psum_scatter(in_grad, ('head', 'blk'), scatter_dimension=1, tiled=True)  247 us
    reduce_scatter x2, waiting for transfers between devices, reduce_grads(): lax.psum_scatter(down_grad.astype(jnp.bfloat16), 'blk', scatter_dimension...  239 us
    reduce_scatter x2, waiting for transfers between devices, reduce_grads(): lax.psum_scatter(up_grad.astype(jnp.bfloat16), 'blk', scatter_dimension=2...  238 us
    reduce_scatter x2, waiting for transfers between devices, reduce_grads(): lax.psum_scatter(gate_grad.astype(jnp.bfloat16), 'blk', scatter_dimension...  238 us
    reduce_scatter x2, waiting for transfers between devices, reduce_grads(): lax.psum_scatter(out_grad, ('head', 'blk'), scatter_dimension=1, tiled=True)  201 us
    all_gather x2, blocking collectives, local(): lax.all_gather(router_weight[layer], ('head', 'blk'), axis=0, tiled=True)  141 us
    all_gather x2, blocking collectives, local(): lax.all_gather(const_mix[layer], ('head', 'blk'), axis=0, tiled=True)  140 us
    all_gather x2, blocking collectives, local(): lax.all_gather(norm_gains[layer], ('head', 'blk'), axis=1, tiled=True)  135 us
  transfers between devices with their start and end apart: 47, of which 29 were waited for; matrix products, arithmetic and copies ran while one was open for 16% of the time, Pallas kernels for 0%

commit v1 on v0

v1 whole, which is shorter than its diff:
```python
import jax
import jax.numpy as jnp
from jax import lax
from jax.experimental import pallas as pl
from jax.experimental.pallas import tpu as pltpu
from jax.sharding import PartitionSpec as P

HEADS = 12
HD = 64
NF = 8
TOP = 2
LAYERS = 2
NE = 12
CAP = 26
SLOT = 32
GROUPS = 4
EPSILON = 1e-05
NEGATIVE = -1e30
SCALE = HD ** (-0.5)
VMEM_BYTES = 60 * 1024 * 1024

BF = jnp.bfloat16
F32 = jnp.float32
MESH = pl.DeviceIdType.MESH
VMEM = pl.BlockSpec(memory_space=pltpu.VMEM)
ANY = pl.BlockSpec(memory_space=pl.ANY)


def mm(a, b, ca=1, cb=0):
    return lax.dot_general(a, b, (((ca,), (cb,)), ((), ())), preferred_element_type=F32)


def split(v):
    high = v.astype(BF)
    return high, (v - high.astype(F32)).astype(BF)


def lanes(shape):
    return lax.broadcasted_iota(jnp.int32, shape, len(shape) - 1)


def lane_of(v, index):
    return jnp.sum(jnp.where(lanes(v.shape) == index, v, 0.0), axis=-1, keepdims=True)


def rows_of(small):
    pick = lax.broadcasted_iota(jnp.int32, (8, 128), 0) + 16 == lanes((8, 128))
    return mm(pick.astype(F32).astype(BF), small, 1, 1)


def swap_halves(v):
    width = v.shape[-1]
    low_half = lanes(v.shape) % HD < HD // 2
    return jnp.where(
        low_half, pltpu.roll(v, width - HD // 2, 1), pltpu.roll(v, HD // 2, 1)
    )


def rotate(v, cosine, sine):
    return v * cosine + swap_halves(v) * sine


def rotate_back(v, cosine, sine):
    return v * cosine - swap_halves(v) * sine


def norm_grad(v, root, gain, grad):
    scaled = grad * gain
    inner = jnp.mean(v * scaled, axis=-1, keepdims=True)
    return root * scaled - v * (root * root * root * inner)


class Links:
    def __init__(self, send, recv):
        self.send, self.recv, self.used = send, recv, 0

    def copy(self, src, dst, device):
        made = pltpu.make_async_remote_copy(
            src_ref=src,
            dst_ref=dst,
            send_sem=self.send.at[self.used],
            recv_sem=self.recv.at[self.used],
            device_id=device,
            device_id_type=MESH,
        )
        self.used += 1
        return made


def greet(devices):
    barrier = pltpu.get_barrier_semaphore()
    for device in devices:
        pl.semaphore_signal(barrier, inc=1, device_id=device, device_id_type=MESH)
    pl.semaphore_wait(barrier, len(devices))


def launch(body, number, ins, in_specs, outs, out_specs, scratch, copies):
    return pl.pallas_call(
        body,
        out_shape=outs,
        in_specs=in_specs,
        out_specs=out_specs,
        scratch_shapes=list(scratch)
        + [pltpu.SemaphoreType.DMA((copies,)), pltpu.SemaphoreType.DMA((copies,))]
        + [pltpu.SemaphoreType.DMA((8,))],
        compiler_params=pltpu.CompilerParams(
            collective_id=number, has_side_effects=True, vmem_limit_bytes=VMEM_BYTES
        ),
    )(*ins)


class Shape:
    def __init__(self, nh, nb, rows, width, hidden):
        self.nh, self.nb, self.rows, self.width = nh, nb, rows, width
        self.hh, self.hl = nh // 2, 2
        self.minor = 2 if nb <= 8 else 4
        self.major = nb // self.minor
        self.splits = nb // GROUPS
        self.nq = nb // 2
        self.ffp = hidden // self.nq
        self.hidden = hidden
        self.drow = width // nb
        self.shard = width // (nh * nb)
        self.slots = 2 * nh * SLOT


def struct(shape, kind):
    return jax.ShapeDtypeStruct(shape, kind)


def weight_copies(z, h, b, parts, layer, gathered, links, local_sem):
    copies = []
    for r in range(z.nb):
        t = lax.rem(b + r, z.nb)
        e, q = t // z.nq, lax.rem(t, z.nq)
        cols = pl.ds(pl.multiple_of(q * z.ffp, 128), z.ffp)
        for w in range(3):
            src, dst = parts[w].at[layer, e, :, cols], gathered.at[w, b]
            if r == 0:
                copies.append(pltpu.make_async_copy(src, dst, local_sem.at[w]))
            else:
                copies.append(links.copy(src, dst, (h, t)))
    return copies


def grad_copies(z, h, b, grads, landed, links, local_sem):
    e, q = b // z.nq, lax.rem(b, z.nq)
    cols = pl.ds(pl.multiple_of(q * z.ffp, 128), z.ffp)
    copies = []
    for r in range(z.nb):
        t = lax.rem(b + r, z.nb)
        for w in range(3):
            src, dst = grads.at[w, t], landed.at[w, e, :, cols]
            if r == 0:
                copies.append(pltpu.make_async_copy(src, dst, local_sem.at[w]))
            else:
                copies.append(links.copy(src, dst, (h, t)))
    return copies


def place_of(z, h, b):
    return h // z.hl, lax.rem(h, z.hl), b // z.minor, lax.rem(b, z.minor)


def gather_weights(z, number, shards, expert_parts, layer):
    pieces = len(shards)
    shape = (z.hh, z.hl, z.major, z.minor)

    def body(*refs):
        own = refs[:pieces]
        parts = refs[pieces : pieces + 3]
        full = refs[pieces + 3 : 2 * pieces + 3]
        experts = refs[2 * pieces + 3]
        send, recv, local_sem, own_sem = refs[2 * pieces + 4 :]
        h, b = lax.axis_index("head"), lax.axis_index("blk")
        y, c, m, n = place_of(z, h, b)
        blk_peers = [(h, lax.rem(b + r, z.nb)) for r in range(1, z.nb)]
        core_peer = (y * z.hl + 1 - c, b)
        y_peers = [(lax.rem(y + r, z.hh) * z.hl + c, b) for r in range(1, z.hh)]
        greet(blk_peers + [core_peer] + y_peers)
        links = Links(send, recv)
        major_peers = [(h, lax.rem(m + r, z.major) * z.minor + n) for r in range(1, z.major)]
        minor_peers = [(h, m * z.minor + lax.rem(n + r, z.minor)) for r in range(1, z.minor)]
        every = slice(None)
        stages = {
            0: [
                ((y, c, m, n), major_peers),
                ((y, c, every, n), minor_peers),
                ((y, c, every, every), y_peers),
                ((every, c, every, every), [core_peer]),
            ],
            1: [
                ((y, c, m, n), major_peers),
                ((y, c, every, n), y_peers),
                ((every, c, every, n), minor_peers),
                ((every, c, every, every), [core_peer]),
            ],
        }
        keep = []
        for p in range(pieces):
            keep.append(pltpu.make_async_copy(own[p], full[p].at[y, c, m, n], own_sem.at[p]))
            keep[p].start()
        side = []
        waiting = [[] for _ in range(pieces)]
        done = []
        for stage in range(4):
            for p in range(pieces):
                for made in waiting[p]:
                    made.wait_recv()
                if stage == 1:
                    keep[p].wait()
                at, peers = stages[p % 2][stage]
                src = own[p] if stage == 0 else full[p].at[at]
                waiting[p] = [links.copy(src, full[p].at[at], peer) for peer in peers]
                for made in waiting[p]:
                    made.start()
                done += waiting[p]
            if stage == 0:
                side = weight_copies(z, h, b, parts, layer, experts, links, local_sem)
                for made in side:
                    made.start()
        for p in range(pieces):
            for made in waiting[p]:
                made.wait_recv()
        for made in done:
            made.wait_send()
        for made in side:
            made.wait()

    steps = z.major - 1 + z.minor - 1 + z.hh - 1 + 1
    return pl.pallas_call(
        body,
        out_shape=[struct(shape + s.shape, BF) for s in shards]
        + [struct((3, z.nb, z.drow, z.ffp), BF)],
        in_specs=[ANY] * (pieces + 3),
        out_specs=[ANY] * (pieces + 1),
        scratch_shapes=[
            pltpu.SemaphoreType.DMA((pieces * steps + 3 * z.nb,)),
            pltpu.SemaphoreType.DMA((pieces * steps + 3 * z.nb,)),
            pltpu.SemaphoreType.DMA((8,)),
            pltpu.SemaphoreType.DMA((8,)),
        ],
        compiler_params=pltpu.CompilerParams(
            collective_id=number, has_side_effects=True, vmem_limit_bytes=VMEM_BYTES
        ),
    )(*shards, *expert_parts)


def head_masks(first):
    where_lane = lanes((1, 256))
    return [
        ((where_lane >= first + HD * j) & (where_lane < first + HD * (j + 1))).astype(F32)
        for j in range(3)
    ]


def window(v, g, shifted):
    start = 384 * (g // 2) + 128 * (g % 2)
    cut = v[:, start : start + 256]
    if shifted:
        if g % 2 == 0:
            cut = pltpu.roll(cut, HD, 1)
        return jnp.where(lanes(cut.shape) >= HD, cut, 0.0)
    if g % 2 == 1:
        cut = pltpu.roll(cut, 256 - HD, 1)
    return jnp.where(lanes(cut.shape) < 192, cut, 0.0)


def unwindow(even, odd):
    odd = pltpu.roll(odd, HD, 1)
    return [even[:, :128], even[:, 128:] + odd[:, :128], odd[:, 128:]]


def causal(z, i, s, keys):
    rows = lax.broadcasted_iota(jnp.int32, (3 * z.rows, keys), 0) % z.rows
    cols = lanes((3 * z.rows, keys))
    return cols <= rows + (i * z.splits + s) * z.rows


def attend(z, number, state, small, w_in, w_out, tables, expert_parts, layer):
    side_on = expert_parts is not None

    def body(*refs):
        x_ref, small_ref, win_ref, wout_ref, cq, sq, ckv, skv = refs[:8]
        at = 8
        if side_on:
            parts = refs[at : at + 3]
            at += 3
        mid_ref, low_ref, q_ref, kv_ref, o_ref, lse_ref, ret_ref = refs[at : at + 7]
        at += 7
        if side_on:
            experts = refs[at]
            at += 1
        q_out, kv_out, o_out, send, recv, local_sem = refs[at:]
        h, b = lax.axis_index("head"), lax.axis_index("blk")
        g, s = b // z.splits, lax.rem(b, z.splits)
        links = Links(send, recv)
        greet([(h, lax.rem(b + r, z.nb)) for r in range(1, z.nb)])
        x = x_ref[...]
        gain = rows_of(small_ref[...])[0:1]
        root = lax.rsqrt(jnp.mean(x * x, axis=-1, keepdims=True) + EPSILON)
        low = (x * root * gain).astype(BF)
        low_ref[...] = low
        for n in range(GROUPS):
            kv = mm(low, win_ref[:, 384 * n : 384 * (n + 1)])
            kv_out[n] = rotate(kv, ckv[...], skv[...]).astype(BF)
        q = rotate(mm(low, win_ref[:, 2 * z.width :]), cq[...], sq[...])
        for n in range(GROUPS):
            q_out[n] = window(q, n, False).astype(BF)
        moved = []
        for r in range(1, z.nb):
            t = lax.rem(b + r, z.nb)
            moved.append(links.copy(kv_out.at[t // z.splits], kv_ref.at[b], (h, t)))
        for r in range(1, GROUPS):
            n = lax.rem(g + r, GROUPS)
            moved.append(links.copy(q_out.at[n], q_ref.at[g], (h, n * z.splits + s)))
        for made in moved:
            made.start()
        kv_ref[b] = kv_out[g]
        q_ref[g] = q_out[g]
        side = []
        if side_on:
            side = weight_copies(z, h, b, parts, layer, experts, links, local_sem)
            for made in side:
                made.start()
        for made in moved:
            made.wait()
        q_masks = [m.astype(BF) for m in head_masks(0)]
        v_masks = head_masks(HD)
        for i in range(GROUPS):
            blocks = (i + 1) * z.splits
            keys = blocks * z.rows
            kv = kv_ref[0:blocks].reshape(keys, 384)
            q3 = jnp.concatenate([q_ref[i] * m for m in q_masks], axis=0)
            scores = mm(q3, kv[:, 0:256], 1, 1) * SCALE
            scores = jnp.where(causal(z, i, s, keys), scores, NEGATIVE)
            peak = jnp.max(scores, axis=-1, keepdims=True)
            weights = jnp.exp(scores - peak)
            total = jnp.sum(weights, axis=-1, keepdims=True)
            out = mm(weights.astype(BF), kv[:, 128:384]) / total
            merged = sum(out[z.rows * j : z.rows * (j + 1)] * v_masks[j] for j in range(3))
            o_ref[i] = merged
            o_out[i] = pltpu.roll(merged, 256 - HD, 1).astype(BF)
            lse_ref[i] = peak + jnp.log(total)
        moved = []
        for r in range(1, GROUPS):
            n = lax.rem(g + r, GROUPS)
            moved.append(links.copy(o_out.at[n], ret_ref.at[g], (h, n * z.splits + s)))
        for made in moved:
            made.start()
        ret_ref[g] = o_out[g]
        for made in moved:
            made.wait()
        middle = x
        for n in range(GROUPS):
            middle = middle + mm(ret_ref[n, :, 0:192], wout_ref[192 * n : 192 * (n + 1), :])
        mid_ref[...] = middle
        for made in side:
            made.wait()

    outs = [
        struct((z.rows, z.width), F32),
        struct((z.rows, z.width), BF),
        struct((GROUPS, z.rows, 256), BF),
        struct((z.nb, z.rows, 384), BF),
        struct((GROUPS, z.rows, 256), F32),
        struct((GROUPS, 3 * z.rows, 1), F32),
        struct((GROUPS, z.rows, 256), BF),
    ]
    out_specs = [VMEM] * 7
    ins = [state, small, w_in, w_out, *tables]
    in_specs = [VMEM] * 8
    if side_on:
        ins += list(expert_parts)
        in_specs += [ANY] * 3
        outs.append(struct((3, z.nb, z.drow, z.ffp), BF))
        out_specs.append(ANY)
    return launch(
        body,
        number,
        ins,
        in_specs,
        outs,
        out_specs,
        [
            pltpu.VMEM((GROUPS, z.rows, 256), BF),
            pltpu.VMEM((GROUPS, z.rows, 384), BF),
            pltpu.VMEM((GROUPS, z.rows, 256), BF),
        ],
        z.nb + 2 * GROUPS + 3 * z.nb,
    )


def attend_back(z, number, grad_mid, state, low, small, w_in, w_out, tables, saved):
    chunk = min(1024, z.nb * z.rows)

    def body(*refs):
        (dm_ref, x_ref, low_ref, small_ref, win_ref, wout_ref, cq, sq, ckv, skv) = refs[:10]
        q_ref, kv_ref, o_ref, lse_ref, ret_ref = refs[10:15]
        ds_ref, gin_ref, gout_ref, gain_ref = refs[15:19]
        (do_out, do_ref, dq_out, dkv_out, dq_ref, dkv_ref, dk_sum, dv_sum) = refs[19:27]
        send, recv, _ = refs[27:]
        h, b = lax.axis_index("head"), lax.axis_index("blk")
        g, s = b // z.splits, lax.rem(b, z.splits)
        links = Links(send, recv)
        greet([(h, lax.rem(b + r, z.nb)) for r in range(1, z.nb)])
        dm = dm_ref[...]
        branch = dm.astype(BF)
        grad_att = mm(branch, wout_ref[...], 1, 1)
        for n in range(GROUPS):
            do_out[n] = window(grad_att, n, True).astype(BF)
        moved = []
        for r in range(1, GROUPS):
            n = lax.rem(g + r, GROUPS)
            moved.append(links.copy(do_out.at[n], do_ref.at[g], (h, n * z.splits + s)))
        for made in moved:
            made.start()
        do_ref[g] = do_out[g]
        per = 192 // z.shard if 192 % z.shard == 0 else 0
        for n in range(GROUPS):
            part = mm(ret_ref[n], branch, 0, 0)[0:192]
            for k in range(192 // z.shard):
                gout_ref[n * per + k] = part[k * z.shard : (k + 1) * z.shard].astype(BF)
        dk_sum[...] = jnp.zeros_like(dk_sum)
        dv_sum[...] = jnp.zeros_like(dv_sum)
        q_masks = head_masks(0)
        v_masks = head_masks(HD)
        for made in moved:
            made.wait()
        for i in range(GROUPS):
            keys_all = (i + 1) * z.splits * z.rows
            q3 = jnp.concatenate([q_ref[i] * m.astype(BF) for m in q_masks], axis=0)
            do3 = jnp.concatenate([do_ref[i] * m.astype(BF) for m in v_masks], axis=0)
            o3 = jnp.concatenate([o_ref[i]] * 3, axis=0)
            delta = jnp.sum(do3.astype(F32) * o3, axis=-1, keepdims=True)
            lse = lse_ref[i]
            dq3 = jnp.zeros((3 * z.rows, 256), F32)
            for start in range(0, keys_all, chunk):
                keys = min(chunk, keys_all - start)
                first = start // z.rows
                kv = kv_ref[first : first + keys // z.rows].reshape(keys, 384)
                key, value = kv[:, 0:256], kv[:, 128:384]
                rows = lax.broadcasted_iota(jnp.int32, (3 * z.rows, keys), 0) % z.rows
                cols = lanes((3 * z.rows, keys)) + start
                mask = cols <= rows + (i * z.splits + s) * z.rows
                scores = mm(q3, key, 1, 1) * SCALE
                weights = jnp.where(mask, jnp.exp(scores - lse), 0.0)
                grad_weights = mm(do3, value, 1, 1)
                grad_scores = (weights * (grad_weights - delta)).astype(BF)
                dq3 = dq3 + mm(grad_scores, key)
                dk_sum[start : start + keys] += mm(grad_scores, q3, 0, 0)
                dv_sum[start : start + keys] += mm(weights.astype(BF), do3, 0, 0)
            dq = sum(dq3[z.rows * j : z.rows * (j + 1)] * q_masks[j] for j in range(3))
            dq_out[i] = (dq * SCALE).astype(BF)
        for n in range(z.nb):
            dk = dk_sum[n * z.rows : (n + 1) * z.rows] * SCALE
            dv = dv_sum[n * z.rows : (n + 1) * z.rows]
            dkv_out[n, :, 0:128] = dk[:, :128].astype(BF)
            dkv_out[n, :, 128:256] = (dk[:, 128:] + dv[:, :128]).astype(BF)
            dkv_out[n, :, 256:384] = dv[:, 128:].astype(BF)
        moved = []
        for r in range(1, z.nb):
            t = lax.rem(b + r, z.nb)
            moved.append(links.copy(dkv_out.at[t], dkv_ref.at[b], (h, t)))
        for r in range(1, GROUPS):
            n = lax.rem(g + r, GROUPS)
            moved.append(links.copy(dq_out.at[n], dq_ref.at[g], (h, n * z.splits + s)))
        for made in moved:
            made.start()
        dkv_ref[b] = dkv_out[b]
        dq_ref[g] = dq_out[g]
        for made in moved:
            made.wait()
        own = low_ref[...]
        grad_low = jnp.zeros((z.rows, z.width), F32)
        shards = z.width // z.shard
        for n in range(GROUPS):
            total = dkv_ref[n * z.splits].astype(F32)
            for k in range(1, z.splits):
                total = total + dkv_ref[n * z.splits + k].astype(F32)
            piece = rotate_back(total, ckv[...], skv[...]).astype(BF)
            grad_low = grad_low + mm(piece, win_ref[:, 384 * n : 384 * (n + 1)], 1, 1)
            part = mm(own, piece, 0, 0)
            for k in range(shards):
                gin_ref[k, :, 384 * n : 384 * (n + 1)] = part[
                    k * z.shard : (k + 1) * z.shard
                ].astype(BF)
        columns = []
        for n in range(0, GROUPS, 2):
            columns += unwindow(dq_ref[n].astype(F32), dq_ref[n + 1].astype(F32))
        piece = rotate_back(jnp.concatenate(columns, axis=1), cq[...], sq[...]).astype(BF)
        grad_low = grad_low + mm(piece, win_ref[:, 2 * z.width :], 1, 1)
        part = mm(own, piece, 0, 0)
        for k in range(shards):
            gin_ref[k, :, 2 * z.width :] = part[k * z.shard : (k + 1) * z.shard].astype(BF)
        x = x_ref[...]
        gain = rows_of(small_ref[...])[0:1]
        root = lax.rsqrt(jnp.mean(x * x, axis=-1, keepdims=True) + EPSILON)
        ds_ref[...] = dm + norm_grad(x, root, gain, grad_low)
        place = (lanes((z.rows, 128)) == 16).astype(F32).astype(BF)
        high, rest = split(grad_low * x * root)
        gain_ref[...] = mm(high, place, 0, 0) + mm(rest, place, 0, 0)

    shards = z.nh * z.nb
    return launch(
        body,
        number,
        [grad_mid, state, low, small, w_in, w_out, *tables, *saved],
        [VMEM] * 15,
        [
            struct((z.rows, z.width), F32),
            struct((shards, z.shard, 3 * z.width), BF),
            struct((shards, z.shard, z.width), BF),
            struct((z.width, 128), F32),
        ],
        [VMEM] * 4,
        [
            pltpu.VMEM((GROUPS, z.rows, 256), BF),
            pltpu.VMEM((GROUPS, z.rows, 256), BF),
            pltpu.VMEM((GROUPS, z.rows, 256), BF),
            pltpu.VMEM((z.nb, z.rows, 384), BF),
            pltpu.VMEM((GROUPS, z.rows, 256), BF),
            pltpu.VMEM((z.nb, z.rows, 384), BF),
            pltpu.VMEM((z.nb * z.rows, 256), F32),
            pltpu.VMEM((z.nb * z.rows, 256), F32),
        ],
        z.nb + 2 * GROUPS,
    )


class Mixing:
    def __init__(self, z, middle, small, routes, target):
        table = rows_of(small)
        self.gain, self.consts = table[1:2], (table[2:3], table[3:4])
        self.root = lax.rsqrt(jnp.mean(middle * middle, axis=-1, keepdims=True) + EPSILON)
        self.normed = middle * self.root * self.gain
        self.low, self.rest = split(self.normed)
        self.product = mm(self.low, small)
        shares = self.product + mm(self.rest, small)
        self.shares = []
        for index in range(2):
            one, two = lane_of(shares, 12 + 2 * index), lane_of(shares, 13 + 2 * index)
            peak = jnp.maximum(one, two)
            one, two = jnp.exp(one - peak), jnp.exp(two - peak)
            self.shares.append((one / (one + two), two / (one + two)))
        self.picks = [(lanes((z.rows, 128)) == routes[:, j : j + 1]).astype(F32) for j in range(TOP)]
        self.chosen = [
            (lanes((z.rows, z.slots)) == target[:, j : j + 1]).astype(F32) for j in range(TOP)
        ]

    def gate(self, logits):
        values = [jnp.sum(p * logits, axis=-1, keepdims=True) for p in self.picks]
        peak = jnp.maximum(values[0], values[1])
        powers = [jnp.exp(v - peak) for v in values]
        total = powers[0] + powers[1]
        self.gates = [p / total for p in powers]
        self.combine = self.gates[0] * self.chosen[0] + self.gates[1] * self.chosen[1]
        spread = self.gates[0] * self.picks[0] + self.gates[1] * self.picks[1]
        self.const_weights = [lane_of(spread, NF + 2 + index) for index in range(2)]
        self.normed_weight = lane_of(spread, NF + 1)
        for index in range(2):
            self.normed_weight = (
                self.normed_weight + self.const_weights[index] * self.shares[index][0]
            )


def expert_peers(z, h, i, q):
    others = []
    for dh in range(z.nh):
        for di in range(2):
            if dh or di:
                others.append((lax.rem(h + dh, z.nh), lax.rem(i + di, 2)))
    parts = [lax.rem(q + r, z.nq) for r in range(1, z.nq)]
    return others, parts


def spread_rows(z, links, h, i, q, others, parts, rows_ref, all_ref):
    mine = 2 * h + i
    first = []
    for oh, oi in others:
        made = links.copy(rows_ref.at[2 * oh + oi], all_ref.at[q, mine], (oh, oi * z.nq + q))
        made.start()
        first.append(made)
    all_ref[q, mine] = rows_ref[mine]
    onward = [[] for _ in parts]
    sources = [(h, i)]
    for dh in range(z.nh):
        for di in range(2):
            if dh or di:
                sources.append((lax.rem(h + z.nh - dh, z.nh), lax.rem(i + 2 - di, 2)))
    for k, (sh, si) in enumerate(sources):
        if k:
            first[k - 1].wait_recv()
        place = all_ref.at[q, 2 * sh + si]
        for n, part in enumerate(parts):
            made = links.copy(place, place, (h, i * z.nq + part))
            made.start()
            onward[n].append(made)
    return first, onward


def return_rows(z, links, h, i, q, others, sum_ref, back_ref):
    mine = 2 * h + i
    made = []
    for oh, oi in others:
        made.append(links.copy(sum_ref.at[2 * oh + oi], back_ref.at[mine], (oh, oi * z.nq + q)))
        made[-1].start()
    back_ref[mine] = sum_ref[mine]
    return made


def expert_greet(z, h, i, q, others, parts):
    greet(
        [(oh, oi * z.nq + q) for oh, oi in others] + [(h, i * z.nq + part) for part in parts]
    )


def expert_copies(z):
    return 2 * (2 * z.nh - 1) + 2 * z.nh * (z.nq - 1) + z.nq


def expert_forward(z, number, middle, small, logits_in, routes, target, weights):
    count = 2 * z.nh * SLOT

    def body(*refs):
        mid_ref, small_ref, logits_ref, routes_ref, target_ref, w_ref = refs[:6]
        state_ref, next_ref, res_ref, all_ref, gate_ref, up_ref = refs[6:12]
        rows_ref, part_ref, got_ref, sum_ref, send, recv, _ = refs[12:]
        h, b = lax.axis_index("head"), lax.axis_index("blk")
        i, q = b // z.nq, lax.rem(b, z.nq)
        others, parts = expert_peers(z, h, i, q)
        links = Links(send, recv)
        expert_greet(z, h, i, q, others, parts)
        middle = mid_ref[...]
        mixing = Mixing(z, middle, small_ref[...], routes_ref[...], target_ref[...])
        select = (mixing.chosen[0] + mixing.chosen[1]).astype(BF)
        rows_ref[...] = mm(select, mixing.low, 0, 0).astype(BF).reshape(rows_ref.shape)
        first, onward = spread_rows(z, links, h, i, q, others, parts, rows_ref, all_ref)
        logits = mixing.product + logits_ref[...]
        next_ref[...] = logits
        mixing.gate(logits)
        back = []
        own = None
        for r in range(z.nq):
            part = lax.rem(q + z.nq - r, z.nq)
            if r:
                for made in onward[r - 1]:
                    made.wait_recv()
            rows = all_ref[part].reshape(count, z.width)
            gate, up = mm(rows, w_ref[0]), mm(rows, w_ref[1])
            gate_ref[part], up_ref[part] = gate, up
            hidden = (gate / (1.0 + jnp.exp(-gate)) * up).astype(BF)
            result = mm(hidden, w_ref[2], 1, 1)
            if r == 0:
                own = result
            else:
                part_ref[r - 1] = result.astype(BF)
                made = links.copy(part_ref.at[r - 1], got_ref.at[r - 1], (h, i * z.nq + part))
                made.start()
                back.append(made)
        total = own
        for r, made in enumerate(back):
            made.wait_recv()
            total = total + got_ref[r].astype(F32)
        sum_ref[...] = total.astype(BF).reshape(sum_ref.shape)
        last = return_rows(z, links, h, i, q, others, sum_ref, res_ref)
        for made in last:
            made.wait_recv()
        results = res_ref[...].reshape(count, z.width)
        high, rest = split(mixing.combine)
        mixed = mm(high, results) + mm(rest, results) + mixing.normed_weight * mixing.normed
        for index in range(2):
            weight = mixing.const_weights[index] * mixing.shares[index][1]
            mixed = mixed + weight * mixing.consts[index]
        state_ref[...] = middle + mixed
        for made in first + back + last:
            made.wait_send()
        for group in onward:
            for made in group:
                made.wait_send()

    block = (2 * z.nh, SLOT, z.width)
    return launch(
        body,
        number,
        [middle, small, logits_in, routes, target, weights],
        [VMEM] * 6,
        [
            struct((z.rows, z.width), F32),
            struct((z.rows, 128), F32),
            struct(block, BF),
            struct((z.nq,) + block, BF),
            struct((z.nq, count, z.ffp), F32),
            struct((z.nq, count, z.ffp), F32),
        ],
        [VMEM] * 6,
        [
            pltpu.VMEM(block, BF),
            pltpu.VMEM((z.nq - 1, count, z.width), BF),
            pltpu.VMEM((z.nq - 1, count, z.width), BF),
            pltpu.VMEM(block, BF),
        ],
        expert_copies(z),
    )


def expert_back(z, number, grad, middle, small, logits, grad_logits, routes, target, weights, saved, late):
    count = 2 * z.nh * SLOT
    side_on = late is not None

    def body(*refs):
        dy_ref, mid_ref, small_ref, logits_ref, dl_ref, routes_ref, target_ref, w_ref = refs[:8]
        res_ref, all_ref, gate_ref, up_ref = refs[8:12]
        at = 12
        if side_on:
            late_ref = refs[at]
            at += 1
        dm_ref, dnext_ref, gsmall_ref, gw_ref = refs[at : at + 4]
        at += 4
        if side_on:
            landed_ref = refs[at]
            at += 1
        (rows_ref, dall_ref, part_ref, got_ref, sum_ref, back_ref, hid_ref, dg_ref, du_ref) = refs[
            at : at + 9
        ]
        send, recv, local_sem = refs[at + 9 :]
        h, b = lax.axis_index("head"), lax.axis_index("blk")
        i, q = b // z.nq, lax.rem(b, z.nq)
        others, parts = expert_peers(z, h, i, q)
        links = Links(send, recv)
        if side_on:
            more = [(h, lax.rem(b + r, z.nb)) for r in range(1, z.nb)]
            far = [
                (lax.rem(h + dh, z.nh), lax.rem(i + di, 2) * z.nq + q)
                for dh in range(1, z.nh)
                for di in range(2)
            ]
            greet(more + far)
        else:
            expert_greet(z, h, i, q, others, parts)
        grad = dy_ref[...]
        mixing = Mixing(z, mid_ref[...], small_ref[...], routes_ref[...], target_ref[...])
        mixing.gate(logits_ref[...])
        high, rest = split(grad)
        weight_high, weight_rest = split(mixing.combine)
        slot_grad = mm(weight_high, high, 0, 0) + mm(weight_rest, high, 0, 0)
        slot_grad = slot_grad + mm(weight_high, rest, 0, 0)
        rows_ref[...] = slot_grad.astype(BF).reshape(rows_ref.shape)
        first, onward = spread_rows(z, links, h, i, q, others, parts, rows_ref, dall_ref)
        side = []
        if side_on:
            side = grad_copies(z, h, b, late_ref, landed_ref, links, local_sem)
            for made in side:
                made.start()
        results = res_ref[...].reshape(count, z.width)
        along = mm(high, results, 1, 1) + mm(rest, results, 1, 1)
        normed_dot = jnp.sum(grad * mixing.normed, axis=-1, keepdims=True)
        const_dots = [jnp.sum(grad * c, axis=-1, keepdims=True) for c in mixing.consts]
        gate_grads = []
        for j in range(TOP):
            value = jnp.sum(mixing.chosen[j] * along, axis=-1, keepdims=True)
            value = value + lane_of(mixing.picks[j], NF + 1) * normed_dot
            for index in range(2):
                share = mixing.shares[index]
                value = value + lane_of(mixing.picks[j], NF + 2 + index) * (
                    share[0] * normed_dot + share[1] * const_dots[index]
                )
            gate_grads.append(value)
        inner = mixing.gates[0] * gate_grads[0] + mixing.gates[1] * gate_grads[1]
        logit_grad = dl_ref[...]
        for j in range(TOP):
            logit_grad = logit_grad + mixing.picks[j] * (mixing.gates[j] * (gate_grads[j] - inner))
        dnext_ref[...] = logit_grad
        where_lane = lanes((z.rows, 128))
        column = jnp.zeros((z.rows, 128), F32)
        const_columns = jnp.zeros((z.rows, 128), F32)
        for index in range(2):
            share, weight = mixing.shares[index], mixing.const_weights[index]
            one, two = weight * normed_dot, weight * const_dots[index]
            mean = share[0] * one + share[1] * two
            column = column + jnp.where(where_lane == 12 + 2 * index, share[0] * (one - mean), 0.0)
            column = column + jnp.where(where_lane == 13 + 2 * index, share[1] * (two - mean), 0.0)
            const_columns = const_columns + jnp.where(
                where_lane == 18 + index, weight * share[1], 0.0
            )
        both_high, both_rest = split(logit_grad + column)
        small = small_ref[...]
        grad_normed = mm(both_high, small, 1, 1) + mm(both_rest, small, 1, 1)
        grad_normed = grad_normed + mixing.normed_weight * grad
        gsmall = mm(mixing.low, both_high, 0, 0) + mm(mixing.low, both_rest, 0, 0)
        gsmall = gsmall + mm(mixing.rest, column.astype(BF), 0, 0)
        const_high, const_rest = split(const_columns)
        gsmall = gsmall + mm(high, const_high, 0, 0) + mm(rest, const_high, 0, 0)
        gsmall = gsmall + mm(high, const_rest, 0, 0)
        back = []
        own = None
        for r in range(z.nq):
            part = lax.rem(q + z.nq - r, z.nq)
            if r:
                for made in onward[r - 1]:
                    made.wait_recv()
            rows = dall_ref[part].reshape(count, z.width)
            grad_hidden = mm(rows, w_ref[2])
            gate, up = gate_ref[part], up_ref[part]
            sig = 1.0 / (1.0 + jnp.exp(-gate))
            silu = gate * sig
            hid_ref[part] = (silu * up).astype(BF)
            up_low = (grad_hidden * silu).astype(BF)
            gate_low = (grad_hidden * up * (sig * (1.0 + gate * (1.0 - sig)))).astype(BF)
            du_ref[part], dg_ref[part] = up_low, gate_low
            result = mm(gate_low, w_ref[0], 1, 1) + mm(up_low, w_ref[1], 1, 1)
            if r == 0:
                own = result
            else:
                part_ref[r - 1] = result.astype(BF)
                made = links.copy(part_ref.at[r - 1], got_ref.at[r - 1], (h, i * z.nq + part))
                made.start()
                back.append(made)
        total = own
        for r, made in enumerate(back):
            made.wait_recv()
            total = total + got_ref[r].astype(F32)
        sum_ref[...] = total.astype(BF).reshape(sum_ref.shape)
        last = return_rows(z, links, h, i, q, others, sum_ref, back_ref)
        every = z.nq * count
        rows = all_ref[...].reshape(every, z.width)
        grown = dall_ref[...].reshape(every, z.width)
        gate_all = dg_ref[...].reshape(every, z.ffp)
        up_all = du_ref[...].reshape(every, z.ffp)
        hidden_all = hid_ref[...].reshape(every, z.ffp)
        for w, (one, two) in enumerate(((rows, gate_all), (rows, up_all), (grown, hidden_all))):
            made = mm(one, two, 0, 0)
            for n in range(z.nb):
                gw_ref[w, n] = made[n * z.drow : (n + 1) * z.drow].astype(BF)
        for made in last:
            made.wait_recv()
        select = (mixing.chosen[0] + mixing.chosen[1]).astype(BF)
        grad_normed = grad_normed + mm(select, back_ref[...].reshape(count, z.width))
        middle = mid_ref[...]
        dm_ref[...] = grad + norm_grad(middle, mixing.root, mixing.gain, grad_normed)
        place = (where_lane == 17).astype(F32).astype(BF)
        high, rest = split(grad_normed * middle * mixing.root)
        gsmall_ref[...] = gsmall + mm(high, place, 0, 0) + mm(rest, place, 0, 0)
        for made in first + back + last:
            made.wait_send()
        for group in onward:
            for made in group:
                made.wait_send()
        for made in side:
            made.wait()

    block = (2 * z.nh, SLOT, z.width)
    ins = [grad, middle, small, logits, grad_logits, routes, target, weights, *saved]
    in_specs = [VMEM] * 12
    outs = [
        struct((z.rows, z.width), F32),
        struct((z.rows, 128), F32),
        struct((z.width, 128), F32),
        struct((3, z.nb, z.drow, z.ffp), BF),
    ]
    out_specs = [VMEM] * 4
    if side_on:
        ins.append(late)
        in_specs.append(ANY)
        outs.append(struct((3, 2, z.drow, z.hidden), BF))
        out_specs.append(ANY)
    return launch(
        body,
        number,
        ins,
        in_specs,
        outs,
        out_specs,
        [
            pltpu.VMEM(block, BF),
            pltpu.VMEM((z.nq,) + block, BF),
            pltpu.VMEM((z.nq - 1, count, z.width), BF),
            pltpu.VMEM((z.nq - 1, count, z.width), BF),
            pltpu.VMEM(block, BF),
            pltpu.VMEM(block, BF),
            pltpu.VMEM((z.nq, count, z.ffp), BF),
            pltpu.VMEM((z.nq, count, z.ffp), BF),
            pltpu.VMEM((z.nq, count, z.ffp), BF),
        ],
        expert_copies(z) + 3 * z.nb,
    )


def reduce_weights(z, number, pieces, late):
    count = len(pieces)

    def body(*refs):
        full = refs[:count]
        late_ref = refs[count]
        outs = refs[count + 1 : 2 * count + 1]
        landed_ref = refs[2 * count + 1]
        at = 2 * count + 2
        bufs = [refs[at + 4 * p : at + 4 * p + 4] for p in range(count)]
        send, recv, local_sem = refs[at + 4 * count :]
        h, b = lax.axis_index("head"), lax.axis_index("blk")
        y, c, m, n = place_of(z, h, b)
        blk_peers = [(h, lax.rem(b + r, z.nb)) for r in range(1, z.nb)]
        core_peer = (y * z.hl + 1 - c, b)
        ys = [lax.rem(y + r, z.hh) for r in range(1, z.hh)]
        y_peers = [(t * z.hl + c, b) for t in ys]
        greet(blk_peers + [core_peer] + y_peers)
        links = Links(send, recv)
        ns = [lax.rem(n + r, z.minor) for r in range(1, z.minor)]
        ms = [lax.rem(m + r, z.major) for r in range(1, z.major)]
        minor_peers = [(h, m * z.minor + t) for t in ns]
        major_peers = [(h, t * z.minor + n) for t in ms]
        made = [[] for _ in range(count)]
        done = []
        for p in range(count):
            made[p] = [links.copy(full[p].at[:, 1 - c], bufs[p][0], core_peer)]
            made[p][0].start()
            done += made[p]
        side = grad_copies(z, h, b, late_ref, landed_ref, links, local_sem)
        for one in side:
            one.start()
        for p in range(count):
            kind = full[p].dtype
            one, two, three, four = bufs[p]
            for copy in made[p]:
                copy.wait_recv()
            for a in range(z.hh):
                for d in range(z.major):
                    one[a, d] = (
                        one[a, d].astype(F32) + full[p][a, c, d].astype(F32)
                    ).astype(kind)
            if p % 2 == 0:
                made[p] = [
                    links.copy(one.at[t], two.at[k], peer)
                    for k, (t, peer) in enumerate(zip(ys, y_peers))
                ]
            else:
                made[p] = [
                    links.copy(one.at[:, :, t], two.at[k], peer)
                    for k, (t, peer) in enumerate(zip(ns, minor_peers))
                ]
            for copy in made[p]:
                copy.start()
            done += made[p]
        for p in range(count):
            kind = full[p].dtype
            one, two, three, four = bufs[p]
            for copy in made[p]:
                copy.wait_recv()
            if p % 2 == 0:
                for d in range(z.major):
                    total = one[y, d].astype(F32)
                    for k in range(z.hh - 1):
                        total = total + two[k, d].astype(F32)
                    two[0, d] = total.astype(kind)
                made[p] = [
                    links.copy(two.at[0, :, t], three.at[k], peer)
                    for k, (t, peer) in enumerate(zip(ns, minor_peers))
                ]
            else:
                for a in range(z.hh):
                    for d in range(z.major):
                        total = one[a, d, n].astype(F32)
                        for k in range(z.minor - 1):
                            total = total + two[k, a, d].astype(F32)
                        two[0, a, d] = total.astype(kind)
                made[p] = [
                    links.copy(two.at[0, t], three.at[k], peer)
                    for k, (t, peer) in enumerate(zip(ys, y_peers))
                ]
            for copy in made[p]:
                copy.start()
            done += made[p]
        for p in range(count):
            kind = full[p].dtype
            one, two, three, four = bufs[p]
            for copy in made[p]:
                copy.wait_recv()
            for d in range(z.major):
                if p % 2 == 0:
                    total = two[0, d, n].astype(F32)
                    for k in range(z.minor - 1):
                        total = total + three[k, d].astype(F32)
                else:
                    total = two[0, y, d].astype(F32)
                    for k in range(z.hh - 1):
                        total = total + three[k, d].astype(F32)
                three[0, d] = total.astype(kind)
            made[p] = [
                links.copy(three.at[0, t], four.at[k], peer)
                for k, (t, peer) in enumerate(zip(ms, major_peers))
            ]
            for copy in made[p]:
                copy.start()
            done += made[p]
        for p in range(count):
            one, two, three, four = bufs[p]
            for copy in made[p]:
                copy.wait_recv()
            total = three[0, m].astype(F32)
            for k in range(z.major - 1):
                total = total + four[k].astype(F32)
            outs[p][...] = total
        for copy in done:
            copy.wait_send()
        for copy in side:
            copy.wait()

    scratch = []
    for p, piece in enumerate(pieces):
        block, kind = piece.shape[4:], piece.dtype
        scratch.append(pltpu.VMEM((z.hh, z.major, z.minor) + block, kind))
        if p % 2 == 0:
            scratch.append(pltpu.VMEM((z.hh - 1, z.major, z.minor) + block, kind))
            scratch.append(pltpu.VMEM((z.minor - 1, z.major) + block, kind))
        else:
            scratch.append(pltpu.VMEM((z.minor - 1, z.hh, z.major) + block, kind))
            scratch.append(pltpu.VMEM((z.hh - 1, z.major) + block, kind))
        scratch.append(pltpu.VMEM((z.major - 1,) + block, kind))
    steps = z.major - 1 + z.minor - 1 + z.hh - 1 + 1
    return launch(
        body,
        number,
        [*pieces, late],
        [VMEM] * count + [ANY],
        [struct(p.shape[4:], F32) for p in pieces] + [struct((3, 2, z.drow, z.hidden), BF)],
        [VMEM] * count + [ANY],
        scratch,
        count * steps + 3 * z.nb,
    )


def rotary(position, columns):
    lane = jnp.arange(columns, dtype=jnp.int32) % HD
    freqs = 10000.0 ** (-(2.0 * (lane % (HD // 2)).astype(F32)) / HD)
    angles = position[:, None] * freqs[None, :]
    return jnp.cos(angles), jnp.where(lane[None, :] < HD // 2, -jnp.sin(angles), jnp.sin(angles))


def slot_targets(routes, order):
    ids, ranks = routes.reshape(LAYERS, -1), order.reshape(LAYERS, -1)
    before = (ids[:, :, None] == ids[:, None, :]) & (ranks[:, None, :] < ranks[:, :, None])
    slot = jnp.sum(before.astype(jnp.int32), axis=-1)
    kept = (ids < NF) & (slot < CAP)
    return jnp.where(kept, ids * SLOT + slot, -1).reshape(routes.shape)


def to_groups(v, axis_size):
    lead, width = v.shape[:-1], axis_size
    part = width // GROUPS
    q, k, w = v[..., :width], v[..., width : 2 * width], v[..., 2 * width :]
    k = k.reshape(lead + (GROUPS, 1, part))
    w = w.reshape(lead + (GROUPS, 1, part))
    kv = jnp.concatenate([k, w], axis=-2).reshape(lead + (2 * width,))
    return jnp.concatenate([kv, q], axis=-1)


def from_groups(v, axis_size):
    lead, width = v.shape[:-1], axis_size
    part = width // GROUPS
    kv = v[..., : 2 * width].reshape(lead + (GROUPS, 2, part))
    k = kv[..., 0, :].reshape(lead + (width,))
    w = kv[..., 1, :].reshape(lead + (width,))
    return jnp.concatenate([v[..., 2 * width :], k, w], axis=-1)


def local(
    tokens,
    prev_logits,
    norm_gains,
    attn_in_weight,
    attn_out_weight,
    router_weight,
    const_mix,
    const_values,
    expert_gate,
    expert_up,
    expert_down,
    routes,
    order,
    cotangent,
):
    rows, width = tokens.shape
    z = Shape(lax.axis_size("head"), lax.axis_size("blk"), rows, width, expert_gate.shape[3])
    b = lax.axis_index("blk")
    position = (b * rows + jnp.arange(rows, dtype=jnp.int32)).astype(F32)
    cos_q, sin_q = rotary(position, width)
    flat = jnp.arange(384) < 192
    cos_kv = jnp.where(flat[None, :], cos_q[:, :384], 1.0)
    sin_kv = jnp.where(flat[None, :], sin_q[:, :384], 0.0)
    tables = (cos_q, sin_q, cos_kv, sin_kv)
    targets = slot_targets(routes, order)
    parts = (expert_gate, expert_up, expert_down)

    in_shards = to_groups(attn_in_weight, width)
    smalls = jnp.concatenate(
        [
            router_weight,
            const_mix,
            jnp.transpose(norm_gains, (0, 2, 1)),
            jnp.transpose(const_values, (0, 2, 1)),
            jnp.zeros((LAYERS, z.shard, 128 - NE - 8), BF),
        ],
        axis=-1,
    )
    shards = []
    for layer in range(LAYERS):
        shards += [in_shards[layer], attn_out_weight[layer], smalls[layer]]
    gathered = gather_weights(z, 0, shards, parts, 0)
    whole = [v.reshape(width, v.shape[-1]) for v in gathered[:-1]]
    in_weights, out_weights, small = whole[0::3], whole[1::3], whole[2::3]
    weights = [gathered[-1].reshape(3, width, z.ffp), None]

    state = tokens.astype(F32)
    logits = jnp.pad(prev_logits, ((0, 0), (0, 128 - NE)))
    saved = []
    for layer in range(LAYERS):
        ahead = parts if layer + 1 < LAYERS else None
        made = attend(
            z,
            1 + layer,
            state,
            small[layer],
            in_weights[layer],
            out_weights[layer],
            tables,
            ahead,
            layer + 1,
        )
        middle, low = made[:2]
        if ahead is not None:
            weights[layer + 1] = made[7].reshape(3, width, z.ffp)
        after = expert_forward(
            z,
            3 + layer,
            middle,
            small[layer],
            logits,
            routes[layer],
            targets[layer],
            weights[layer],
        )
        saved.append((state, low, middle, after[1], made[2:7], after[2:6]))
        state, logits = after[:2]

    grad = cotangent.astype(F32)
    grad_logits = jnp.zeros((rows, 128), F32)
    in_grads, out_grads, small_grads, expert_grads = {}, {}, {}, {}
    late = None
    for layer in reversed(range(LAYERS)):
        state_in, low, middle, layer_logits, attention, experts = saved[layer]
        made = expert_back(
            z,
            5 + layer,
            grad,
            middle,
            small[layer],
            layer_logits,
            grad_logits,
            routes[layer],
            targets[layer],
            weights[layer],
            experts,
            late,
        )
        if late is not None:
            expert_grads[layer + 1] = made[4]
        grad_mid, grad_logits, gsmall, late = made[:4]
        grad, in_grads[layer], out_grads[layer], gain = attend_back(
            z,
            7 + layer,
            grad_mid,
            state_in,
            low,
            small[layer],
            in_weights[layer],
            out_weights[layer],
            tables,
            attention,
        )
        small_grads[layer] = gsmall + gain
    grid = (z.hh, z.hl, z.major, z.minor, z.shard)
    pieces = []
    for layer in reversed(range(LAYERS)):
        pieces += [in_grads[layer], out_grads[layer], small_grads[layer]]
    pieces = [v.reshape(grid + (v.shape[-1],)) for v in pieces]
    reduced = reduce_weights(z, 9, pieces, late)
    expert_grads[0] = reduced[-1]
    in_sum = jnp.stack([reduced[3], reduced[0]])
    out_sum = jnp.stack([reduced[4], reduced[1]])
    small_sum = jnp.stack([reduced[5], reduced[2]])
    expert_out = [
        jnp.stack([expert_grads[layer][w] for layer in range(LAYERS)]).astype(F32)
        for w in range(3)
    ]
    return (
        state.astype(BF),
        grad,
        grad_logits[:, :NE],
        jnp.transpose(small_sum[:, :, 16:18], (0, 2, 1)),
        from_groups(in_sum, width),
        out_sum,
        small_sum[:, :, :NE],
        small_sum[:, :, NE : NE + 4],
        jnp.transpose(small_sum[:, :, 18:20], (0, 2, 1)),
        expert_out[0],
        expert_out[1],
        expert_out[2],
    )


def solution(mesh):
    placed = (
        P(("head", "blk"), None),
        P(("head", "blk"), None),
        P(None, None, ("head", "blk")),
        P(None, ("head", "blk"), None),
        P(None, ("head", "blk"), None),
        P(None, ("head", "blk"), None),
        P(None, ("head", "blk"), None),
        P(None, None, ("head", "blk")),
        P(None, "head", "blk", None),
        P(None, "head", "blk", None),
        P(None, "head", "blk", None),
        P(None, ("head", "blk"), None),
        P(None, ("head", "blk"), None),
        P(("head", "blk"), None),
    )
    return jax.shard_map(
        local,
        mesh=mesh,
        in_specs=placed,
        out_specs=(
            P(("head", "blk"), None),
            P(("head", "blk"), None),
            P(("head", "blk"), None),
            P(None, None, ("head", "blk")),
            P(None, ("head", "blk"), None),
            P(None, ("head", "blk"), None),
            P(None, ("head", "blk"), None),
            P(None, ("head", "blk"), None),
            P(None, None, ("head", "blk")),
            P(None, "head", "blk", None),
            P(None, "head", "blk", None),
            P(None, "head", "blk", None),
        ),
        check_vma=False,
    )
```

time: 2990 us -> 757 us (0.25)
  waiting for transfers between devices: 1500 us -> 0 us
  blocking collectives: 719 us -> 0 us
  Pallas kernels: 0 us -> 708 us
  local copies, waits for them, and re-layouts: 275 us -> 16.9 us
  matrix products: 251 us -> 0 us
  other arithmetic: 115 us -> 20 us
  starting transfers between devices: 65.5 us -> 0 us
    reduce_scatter x10 -> x0, waiting for transfers between devices: 1160 us -> none  [the longest x2 247 us: reduce_grads(): lax.psum_scatter(in_grad, ('head', 'blk'), scatter_dimension=1, tiled=True)]
    pallas_call x0 -> x10, Pallas kernels: none -> 708 us  [the longest x9 609 us: launch(): pl.pallas_call(body, out_shape=outs, in_specs=in_specs, out_specs=out_spe...]
    all_gather x12 -> x0, blocking collectives: 672 us -> none  [the longest x2 141 us: local(): lax.all_gather(router_weight[layer], ('head', 'blk'), axis=0, tiled=True)]
    dot_general x202 -> x0, matrix products: 251 us -> none  [the longest x16 21.4 us: grad_block(): jnp.einsum(SCORE_FORM[grouped], own_queries, key_block, preferred_element...]
    all_gather x18 -> x0, waiting for transfers between devices: 208 us -> none  [the longest x2 94.1 us: local(): lax.all_gather(expert_gate[layer], 'blk', axis=1, tiled=True)]
    dynamic_slice x96 -> x0, local copies, waits for them, and re-layouts: 92.6 us -> none  [over_rows(): lax.scan(step, carry, (jnp.arange(blocks, dtype=jnp.int32), stacked))]
    unnamed x30 -> x0, waiting for transfers between devices: 78.6 us -> none
    all_to_all x18 -> x0, starting transfers between devices: 63.4 us -> none  [the longest x2 7.97 us: local(): lax.all_to_all(slot_low, 'head', split_axis=0, concat_axis=0, tiled=True)]
  transfers between devices with their start and end apart: 47 -> 0, of which waited for: 29 -> 0; matrix products, arithmetic and copies ran while one was open for 16% -> 0% of each run, Pallas kernels for 0% -> 0%
where the time goes in v1:
time: 757 us; the launch traced here: 746 us
  Pallas kernels  708 us (94%)
  other arithmetic  20 us (3%)
  local copies, waits for them, and re-layouts  16.9 us (2%)
    pallas_call x9, Pallas kernels, launch(): pl.pallas_call(body, out_shape=outs, in_specs=in_specs, out_specs=out_spe...  609 us
    pallas_call x1, Pallas kernels, gather_weights(): pl.pallas_call(body, out_shape=[struct(shape + s.shape, BF) for s in shar...  98.4 us

profile of v1, /device:TPU:8, one launch (start us, length us, event | category | flops | bytes accessed | tf_op | source)
XLA Modules:
  0.0 746.0 jit_solution(9320767505848225702)
XLA Ops:
  0.7 1.7 convert_element_type.37.refs_0_.refs_1_
  2.4 1.0 fusion.22
  4.4 0.7 fusion.4
  6.9 98.4 %shard_map.229 = (bf16[2,2,4,2,24,2304]{5,4,3,2,1,0:T(8,128)(2,1)}, bf16[2,2,4,2,24,768]{5,4,3,2,1,0:T(8,128)(2,1)}, bf16[2,2,4,2,24,128]{5,4,3,2,1,0:T(8,128)(2...) custom-call(bf16[24,2304]{1,0:T(8,128)(2,1)} %get-tuple-element.175., ...), custom_call_target="tpu_custom_call" | custom-call | tf_op jit(solution)/shard_map/pallas_call | solution.py:231
  105.4 1.5 negate_select_fusion
  106.9 0.9 slice_select_fusion
  107.9 90.9 %shard_map.230 = (f32[128,768]{1,0:T(8,128)}, bf16[128,768]{1,0:T(8,128)(2,1)}, bf16[4,128,256]{2,1,0:T(8,128)(2,1)}, bf16[8,128,384]{2,1,0:T(8,128)(2,1)}, f32[...) custom-call(f32[128,768]{1,0:T(8,128)} %convert_element_type.37.refs_, ...), custom_call_target="tpu_custom_call" | custom-call | tf_op jit(solution)/shard_map/pallas_call | solution.py:98
  201.2 0.8 squeeze.41.refs_4_.refs_6_
  201.9 56.3 %shard_map.231 = (f32[128,768]{1,0:T(8,128)}, f32[128,128]{1,0:T(8,128)}, bf16[8,32,768]{2,1,0:T(8,128)(2,1)}, bf16[4,8,32,768]{3,2,1,0:T(8,128)(2,1)}, f32[4,256,512]{2,1,0:T(8,128)}, /*index=5*/f32[4,256,512]{2,1,0:T(8,128)}) custom-call(f32[128,768]{1,0:T(8,128)} %get-tuple-element.73.refs_0_.refs_1_, bf16[768,128]{1,0:T(8,128)(2,1)} %bitcast.62, ...), custom_call_target="tpu_custom_call" | custom-call | tf_op jit(solution)/shard_map/pallas_call | solution.py:98
  258.2 44.4 %shard_map.232 = (f32[128,768]{1,0:T(8,128)}, bf16[128,768]{1,0:T(8,128)(2,1)}, bf16[4,128,256]{2,1,0:T(8,128)(2,1)}, bf16[8,128,384]{2,1,0:T(8,128)(2,1)}, f32[...) custom-call(f32[128,768]{1,0:T(8,128)} %get-tuple-element.75.refs_0_.refs_1_, ...), custom_call_target="tpu_custom_call" | custom-call | tf_op jit(solution)/shard_map/pallas_call | solution.py:98
  302.6 0.8 squeeze.43.refs_4_.refs_6_
  303.4 57.9 %shard_map.233 = (f32[128,768]{1,0:T(8,128)}, f32[128,128]{1,0:T(8,128)}, bf16[8,32,768]{2,1,0:T(8,128)(2,1)}, bf16[4,8,32,768]{3,2,1,0:T(8,128)(2,1)}, f32[4,256,512]{2,1,0:T(8,128)}, /*index=5*/f32[4,256,512]{2,1,0:T(8,128)}) custom-call(f32[128,768]{1,0:T(8,128)} %get-tuple-element.79.refs_0_.refs_1_, bf16[768,128]{1,0:T(8,128)(2,1)} %bitcast.58, ...), custom_call_target="tpu_custom_call" | custom-call | tf_op jit(solution)/shard_map/pallas_call | solution.py:98
  361.3 1.7 convert_element_type.41
  363.0 0.8 convert_element_type.42.refs_0_
  364.4 62.2 %shard_map.234 = (f32[128,768]{1,0:T(8,128)}, f32[128,128]{1,0:T(8,128)}, f32[768,128]{1,0:T(8,128)}, bf16[3,8,96,512]{3,2,1,0:T(8,128)(2,1)}) custom-call(f32[128,768]{1,0:T(8,128)} %convert_element_type.42.refs_0_, f32[128,768]{1,0:T(8,128)} %get-tuple-element.79.refs_0_.refs_1_, bf16[768,128]{1,0:T(8,128)(2,1)} %bitcast.59, ...), custom_call_target="tpu_custom_call" | custom-call | tf_op jit(solution)/shard_map/pallas_call | solution.py:98
  426.6 50.3 %shard_map.235 = (f32[128,768]{1,0:T(8,128)}, bf16[32,24,2304]{2,1,0:T(8,128)(2,1)}, bf16[32,24,768]{2,1,0:T(8,128)(2,1)}, f32[768,128]{1,0:T(8,128)}) custom-call(f32[128,768]{1,0:T(8,128)} %get-tuple-element.88.refs_0_, f32[128,768]{1,0:T(8,128)} %get-tuple-element.75.refs_0_.refs_1_, bf16[128,768]{1,0:T(8,128)(2,1)} %get-tuple-element.89.refs_2_, ...), custom_call_target="tpu_custom_call" | custom-call | tf_op jit(solution)/shard_map/pallas_call | solution.py:98
  476.9 99.4 %shard_map.236 = (f32[128,768]{1,0:T(8,128)}, f32[128,128]{1,0:T(8,128)}, f32[768,128]{1,0:T(8,128)}, bf16[3,8,96,512]{3,2,1,0:T(8,128)(2,1)}, bf16[3,2,96,2048]{3,2,1,0:T(8,128)(2,1)}) custom-call(f32[128,768]{1,0:T(8,128)} %get-tuple-element.95.refs_0_, f32[128,768]{1,0:T(8,128)} %get-tuple-element.73.refs_0_.refs_1_, bf16[768,128]{1,0:T(8,128)(2,1)} %bitcast.63, ...), custom_call_target="tpu_custom_call" | custom-call | tf_op jit(solution)/shard_map/pallas_call | solution.py:98
  576.4 47.5 %shard_map.237 = (f32[128,768]{1,0:T(8,128)}, bf16[32,24,2304]{2,1,0:T(8,128)(2,1)}, bf16[32,24,768]{2,1,0:T(8,128)(2,1)}, f32[768,128]{1,0:T(8,128)}) custom-call(f32[128,768]{1,0:T(8,128)} %get-tuple-element.102.refs_0_, f32[128,768]{1,0:T(8,128)} %convert_element_type.37.refs_0_.refs_1_, bf16[128,768]{1,0:T(8,128)(2,1)} %get-tuple-element.103.refs_2_, ...), custom_call_target="tpu_custom_call" | custom-call | tf_op jit(solution)/shard_map/pallas_call | solution.py:98
  624.6 0.8 add.49
  625.4 1.8 add.50
  627.1 100.6 %shard_map.238 = (f32[24,2304]{1,0:T(8,128)}, f32[24,768]{1,0:T(8,128)}, f32[24,128]{1,0:T(8,128)}, f32[24,2304]{1,0:T(8,128)}, f32[24,768]{1,0:T(8,128)}, /*ind...) custom-call(bf16[2,2,4,2,24,2304]{5,4,3,2,1,0:T(8,128)(2,1)} %bitcast.55, bf16[2,2,4,2,24,768]{5,4,3,2,1,0:T(8,128)(2,1)} %bitcast.67, ...), custom_call_target="tpu_custom_call" | custom-call | tf_op jit(solution)/shard_map/pallas_call | solution.py:98
  727.7 0.9 fusion.9
  729.3 1.0 pad_maximum_fusion.1
  730.7 1.8 slice_reduce_fusion.1
  732.5 1.1 reshape_squeeze.7
  733.8 0.8 fusion.1
  734.6 1.6 pad_maximum_fusion.3
  736.1 0.7 copy.69
  738.4 1.5 copy-done.3
  740.0 3.1 maximum_convert_fusion
  743.2 1.9 maximum_convert_fusion.2
  745.0 0.7 copy.73
  (82 shorter events, 9.5 us)
Async XLA Ops:
  0.6 4.5 copy-start.13
  0.7 5.1 copy-start.17
  0.7 5.2 copy-start.20
  0.7 5.3 copy-start.21
  0.7 5.4 copy-start.22
  106.9 0.9 copy-start
  106.9 1.0 copy-start.1
  107.9 90.9 %copy-start.16 = (f32[128,12]{0,1:T(8,128)S(1)}, f32[128,12]{0,1:T(8,128)}, u32[]{:S(2)}) copy-start(f32[128,12]{0,1:T(8,128)} %param.15) | copy-start | bytes 18436
  107.9 91.7 %copy-start.18 = (s32[2,128,2]{1,2,0:T(2,128)S(1)}, s32[2,128,2]{1,2,0:T(2,128)}, u32[]{:S(2)}) copy-start(s32[2,128,2]{1,2,0:T(2,128)} %param.25) | copy-start | bytes 6148
  107.9 92.5 %copy-start.19 = (s32[2,128,2]{1,2,0:T(2,128)S(1)}, s32[2,128,2]{1,2,0:T(2,128)}, u32[]{:S(2)}) copy-start(s32[2,128,2]{1,2,0:T(2,128)} %param.26) | copy-start | bytes 6148
  302.6 60.4 %copy-start.10 = (bf16[128,768]{1,0:T(8,128)(2,1)S(1)}, bf16[128,768]{1,0:T(8,128)(2,1)}, u32[]{:S(2)}) copy-start(bf16[128,768]{1,0:T(8,128)(2,1)} %param.27) | copy-start | bytes 589828
  576.3 47.5 %copy-start.15 = (f32[128,128]{1,0:T(8,128)S(1)}, f32[128,128]{1,0:T(8,128)}, u32[]{:S(2)}) copy-start(f32[128,128]{1,0:T(8,128)} %get-tuple-element.110) | copy-start | bytes 196612
  576.3 48.2 %copy-start.7 = (f32[768,128]{1,0:T(8,128)S(1)}, f32[768,128]{1,0:T(8,128)}, u32[]{:S(2)}) copy-start(f32[768,128]{1,0:T(8,128)} %get-tuple-element.113) | copy-start | bytes 1179652
  576.3 48.2 %copy-start.8 = (f32[768,128]{1,0:T(8,128)S(1)}, f32[768,128]{1,0:T(8,128)}, u32[]{:S(2)}) copy-start(f32[768,128]{1,0:T(8,128)} %get-tuple-element.114) | copy-start | bytes 1179652
  576.4 49.0 %copy-start.9 = (f32[768,128]{1,0:T(8,128)S(1)}, f32[768,128]{1,0:T(8,128)}, u32[]{:S(2)}) copy-start(f32[768,128]{1,0:T(8,128)} %get-tuple-element.117) | copy-start | bytes 1179652
  727.7 6.0 copy-start.4
  727.7 6.0 copy-start.5
  729.3 6.8 copy-start.11
  729.3 6.8 copy-start.12
  730.3 7.9 %copy-start.2 = (bf16[3,2,96,2048]{3,2,1,0:T(8,128)(2,1)S(1)}, bf16[3,2,96,2048]{3,2,1,0:T(8,128)(2,1)}, u32[]{:S(2)}) copy-start(bf16[3,2,96,2048]{3,2,1,0:T(8,128)(2,1)} %get-tuple-element.127) | copy-start | bytes 7077892
  730.7 3.8 copy-start.14
  738.2 1.7 copy-start.3
  743.1 1.9 copy-start.6

commit v2 on v0

v2 whole, which is shorter than its diff:
```python
import jax
import jax.numpy as jnp
import numpy as np
from jax import lax
from jax.experimental import pallas as pl
from jax.experimental.pallas import tpu as pltpu
from jax.sharding import PartitionSpec as P

HEADS = 12
HD = 64
NF = 8
TOP = 2
LAYERS = 2
NE = 12
CAP = 26
SLOT = 32
GROUPS = 4
EPSILON = 1e-05
NEGATIVE = -1e30
SCALE = HD ** (-0.5)
VMEM_BYTES = 65200 * 1024

BF = jnp.bfloat16
F32 = jnp.float32
MESH = pl.DeviceIdType.MESH
VMEM = pl.BlockSpec(memory_space=pltpu.VMEM)
ANY = pl.BlockSpec(memory_space=pl.ANY)


def mm(a, b, ca=1, cb=0):
    return lax.dot_general(a, b, (((ca,), (cb,)), ((), ())), preferred_element_type=F32)


def split(v):
    high = v.astype(BF)
    return high, (v - high.astype(F32)).astype(BF)


def lanes(shape):
    return lax.broadcasted_iota(jnp.int32, shape, len(shape) - 1)


def lane_of(v, index):
    return jnp.sum(jnp.where(lanes(v.shape) == index, v, 0.0), axis=-1, keepdims=True)


def rows_of(small):
    pick = lax.broadcasted_iota(jnp.int32, (8, 128), 0) + 16 == lanes((8, 128))
    return mm(pick.astype(F32).astype(BF), small, 1, 1)


def swap_halves(v):
    width = v.shape[-1]
    low_half = lanes(v.shape) % HD < HD // 2
    return jnp.where(
        low_half, pltpu.roll(v, width - HD // 2, 1), pltpu.roll(v, HD // 2, 1)
    )


def rotate(v, cosine, sine):
    return v * cosine + swap_halves(v) * sine


def rotate_back(v, cosine, sine):
    return v * cosine - swap_halves(v) * sine


def norm_grad(v, root, gain, grad):
    scaled = grad * gain
    inner = jnp.mean(v * scaled, axis=-1, keepdims=True)
    return root * scaled - v * (root * root * root * inner)


class Shape:
    def __init__(self, nh, nb, rows, width, hidden):
        self.nh, self.nb, self.rows, self.width, self.hidden = nh, nb, rows, width, hidden
        self.hh = nh // 2
        self.splits = nb // GROUPS
        self.nq = 2 * self.splits
        self.experts = self.hh * GROUPS
        self.ffp = hidden // self.nq
        self.drow = width // nb
        self.shards = nh * nb
        self.shard = width // self.shards
        self.count = self.experts * SLOT


class Links:
    def __init__(self, z, send, recv):
        self.z, self.send, self.recv, self.used = z, send, recv, 0
        self.sent, self.sent_if = [], []
        h, b = lax.axis_index("head"), lax.axis_index("blk")
        self.h, self.b = h, b
        self.y, self.c = h // 2, lax.rem(h, 2)
        self.g, self.s = b // z.splits, lax.rem(b, z.splits)
        self.q = self.c * z.splits + self.s

    def device(self, y, c, g, s):
        return (y * 2 + c, g * self.z.splits + s)

    def near(self, dy=0, dc=0, dg=0, ds=0):
        z = self.z
        return self.device(
            lax.rem(self.y + dy, z.hh),
            lax.rem(self.c + dc, 2),
            lax.rem(self.g + dg, GROUPS),
            lax.rem(self.s + ds, z.splits),
        )

    def beside(self):
        low = lax.rem(self.g, 2)
        return self.device(self.y, self.c, self.g + 1 - 2 * low, self.s)

    def up(self, value, step, size):
        return lax.rem(value + step, size)

    def down(self, value, step, size):
        return lax.rem(value + size - step, size)

    def take(self, amount):
        first = self.used
        self.used += amount
        return first

    def remote(self, src, dst, device, send, recv):
        return pltpu.make_async_remote_copy(
            src_ref=src,
            dst_ref=dst,
            send_sem=self.send.at[send],
            recv_sem=self.recv.at[recv],
            device_id=device,
            device_id_type=MESH,
        )

    def push(self, src, dst, device):
        place = self.take(1)
        made = self.remote(src, dst, device, place, place)
        made.start()
        self.sent.append(made)
        return made

    def push_or_keep(self, src, dst, device, here, send, recv):
        made = self.remote(src, dst, device, send, recv)

        @pl.when(jnp.logical_not(here))
        def _():
            made.start()

        @pl.when(here)
        def _():
            pltpu.make_async_copy(src, dst, self.recv.at[recv]).start()

        self.sent_if.append((here, made))

    def arrived(self, place, recv):
        pltpu.make_async_copy(place, place, self.recv.at[recv]).wait()

    def settle(self):
        for made in self.sent:
            made.wait_send()
        for here, made in self.sent_if:

            @pl.when(jnp.logical_not(here))
            def _(made=made):
                made.wait_send()

        self.sent, self.sent_if = [], []


def greet(devices):
    barrier = pltpu.get_barrier_semaphore()
    for device in devices:
        pl.semaphore_signal(barrier, inc=1, device_id=device, device_id_type=MESH)
    pl.semaphore_wait(barrier, len(devices))


def greet_all(net):
    z = net.z
    known = [net.near(dg=dg, ds=ds) for dg in range(GROUPS) for ds in range(z.splits) if dg or ds]
    known += [
        net.near(dc=1, dg=dg, ds=ds) for dg in range(GROUPS) for ds in range(z.splits)
    ]
    known += [
        net.near(dy=dy, dg=dg) for dy in range(1, z.hh) for dg in range(GROUPS)
    ]
    greet(known)


class Names:
    def __init__(self, **more):
        self.__dict__.update(more)


class Beside:
    start = sent = mid = out = rows = side = last = ()
    rows_back = side_back = last_back = back_sent = back_out = ()
    back = {}

    def __init__(self, **more):
        self.__dict__.update(more)


def act(functions):
    for function in functions:
        function()


def launch(body, number, z, ins, outs, scratch, copies, same=()):
    names = list(ins) + list(outs) + list(scratch) + ["send", "recv"]

    def kernel(*refs):
        held = Names(**dict(zip(names, refs)))
        net = Links(z, held.send, held.recv)
        greet_all(net)
        body(held, net)
        net.settle()
        assert net.used <= copies, net.used

    made = pl.pallas_call(
        kernel,
        out_shape=[v[0] for v in outs.values()],
        in_specs=[v[1] for v in ins.values()],
        out_specs=[v[1] for v in outs.values()],
        scratch_shapes=list(scratch.values())
        + [pltpu.SemaphoreType.DMA((copies,)), pltpu.SemaphoreType.DMA((copies,))],
        input_output_aliases={list(ins).index(i): list(outs).index(o) for i, o in same},
        compiler_params=pltpu.CompilerParams(
            collective_id=number, has_side_effects=True, vmem_limit_bytes=VMEM_BYTES
        ),
    )(*[v[0] for v in ins.values()])
    return Names(**dict(zip(outs, made)))


def struct(shape, kind):
    return jax.ShapeDtypeStruct(shape, kind)


class NearWeights:
    def __init__(self, net, part, layer, landed):
        self.net, self.part, self.layer, self.landed = net, part, layer, landed
        self.first = net.take(GROUPS)

    def start(self):
        net = self.net
        for dc in range(2):
            for dl in range(2):
                device, src = weight_source(net, self.part, self.layer, dc, 0, dl)
                dst, place, at = self.landed.at[net.g], self.first + 2 * dc + dl, self.first + net.g
                if dc or dl:
                    made = net.remote(src, dst, device, place, at)
                    made.start()
                    net.sent.append(made)
                else:
                    net.push_or_keep(src, dst, device, net.g // 2 == net.c, place, at)

    def wait(self):
        for n in range(GROUPS):
            self.net.arrived(self.landed.at[n], self.first + n)


class FarWeights:
    def __init__(self, net, part, layer, near, landed):
        self.net, self.part, self.layer, self.landed = net, part, layer, landed
        self.first = net.take(net.z.nb)
        for n in range(GROUPS):
            at = n * net.z.splits + net.s
            pltpu.make_async_copy(near.at[n], landed.at[at], net.recv.at[self.first + at]).start()

    def start(self):
        net, z = self.net, self.net.z
        place = self.first
        for ds in range(1, z.splits):
            for dc in range(2):
                for dl in range(2):
                    device, src = weight_source(net, self.part, self.layer, dc, ds, dl)
                    dst = self.landed.at[net.b]
                    made = net.remote(src, dst, device, place, self.first + net.b)
                    made.start()
                    net.sent.append(made)
                    place += 1

    def wait(self):
        for n in range(self.net.z.nb):
            self.net.arrived(self.landed.at[n], self.first + n)


def weight_source(net, part, layer, dc, ds, dl):
    z = net.z
    e = lax.rem(net.g + dl, 2)
    c, s = net.up(net.c, dc, 2), net.up(net.s, ds, z.splits)
    cols = pl.ds(pl.multiple_of((c * z.splits + s) * z.ffp, 128), z.ffp)
    return net.device(net.y, c, 2 * net.c + e, s), part.at[layer, e, :, cols]


class GradMove:
    def __init__(self, net, grads, landed):
        self.net, self.grads, self.landed = net, grads, landed
        self.first = net.take(net.z.nb)

    def near(self):
        self.start([r for r in range(self.net.z.nb) if r % self.net.z.splits == 0])

    def far(self):
        self.start([r for r in range(self.net.z.nb) if r % self.net.z.splits])

    def start(self, steps):
        net, z = self.net, self.net.z
        e = lax.rem(net.g, 2)
        cols = pl.ds(pl.multiple_of(net.q * z.ffp, 128), z.ffp)
        at = self.first + e * z.nq + net.q
        for r in steps:
            t = net.up(net.b, r, z.nb)
            src, dst = self.grads.at[t], self.landed.at[e, :, cols]
            device = (net.y * 2 + net.g // 2, t)
            if r:
                made = net.remote(src, dst, device, self.first + r, at)
                made.start()
                net.sent.append(made)
            else:
                net.push_or_keep(src, dst, device, net.g // 2 == net.c, self.first, at)

    def wait(self, shares=(True, True)):
        net, z = self.net, self.net.z
        for e in range(2):
            for c in range(2):
                for ds in range(z.splits):
                    if shares[1 if ds else 0]:
                        n = c * z.splits + net.up(net.s, ds, z.splits)
                        cols = pl.ds(pl.multiple_of(n * z.ffp, 128), z.ffp)
                        net.arrived(self.landed.at[e, :, cols], self.first + e * z.nq + n)


def cuts_of(names, widths, size):
    return [
        (name, at, min(size, width - at))
        for name, width in zip(names, widths)
        for at in range(0, width, size)
    ]


class Gather:
    STEPS = 6

    def __init__(self, net, pieces, own_sems):
        self.net, self.pieces, self.stage = net, pieces, 0
        at = (net.y, net.c, net.g // 2, lax.rem(net.g, 2), net.s)
        self.keep = []
        for p in range(len(pieces)):
            self.keep.append(
                pltpu.make_async_copy(self.own(p), self.full(p, at), own_sems.at[p])
            )
            self.keep[-1].start()
        self.waiting = [[] for _ in pieces]

    def own(self, p):
        ref, _, first, columns = self.pieces[p]
        return ref.at[:, first : first + columns]

    def full(self, p, at):
        _, ref, first, columns = self.pieces[p]
        return ref.at[at + (slice(None), slice(first, first + columns))]

    def step(self):
        net, z, every = self.net, self.net.z, slice(None)
        y, c, s = net.y, net.c, net.s
        high, low = net.g // 2, lax.rem(net.g, 2)
        splits = [net.near(ds=d) for d in range(1, z.splits)]
        ys = [net.near(dy=d) for d in range(1, z.hh)]
        by_split = [((y, c, every, every, s), splits), ((y, c, every, every, every), ys)]
        by_y = [((y, c, every, every, s), ys), ((every, c, every, every, s), splits)]
        for p in range(len(self.pieces)):
            for made in self.waiting[p]:
                made.wait_recv()
            self.waiting[p] = []
            if self.stage == 1:
                self.keep[p].wait()
            if self.stage == 5:
                continue
            if self.stage == 0:
                at, peers = (y, c, high, low, s), [net.near(dg=2)]
            elif self.stage == 1:
                at, peers = (y, c, every, low, s), [net.beside()]
            elif self.stage == 4:
                at, peers = (every, c, every, every, every), [net.near(dc=1)]
            else:
                at, peers = (by_y if p % 2 else by_split)[self.stage - 2]
            place = self.full(p, at)
            src = self.own(p) if self.stage == 0 else place
            self.waiting[p] = [net.push(src, place, peer) for peer in peers]
        self.stage += 1


class Reduce:
    STEPS = 6

    def __init__(self, net, pieces, bufs, sems):
        self.net, self.pieces, self.bufs, self.stage = net, pieces, bufs, 0
        self.waiting = [[] for _ in pieces]
        self.mine = []
        for p, (full, _, lo, columns) in enumerate(pieces):
            own = full.at[:, net.c, :, :, :, :, slice(lo, lo + columns)]
            self.mine.append(pltpu.make_async_copy(own, bufs[p][5], sems.at[p]))

    def step(self):
        net, z = self.net, self.net.z
        y, c, s = net.y, net.c, net.s
        high, low = net.g // 2, lax.rem(net.g, 2)
        to_y = [(net.up(y, d, z.hh), net.near(dy=d)) for d in range(1, z.hh)]
        to_split = [(net.up(s, d, z.splits), net.near(ds=d)) for d in range(1, z.splits)]
        bits = [(i, j) for i in range(2) for j in range(2)]
        for p, (full, out, lo, columns) in enumerate(self.pieces):
            cut = slice(lo, lo + columns)
            one, two, three, four, five, own = self.bufs[p]
            kind = full.dtype
            for made in self.waiting[p]:
                made.wait_recv()
            moves = []
            split_first = p % 2 == 1
            firsts, seconds = (to_split, to_y) if split_first else (to_y, to_split)
            if self.stage == 0:
                moves = [(full.at[:, 1 - c, :, :, :, :, cut], one, net.near(dc=1))]
                self.mine[p].start()
            elif self.stage == 1:
                self.mine[p].wait()
                for a in range(z.hh):
                    for i, j in bits:
                        total = one[a, i, j].astype(F32) + own[a, i, j].astype(F32)
                        one[a, i, j] = total.astype(kind)
                for k, (t, peer) in enumerate(firsts):
                    moves.append((one.at[:, :, :, t] if split_first else one.at[t], two.at[k], peer))
            elif self.stage == 2:
                for i, j in bits:
                    for a in range(z.hh) if split_first else (0,):
                        at = (a, i, j) if split_first else (i, j)
                        total = (one[a, i, j, s] if split_first else one[y, i, j]).astype(F32)
                        for k in range(len(firsts)):
                            total = total + two[(k,) + at].astype(F32)
                        two[(0,) + at] = total.astype(kind)
                for k, (t, peer) in enumerate(seconds):
                    moves.append((two.at[0, t] if split_first else two.at[0, :, :, t], three.at[k], peer))
            elif self.stage == 3:
                for i, j in bits:
                    total = (two[0, y, i, j] if split_first else two[0, i, j, s]).astype(F32)
                    for k in range(len(seconds)):
                        total = total + three[k, i, j].astype(F32)
                    three[0, i, j] = total.astype(kind)
                moves = [(three.at[0, :, 1 - low], four, net.beside())]
            elif self.stage == 4:
                for i in range(2):
                    four[i] = (three[0, i, low].astype(F32) + four[i].astype(F32)).astype(kind)
                moves = [(four.at[1 - high], five, net.near(dg=2))]
            else:
                out[:, cut] = four[high].astype(F32) + five[...].astype(F32)
            self.waiting[p] = [net.push(*move) for move in moves]
        self.stage += 1


def reduce_buffers(z, columns_kinds):
    made = {}
    for p, (columns, kind) in enumerate(columns_kinds):
        block = (z.shard, columns)
        made[f"r{p}a"] = pltpu.VMEM((z.hh, 2, 2, z.splits) + block, kind)
        if p % 2 == 0:
            made[f"r{p}b"] = pltpu.VMEM((z.hh - 1, 2, 2, z.splits) + block, kind)
            made[f"r{p}c"] = pltpu.VMEM((z.splits - 1, 2, 2) + block, kind)
        else:
            made[f"r{p}b"] = pltpu.VMEM((z.splits - 1, z.hh, 2, 2) + block, kind)
            made[f"r{p}c"] = pltpu.VMEM((z.hh - 1, 2, 2) + block, kind)
        made[f"r{p}d"] = pltpu.VMEM((2,) + block, kind)
        made[f"r{p}e"] = pltpu.VMEM(block, kind)
        made[f"r{p}f"] = pltpu.VMEM((z.hh, 2, 2, z.splits) + block, kind)
    return made


def buffers_of(held, pieces):
    return [[getattr(held, f"r{p}{k}") for k in "abcdef"] for p in range(pieces)]


def head_masks(first):
    where_lane = lanes((1, 256))
    return [
        ((where_lane >= first + HD * j) & (where_lane < first + HD * (j + 1))).astype(F32)
        for j in range(3)
    ]


def window(v, g, shifted):
    start = 384 * (g // 2) + 128 * (g % 2)
    cut = v[:, start : start + 256]
    if shifted:
        if g % 2 == 0:
            cut = pltpu.roll(cut, HD, 1)
        return jnp.where(lanes(cut.shape) >= HD, cut, 0.0)
    if g % 2 == 1:
        cut = pltpu.roll(cut, 256 - HD, 1)
    return jnp.where(lanes(cut.shape) < 192, cut, 0.0)


def pack(v):
    half = v.shape[0] // 2
    last = v[:half, 128:] + pltpu.roll(v[half:, 128:], HD, 1)
    return v[:, :128].astype(BF), last.astype(BF)


def put_packed(ref, v):
    upper, last = pack(v)
    rows = v.shape[0]
    ref[:rows], ref[rows:] = upper, last


def unpack(packed):
    rows = packed.shape[0] * 2 // 3
    last = packed[rows:].astype(F32)
    keep = lanes(last.shape) < HD
    lower = jnp.concatenate(
        [jnp.where(keep, last, 0.0), jnp.where(keep, pltpu.roll(last, HD, 1), 0.0)], axis=0
    )
    return jnp.concatenate([packed[:rows].astype(F32), lower], axis=1)


def unwindow(even, odd):
    odd = pltpu.roll(odd, HD, 1)
    return [even[:, :128], even[:, 128:] + odd[:, :128], odd[:, 128:]]


def joined(key, value):
    return [key[:, :128], key[:, 128:] + value[:, :128], value[:, 128:]]


def places(net, first, last):
    z = net.z
    row = lax.broadcasted_iota(jnp.int32, ((last - first) * 3 * z.rows, 1), 0)
    block = first + row // (3 * z.rows)
    return (block * z.splits + net.s) * z.rows + row % z.rows


def attend(net, a, x, at):
    z = net.z
    act(at.start)
    gain = rows_of(a.small[...])[0:1]
    root = lax.rsqrt(jnp.mean(x * x, axis=-1, keepdims=True) + EPSILON)
    low = (x * root * gain).astype(BF)
    a.low[...] = low
    k = rotate(mm(low, a.w_in[:, z.width : 2 * z.width]), a.cq[...], a.sq[...])
    v = mm(low, a.w_in[:, 2 * z.width :])
    for n in range(GROUPS):
        for j, part in enumerate(joined(window(k, n, False), window(v, n, True))):
            a.kv_out[n, :, 128 * j : 128 * (j + 1)] = part.astype(BF)
    far = {}
    for dg in (2, 1, 3):
        t = net.up(net.g, dg, GROUPS)
        far[dg] = net.push(a.kv_out.at[t], a.kv.at[net.b], net.near(dg=dg))
    a.kv[net.b] = a.kv_out[net.g]
    q = rotate(mm(low, a.w_in[:, : z.width]), a.cq[...], a.sq[...])
    for n in range(GROUPS):
        put_packed(a.q_out.at[n], window(q, n, False))
    moved = []
    for dg in (2, 1, 3):
        t = net.up(net.g, dg, GROUPS)
        moved.append(net.push(a.q_out.at[t], a.q.at[net.g], net.near(dg=dg)))
    a.q[net.g] = a.q_out[net.g]
    act(at.sent)
    for dg in (0, 1, 3, 2):
        if dg:
            far[dg].wait_recv()
        place = a.kv.at[net.down(net.g, dg, GROUPS) * z.splits + net.s]
        for ds in range(1, z.splits):
            moved.append(net.push(place, place, net.near(ds=ds)))
    for made in moved:
        made.wait_recv()
    act(at.mid)
    q_masks = [m.astype(BF) for m in head_masks(0)]
    v_masks = head_masks(HD)
    first = net.take(GROUPS)
    chunk = z.nb * z.rows if z.nb * z.rows <= 1024 else 512
    for i in range(GROUPS):
        own = unpack(a.q[i]).astype(BF)
        q3 = jnp.concatenate([own * m for m in q_masks], axis=0)
        row = places(net, i, i + 1)
        peak = total = out = None
        for start in range(0, (i + 1) * z.splits * z.rows, chunk):
            keys = min(chunk, (i + 1) * z.splits * z.rows - start)
            kv = a.kv[start // z.rows : (start + keys) // z.rows].reshape(keys, 384)
            mask = lanes((1, keys)) + start <= row
            scores = jnp.where(mask, mm(q3, kv[:, 0:256], 1, 1) * SCALE, NEGATIVE)
            top = jnp.max(scores, axis=-1, keepdims=True)
            top = top if peak is None else jnp.maximum(top, peak)
            weights = jnp.exp(scores - top)
            more = jnp.sum(weights, axis=-1, keepdims=True)
            product = mm(weights.astype(BF), kv[:, 128:384])
            if peak is None:
                total, out = more, product
            else:
                factor = jnp.exp(peak - top)
                total, out = total * factor + more, out * factor + product
            peak = top
        out = out / total
        merged = sum(out[z.rows * j : z.rows * (j + 1)] * v_masks[j] for j in range(3))
        a.o[i] = merged
        put_packed(a.o_out.at[i], pltpu.roll(merged, 256 - HD, 1))
        a.lse[i] = peak + jnp.log(total)
        device = net.device(net.y, net.c, i, net.s)
        net.push_or_keep(
            a.o_out.at[i], a.ret.at[net.g], device, net.g == i, first + i, first + net.g
        )
    act(at.out)
    middle = x
    for n in range(GROUPS):
        net.arrived(a.ret.at[n], first + n)
        got = unpack(a.ret[n]).astype(BF)
        middle = middle + mm(got[:, 0:192], a.w_out[192 * n : 192 * (n + 1), :])
    a.middle[...] = middle
    return middle


def attend_back(net, a, x, dm, at):
    z = net.z
    branch = dm.astype(BF)
    grad_att = mm(branch, a.w_out[...], 1, 1)
    for n in range(GROUPS):
        put_packed(a.do_out.at[n], window(grad_att, n, False))
    moved = []
    for dg in (2, 1, 3):
        t = net.up(net.g, dg, GROUPS)
        moved.append(net.push(a.do_out.at[t], a.do.at[net.g], net.near(dg=dg)))
    a.do[net.g] = a.do_out[net.g]
    act(at.back_sent)
    per = 192 // z.shard
    for n in range(GROUPS):
        part = mm(unpack(a.ret[n]).astype(BF), branch, 0, 0)[0:192]
        for k in range(per):
            a.gout[n * per + k] = part[k * z.shard : (k + 1) * z.shard].astype(BF)
    q_masks = head_masks(0)
    v_masks = head_masks(HD)
    for i in range(GROUPS):
        own = unpack(a.q[i]).astype(BF)
        for j in range(3):
            a.q3[i, z.rows * j : z.rows * (j + 1)] = own * q_masks[j].astype(BF)
    a.dq_sum[...] = jnp.zeros(a.dq_sum.shape, F32)
    for made in moved:
        made.wait_recv()
    for i in range(GROUPS):
        own = pltpu.roll(unpack(a.do[i]), HD, 1)
        product = own * a.o[i]
        for j in range(3):
            span = slice(z.rows * j, z.rows * (j + 1))
            a.do3[i, span] = (own * v_masks[j]).astype(BF)
            a.delta[i, span] = jnp.sum(product * v_masks[j], axis=-1, keepdims=True)
    first_q, first_kv = net.take(GROUPS), net.take(GROUPS)
    between = {}
    size = 3 * z.rows

    def onward(i):
        total = a.dkv_out[i * z.splits + net.s].astype(F32)
        for ds, made in between[i]:
            made.wait_recv()
            total = total + a.dkv_got[ds - 1, i].astype(F32)
        a.dkv_sum[i] = total.astype(BF)
        device = net.device(net.y, net.c, i, net.s)
        net.push_or_keep(
            a.dkv_sum.at[i], a.dkv.at[net.g], device, net.g == i, first_kv + i, first_kv + net.g
        )

    some = min(4, z.splits)
    keys = some * z.rows
    for n in range(GROUPS):
        spans = [(n, GROUPS)] if keys <= 256 else [(i, i + 1) for i in range(n, GROUPS)]
        for block in range(n * z.splits, (n + 1) * z.splits, some):
            kv = a.kv[block : block + some].reshape(keys, 384)
            key, value = kv[:, 0:256], kv[:, 128:384]
            dk = jnp.zeros((keys, 256), F32)
            dv = jnp.zeros((keys, 256), F32)
            for lo, hi in spans:
                rows = (hi - lo) * size
                q3 = a.q3[lo:hi].reshape(rows, 256)
                do3 = a.do3[lo:hi].reshape(rows, 256)
                lse = a.lse[lo:hi].reshape(rows, 1)
                delta = a.delta[lo:hi].reshape(rows, 1)
                mask = lanes((1, keys)) + block * z.rows <= places(net, lo, hi)
                scores = mm(q3, key, 1, 1) * SCALE
                weights = jnp.where(mask, jnp.exp(scores - lse), 0.0)
                grad_scores = (weights * (mm(do3, value, 1, 1) - delta)).astype(BF)
                more = mm(grad_scores, key).reshape((hi - lo) * 3, z.rows, 256)
                for i in range(lo, hi):
                    at_i = 3 * (i - lo)
                    a.dq_sum[i] += sum(more[at_i + j] * q_masks[j] for j in range(3))
                dk = dk + mm(grad_scores, q3, 0, 0)
                dv = dv + mm(weights.astype(BF), do3, 0, 0)
            for j, part in enumerate(joined(dk * SCALE, dv)):
                a.dkv_out[block : block + some, :, 128 * j : 128 * (j + 1)] = part.astype(
                    BF
                ).reshape(some, z.rows, 128)
        between[n] = []
        for ds in range(1, z.splits):
            t = net.up(net.s, ds, z.splits)
            made = net.push(a.dkv_out.at[n * z.splits + t], a.dkv_got.at[ds - 1, n], net.near(ds=ds))
            between[n].append((ds, made))
        put_packed(a.dq_out.at[n], a.dq_sum[n] * SCALE)
        device = net.device(net.y, net.c, n, net.s)
        net.push_or_keep(
            a.dq_out.at[n], a.dq.at[net.g], device, net.g == n, first_q + n, first_q + net.g
        )
        if n:
            onward(n - 1)
        act(at.back.get(n, ()))
    onward(GROUPS - 1)
    act(at.back_out)
    own = a.low[...]
    grad_low = jnp.zeros((z.rows, z.width), F32)
    from_zero = lanes((1, 256)) < 192

    leaving = []

    def weigh(piece, start):
        slot = len(leaving) % 2
        if len(leaving) >= 2:
            leaving[-2].wait()
        part = mm(own, piece, 0, 0)
        for k in range(z.shards):
            a.gin_part[slot, k] = part[k * z.shard : (k + 1) * z.shard].astype(BF)
        place = a.gin.at[:, :, start : start + 384]
        leaving.append(pltpu.make_async_copy(a.gin_part.at[slot], place, a.gin_sem.at[slot]))
        leaving[-1].start()
        return mm(piece, a.w_in[:, start : start + 384], 1, 1)

    def turned(columns, n):
        cut = slice(192 * n, 192 * n + 384)
        return rotate_back(jnp.concatenate(columns, axis=1), a.cq[:, cut], a.sq[:, cut]).astype(BF)

    for n in range(0, GROUPS, 2):
        net.arrived(a.dq.at[n], first_q + n)
        net.arrived(a.dq.at[n + 1], first_q + n + 1)
        columns = unwindow(unpack(a.dq[n]), unpack(a.dq[n + 1]))
        grad_low = grad_low + weigh(turned(columns, n), 192 * n)
    for n in range(0, GROUPS, 2):
        pair = []
        for m in (n, n + 1):
            net.arrived(a.dkv.at[m], first_kv + m)
            both = a.dkv[m].astype(F32)
            key = jnp.where(from_zero, both[:, :256], 0.0)
            value = jnp.where(from_zero, pltpu.roll(both[:, 128:], 256 - HD, 1), 0.0)
            pair.append((key, value))
        columns = unwindow(pair[0][0], pair[1][0])
        grad_low = grad_low + weigh(turned(columns, n), z.width + 192 * n)
        columns = unwindow(pair[0][1], pair[1][1])
        piece = jnp.concatenate(columns, axis=1).astype(BF)
        grad_low = grad_low + weigh(piece, 2 * z.width + 192 * n)
    for copy in leaving[-2:]:
        copy.wait()
    gain = rows_of(a.small[...])[0:1]
    root = lax.rsqrt(jnp.mean(x * x, axis=-1, keepdims=True) + EPSILON)
    place = (lanes((z.rows, 128)) == 16).astype(F32).astype(BF)
    high, rest = split(grad_low * x * root)
    a.gsmall[...] += mm(high, place, 0, 0) + mm(rest, place, 0, 0)
    return dm + norm_grad(x, root, gain, grad_low)


class Mixing:
    def __init__(self, z, middle, small, plan):
        table = rows_of(small)
        self.gain, self.consts = table[1:2], (table[2:3], table[3:4])
        self.root = lax.rsqrt(jnp.mean(middle * middle, axis=-1, keepdims=True) + EPSILON)
        self.normed = middle * self.root * self.gain
        self.low, self.rest = split(self.normed)
        expert_of, slot_of = lanes((z.rows, 128)).astype(F32), lanes((z.rows, z.count)).astype(F32)
        self.picks = [(expert_of == plan[:, j : j + 1]).astype(F32) for j in range(TOP)]
        self.chosen = [(slot_of == plan[:, TOP + j : TOP + j + 1]).astype(F32) for j in range(TOP)]
        self.select = (self.chosen[0] + self.chosen[1]).astype(BF)
        self.small = small

    def share(self):
        self.product = mm(self.low, self.small)
        shares = self.product + mm(self.rest, self.small)
        self.shares = []
        for index in range(2):
            one, two = lane_of(shares, 12 + 2 * index), lane_of(shares, 13 + 2 * index)
            peak = jnp.maximum(one, two)
            one, two = jnp.exp(one - peak), jnp.exp(two - peak)
            self.shares.append((one / (one + two), two / (one + two)))

    def gate(self, logits):
        values = [jnp.sum(p * logits, axis=-1, keepdims=True) for p in self.picks]
        peak = jnp.maximum(values[0], values[1])
        powers = [jnp.exp(v - peak) for v in values]
        total = powers[0] + powers[1]
        self.gates = [p / total for p in powers]
        self.combine = self.gates[0] * self.chosen[0] + self.gates[1] * self.chosen[1]

    def weigh(self):
        spread = self.gates[0] * self.picks[0] + self.gates[1] * self.picks[1]
        self.const_weights = [lane_of(spread, NF + 2 + index) for index in range(2)]
        self.normed_weight = lane_of(spread, NF + 1)
        for index in range(2):
            self.normed_weight = (
                self.normed_weight + self.const_weights[index] * self.shares[index][0]
            )


class ExpertRun:
    def __init__(self, net, e, rows_ref, all_ref, chunk):
        self.net, self.e, self.rows_ref, self.all_ref, self.chunk = net, e, rows_ref, all_ref, chunk
        self.mine = net.y * GROUPS + net.g

    def send(self):
        net, z = self.net, self.net.z
        steps = [(dy, dg) for dg in (2, 1, 3, 0) for dy in range(z.hh) if dy or dg]
        first = []
        for dy, dg in steps:
            target = net.up(net.y, dy, z.hh) * GROUPS + net.up(net.g, dg, GROUPS)
            place = self.all_ref.at[net.q, self.mine]
            first.append(net.push(self.rows_ref.at[target], place, net.near(dy=dy, dg=dg)))
        self.all_ref[net.q, self.mine] = self.rows_ref[self.mine]
        self.sources = [(0, 0, None)] + [
            (dy, dg, made) for (dy, dg), made in zip(reversed(steps), reversed(first))
        ]

    def relay(self, while_first):
        net, z = self.net, self.net.z
        self.slots = []
        self.aside, self.across = [[] for _ in range(z.splits)], [[] for _ in range(z.splits)]
        for k, (dy, dg, made) in enumerate(self.sources):
            if made is not None:
                made.wait_recv()
            self.slots.append(net.down(net.y, dy, z.hh) * GROUPS + net.down(net.g, dg, GROUPS))
            place = self.all_ref.at[net.q, self.slots[k]]
            for ds in range(1, z.splits):
                self.aside[ds].append(net.push(place, place, net.near(ds=ds)))
            self.across[0].append(net.push(place, place, net.near(dc=1)))
            if k == 0:
                while_first()

    def compute(self):
        net, z, e = self.net, self.net.z, self.e
        block = (z.experts, SLOT, z.width)
        e.base[...] = self.chunk(net.q).reshape(block)
        other = 1 - net.c
        for ds in range(1, z.splits):
            s = net.down(net.s, ds, z.splits)
            for k, made in enumerate(self.aside[ds]):
                made.wait_recv()
                place = self.all_ref.at[net.c * z.splits + s, self.slots[k]]
                self.across[ds].append(net.push(place, place, net.near(dc=1)))
        self.halves = {}
        for ds in range(z.splits):
            s = net.down(net.s, ds, z.splits)
            for made in self.across[ds]:
                made.wait_recv()
            e.part[ds] = self.chunk(other * z.splits + s).astype(BF).reshape(block)
            to_core = net.push(e.part.at[ds], e.got.at[ds], net.near(dc=1))
            if ds == 0:
                self.first_core = to_core
                continue
            kept = self.chunk(net.c * z.splits + s)
            to_core.wait_recv()
            net.sent = [made for made in net.sent if made is not to_core]
            to_core.wait_send()
            e.part[ds] = (kept.reshape(block) + e.got[ds].astype(F32)).astype(BF)
            for dy in reversed(range(z.hh)):
                span = pl.ds(net.up(net.y, dy, z.hh) * GROUPS, GROUPS)
                device = net.near(ds=z.splits - ds)
                made = net.push(e.part.at[ds, span], e.side_got.at[ds - 1, span], device)
                self.halves[ds, dy] = made

    def give_back(self):
        net, z, e = self.net, self.net.z, self.e
        self.first_core.wait_recv()
        e.base[...] += e.got[0].astype(F32)
        self.last = []
        for dy in reversed(range(z.hh)):
            y = net.up(net.y, dy, z.hh)
            span = pl.ds(y * GROUPS, GROUPS)
            total = e.base[span]
            for ds in range(1, z.splits):
                self.halves[ds, dy].wait_recv()
                total = total + e.side_got[ds - 1, span].astype(F32)
            e.sum[span] = total.astype(BF)
            for dg in (2, 1, 3, 0):
                if dy or dg:
                    src = e.sum.at[y * GROUPS + net.up(net.g, dg, GROUPS)]
                    made = net.push(src, e.back.at[self.mine], net.near(dy=dy, dg=dg))
                    self.last.append(made)
        e.back[self.mine] = e.sum[self.mine]

    def wait(self):
        for made in self.last:
            made.wait_recv()


def weight_of(z, e, w):
    e.wait_weight(w)
    ref = e.weights[w]
    if z.drow % 16 == 0:
        return ref[...].reshape(z.width, z.ffp)
    return jnp.concatenate([ref[n].astype(F32) for n in range(z.nb)], axis=0).astype(BF)


def held_weights(net, e):
    held = {}

    def weight(w):
        if w not in held:
            held[w] = weight_of(net.z, e, w)
        return held[w]

    return weight


def forward_chunk(net, e, weight):
    z = net.z

    def chunk(part):
        rows = e.all[part].reshape(z.count, z.width)
        gate, up = mm(rows, weight(0)), mm(rows, weight(1))
        e.gate[part], e.up[part] = gate.astype(BF), up.astype(BF)
        hidden = (gate / (1.0 + jnp.exp(-gate)) * up).astype(BF)
        return mm(hidden, weight(2), 1, 1)

    return chunk


def backward_chunk(net, e, weight):
    z = net.z

    def chunk(part):
        weight(0), weight(1)
        rows = e.dall[part].reshape(z.count, z.width)
        grad_hidden = mm(rows, weight(2))
        gate, up = e.gate[part].astype(F32), e.up[part].astype(F32)
        sig = 1.0 / (1.0 + jnp.exp(-gate))
        silu = gate * sig
        e.hid[part] = (silu * up).astype(BF)
        up_low = (grad_hidden * silu).astype(BF)
        gate_low = (grad_hidden * up * (sig * (1.0 + gate * (1.0 - sig)))).astype(BF)
        e.du[part], e.dg[part] = up_low, gate_low
        return mm(gate_low, weight(0), 1, 1) + mm(up_low, weight(1), 1, 1)

    return chunk


def weight_grads(net, e):
    z = net.z
    step = min(4, z.nq)
    for w, one, two in ((0, e.all, e.dg), (1, e.all, e.du), (2, e.dall, e.hid)):
        product = None
        for first in range(0, z.nq, step):
            span = slice(first, first + step)
            left = one[span].reshape(step * z.count, z.width)
            more = mm(left, two[span].reshape(step * z.count, z.ffp), 0, 0)
            product = more if product is None else product + more
        for n in range(z.nb):
            e.gw[w][n] = product[n * z.drow : (n + 1) * z.drow].astype(BF)


def put_rows(mixing, e):
    e.rows[...] = mm(mixing.select, mixing.low, 0, 0).astype(BF).reshape(e.rows.shape)


def put_grad_rows(mixing, e, high, rest):
    weight_high, weight_rest = split(mixing.combine)
    slot_grad = mm(weight_high, high, 0, 0) + mm(weight_rest, high, 0, 0)
    slot_grad = slot_grad + mm(weight_high, rest, 0, 0)
    e.rows[...] = slot_grad.astype(BF).reshape(e.rows.shape)


def mixture(z, mixing, middle, results):
    high, rest = split(mixing.combine)
    mixed = mm(high, results) + mm(rest, results) + mixing.normed_weight * mixing.normed
    for index in range(2):
        weight = mixing.const_weights[index] * mixing.shares[index][1]
        mixed = mixed + weight * mixing.consts[index]
    return middle + mixed


def mixture_grads(z, mixing, grad, grad_logits, high, rest, results):
    where_lane = lanes((z.rows, 128))
    along = mm(high, results, 1, 1) + mm(rest, results, 1, 1)
    normed_dot = jnp.sum(grad * mixing.normed, axis=-1, keepdims=True)
    const_dots = [jnp.sum(grad * c, axis=-1, keepdims=True) for c in mixing.consts]
    gate_grads = []
    for j in range(TOP):
        value = jnp.sum(mixing.chosen[j] * along, axis=-1, keepdims=True)
        value = value + lane_of(mixing.picks[j], NF + 1) * normed_dot
        for index in range(2):
            share = mixing.shares[index]
            value = value + lane_of(mixing.picks[j], NF + 2 + index) * (
                share[0] * normed_dot + share[1] * const_dots[index]
            )
        gate_grads.append(value)
    inner = mixing.gates[0] * gate_grads[0] + mixing.gates[1] * gate_grads[1]
    logit_grad = grad_logits
    for j in range(TOP):
        logit_grad = logit_grad + mixing.picks[j] * (mixing.gates[j] * (gate_grads[j] - inner))
    column = jnp.zeros((z.rows, 128), F32)
    const_columns = jnp.zeros((z.rows, 128), F32)
    for index in range(2):
        share, weight = mixing.shares[index], mixing.const_weights[index]
        one, two = weight * normed_dot, weight * const_dots[index]
        mean = share[0] * one + share[1] * two
        column = column + jnp.where(where_lane == 12 + 2 * index, share[0] * (one - mean), 0.0)
        column = column + jnp.where(where_lane == 13 + 2 * index, share[1] * (two - mean), 0.0)
        const_columns = const_columns + jnp.where(where_lane == 18 + index, weight * share[1], 0.0)
    both_high, both_rest = split(logit_grad + column)
    grad_normed = mm(both_high, mixing.small, 1, 1) + mm(both_rest, mixing.small, 1, 1)
    grad_normed = grad_normed + mixing.normed_weight * grad
    gsmall = mm(mixing.low, both_high, 0, 0) + mm(mixing.low, both_rest, 0, 0)
    gsmall = gsmall + mm(mixing.rest, column.astype(BF), 0, 0)
    const_high, const_rest = split(const_columns)
    gsmall = gsmall + mm(high, const_high, 0, 0) + mm(rest, const_high, 0, 0)
    return logit_grad, grad_normed, gsmall + mm(high, const_rest, 0, 0)


def middle_grads(z, mixing, e, middle, grad, grad_normed, gsmall):
    grad_normed = grad_normed + mm(mixing.select, e.back[...].reshape(z.count, z.width))
    place = (lanes((z.rows, 128)) == 17).astype(F32).astype(BF)
    high, rest = split(grad_normed * middle * mixing.root)
    e.gsmall[...] = gsmall + mm(high, place, 0, 0) + mm(rest, place, 0, 0)
    return grad + norm_grad(middle, mixing.root, mixing.gain, grad_normed)


def experts(net, e, middle, logits_in, at):
    z = net.z
    mixing = Mixing(z, middle, e.small[...], e.plan[...])
    put_rows(mixing, e)
    run = ExpertRun(net, e, e.rows, e.all, forward_chunk(net, e, held_weights(net, e)))

    def while_first():
        mixing.share()
        logits = mixing.product + logits_in
        e.logits[...] = logits
        mixing.gate(logits)
        mixing.weigh()
        act(at.rows)

    run.send()
    run.relay(while_first)
    run.compute()
    act(at.side)
    run.give_back()
    act(at.last)
    run.wait()
    e.results[...] = e.back[...]
    return mixture(z, mixing, middle, e.back[...].reshape(z.count, z.width))


def experts_back(net, e, middle, grad, grad_logits, at):
    z = net.z
    mixing = Mixing(z, middle, e.small[...], e.plan[...])
    mixing.gate(e.logits[...])
    high, rest = split(grad)
    put_grad_rows(mixing, e, high, rest)
    run = ExpertRun(net, e, e.rows, e.dall, backward_chunk(net, e, held_weights(net, e)))
    made = []

    def while_first():
        mixing.share()
        mixing.weigh()
        results = e.results[...].reshape(z.count, z.width)
        made.extend(mixture_grads(z, mixing, grad, grad_logits, high, rest, results))
        act(at.rows_back)

    run.send()
    run.relay(while_first)
    run.compute()
    weight_grads(net, e)
    act(at.side_back)
    run.give_back()
    act(at.last_back)
    run.wait()
    logit_grad, grad_normed, gsmall = made
    return middle_grads(z, mixing, e, middle, grad, grad_normed, gsmall), logit_grad


def experts_both(net, e, later, middle, logits_in, grad, grad_logits, at):
    z = net.z
    mixing = Mixing(z, middle, e.small[...], e.plan[...])
    put_rows(mixing, e)
    weight = held_weights(net, e)
    run = ExpertRun(net, e, e.rows, e.all, forward_chunk(net, e, weight))
    back = ExpertRun(net, later, later.rows, e.dall, backward_chunk(net, e, weight))
    run.send()
    act(at.rows)
    mixing.share()
    mixing.gate(mixing.product + logits_in)
    high, rest = split(grad)
    put_grad_rows(mixing, later, high, rest)
    back.send()
    mixing.weigh()
    run.relay(lambda: None)
    run.compute()
    back.relay(lambda: None)
    back.compute()
    run.give_back()
    weight_grads(net, e)
    act(at.side_back)
    back.give_back()
    act(at.last_back)
    run.wait()
    results = e.back[...].reshape(z.count, z.width)
    result = mixture(z, mixing, middle, results)
    made = mixture_grads(z, mixing, grad, grad_logits, high, rest, results)
    back.wait()
    logit_grad, grad_normed, gsmall = made
    return result, middle_grads(z, mixing, later, middle, grad, grad_normed, gsmall), logit_grad


def attend_kept(z):
    return dict(
        middle=struct((z.rows, z.width), F32),
        low=struct((z.rows, z.width), BF),
        q=struct((GROUPS, 3 * z.rows // 2, 128), BF),
        kv=struct((z.nb, z.rows, 384), BF),
        o=struct((GROUPS, z.rows, 256), F32),
        lse=struct((GROUPS, 3 * z.rows, 1), F32),
        ret=struct((GROUPS, 3 * z.rows // 2, 128), BF),
    )


def experts_kept(z):
    block = (z.experts, SLOT, z.width)
    return dict(
        logits=struct((z.rows, 128), F32),
        results=struct(block, BF),
        all=struct((z.nq,) + block, BF),
        gate=struct((z.nq, z.count, z.ffp), BF),
        up=struct((z.nq, z.count, z.ffp), BF),
    )


def attend_scratch(z):
    return dict(
        q_out=pltpu.VMEM((GROUPS, 3 * z.rows // 2, 128), BF),
        kv_out=pltpu.VMEM((GROUPS, z.rows, 384), BF),
        o_out=pltpu.VMEM((GROUPS, 3 * z.rows // 2, 128), BF),
    )


def attend_back_scratch(z, own_output=True):
    one = pltpu.VMEM((GROUPS, 3 * z.rows // 2, 128), BF)
    three = pltpu.VMEM((GROUPS, 3 * z.rows, 256), BF)
    two = pltpu.VMEM((GROUPS, z.rows, 384), BF)
    made = dict(
        do_out=one,
        do=one,
        dq_out=one,
        dq=one,
        dkv_out=pltpu.VMEM((z.nb, z.rows, 384), BF),
        dkv_got=pltpu.VMEM((z.splits - 1, GROUPS, z.rows, 384), BF),
        dkv_sum=two,
        dkv=two,
        q3=three,
        do3=three,
        dq_sum=pltpu.VMEM((GROUPS, z.rows, 256), F32),
        gin_part=pltpu.VMEM((2, z.shards, z.shard, 384), BF),
        gin_sem=pltpu.SemaphoreType.DMA((2,)),
        delta=pltpu.VMEM((GROUPS, 3 * z.rows, 1), F32),
    )
    if not own_output:
        del made["dkv_out"]
    return made


def experts_scratch(z):
    block = (z.experts, SLOT, z.width)
    flat = pltpu.VMEM((z.splits,) + block, BF)
    return dict(
        rows=pltpu.VMEM(block, BF),
        part=flat,
        got=flat,
        side_got=pltpu.VMEM((z.splits - 1,) + block, BF),
        base=pltpu.VMEM(block, F32),
        sum=pltpu.VMEM(block, BF),
        back=pltpu.VMEM(block, BF),
    )


def experts_back_scratch(z, both=True):
    part = pltpu.VMEM((z.nq, z.count, z.ffp), BF)
    block = (z.experts, SLOT, z.width)
    made = dict(dall=pltpu.VMEM((z.nq,) + block, BF), hid=part)
    if both:
        made.update(dict(dg=part, du=part))
    return made


def scratch_of(kept):
    return {name: pltpu.VMEM(v.shape, v.dtype) for name, v in kept.items()}


def view(held, **more):
    return Names(**{**held.__dict__, **more})


def landing(z):
    return struct((z.nb, z.drow, z.ffp), BF)


def near_landing(z):
    return struct((GROUPS, z.drow, z.ffp), BF)


def grad_landing(z):
    return struct((2, z.drow, z.hidden), BF)


def nothing():
    pass


CUT = 384


def in_vmem(arrays):
    return {name: (array, VMEM) for name, array in arrays.items()}


def in_place(arrays):
    return {name: (array, ANY) for name, array in arrays.items()}


def weight_pieces(z, owns, wholes):
    widths = (3 * z.width, z.width)
    return [
        (owns[which], wholes[which], first, columns)
        for which, first, columns in cuts_of((0, 1), widths, CUT)
    ]


def pieces_sems(z, pieces):
    return pieces * (2 + z.splits + z.hh)


def eye(size):
    shape = (size, size)
    return lax.broadcasted_iota(jnp.int32, shape, 0) == lax.broadcasted_iota(jnp.int32, shape, 1)


def upright(row, same):
    return jnp.sum(jnp.where(same, row, 0.0), axis=1, keepdims=True)


def plan_of(z, routes, order):
    same, lane = eye(z.rows), lanes((z.rows, 128))
    ids, ranks = routes.astype(F32), order.astype(F32)
    plan = jnp.zeros((z.rows, 128), F32)
    for j in range(TOP):
        own, rank = upright(ids[j : j + 1], same), upright(ranks[j : j + 1], same)
        before = jnp.zeros((z.rows, 1), F32)
        for k in range(TOP):
            counts = (own == ids[k : k + 1]) & (ranks[k : k + 1] < rank)
            before = before + jnp.sum(counts.astype(F32), axis=1, keepdims=True)
        slot = jnp.where((own < NF) & (before < CAP), own * SLOT + before, -1.0)
        plan = plan + jnp.where(lane == j, own, 0.0) + jnp.where(lane == TOP + j, slot, 0.0)
    return plan


def grid_of(z):
    return (z.hh, 2, 2, 2, z.splits, z.shard)


def gather_first(z, large, little):
    def body(k, net):
        owns, wholes = (k.attn_in.at[0], k.attn_out.at[0]), (k.w_in, k.w_out)
        pieces = weight_pieces(z, owns, wholes)
        gather = Gather(net, pieces, k.own)
        gather.step()
        moves = [
            NearWeights(net, k.expert_0, 0, k.near_0),
            NearWeights(net, k.expert_1, 0, k.near_1),
            NearWeights(net, k.expert_2, 0, k.near_2),
        ]
        same, lane = eye(z.shard), lanes((z.shard, 128))
        for layer in range(LAYERS):
            rows = [k.router[n][layer : layer + 1] for n in range(NE)]
            rows += [k.mix[layer][n : n + 1] for n in range(4)]
            rows += [k.gains[layer][n : n + 1] for n in range(2)]
            rows += [k.consts[layer][n : n + 1] for n in range(2)]
            table = jnp.zeros((z.shard, 128), F32)
            for n, row in enumerate(rows):
                table = table + jnp.where(lane == n, upright(row.astype(F32), same), 0.0)
            k.small_own[layer] = table.astype(BF)
        smalls = [
            (k.small_own.at[layer], whole, 0, 128)
            for layer, whole in enumerate((k.small_0, k.small_1))
        ]
        other = Gather(net, smalls, k.own_too)
        other.step()
        gather.step()
        moves[0].start()
        for layer, plan in enumerate((k.plan_0, k.plan_1)):
            plan[...] = plan_of(z, k.routes[layer], k.order[layer])
        same, lane = eye(z.rows), lanes((z.rows, 128))
        table = jnp.zeros((z.rows, 128), F32)
        for n in range(NE):
            table = table + jnp.where(lane == n, upright(k.prev[n : n + 1], same), 0.0)
        k.logits[...] = table
        gather.step()
        other.step()
        moves[1].start()
        moves[2].start()
        row = lax.broadcasted_iota(jnp.int32, (z.rows, 1), 0) + net.b * z.rows
        angles = row.astype(F32) * k.freqs[...]
        cosine, sine = jnp.cos(angles), jnp.sin(angles)
        sine = jnp.where(lane % HD < HD // 2, -sine, sine)
        for n in range(z.width // 128):
            k.cq[:, 128 * n : 128 * (n + 1)] = cosine
            k.sq[:, 128 * n : 128 * (n + 1)] = sine
        for _ in range(3):
            gather.step()
            other.step()
        other.step()
        for move in moves:
            move.wait()

    ins = {**in_place(large), **in_vmem(little)}
    outs = in_place(
        dict(
            w_in=struct(grid_of(z) + (3 * z.width,), BF),
            w_out=struct(grid_of(z) + (z.width,), BF),
            small_0=struct(grid_of(z) + (128,), BF),
            small_1=struct(grid_of(z) + (128,), BF),
            near_0=near_landing(z),
            near_1=near_landing(z),
            near_2=near_landing(z),
        )
    )
    table, wide = struct((z.rows, 128), F32), struct((z.rows, z.width), F32)
    outs.update(in_vmem(dict(plan_0=table, plan_1=table, logits=table, cq=wide, sq=wide)))
    pieces = len(weight_pieces(z, (0, 0), (0, 0)))
    scratch = dict(
        small_own=pltpu.VMEM((LAYERS, z.shard, 128), BF),
        own=pltpu.SemaphoreType.DMA((pieces,)),
        own_too=pltpu.SemaphoreType.DMA((LAYERS,)),
    )
    return launch(body, 0, z, ins, outs, scratch, pieces_sems(z, pieces + LAYERS) + 3 * GROUPS)


def layer_sems(z):
    attention = 6 + GROUPS * (z.splits - 1) + GROUPS
    expert = (z.experts - 1) * 2 + z.experts * (2 * z.splits - 1) + z.splits + z.hh * z.splits
    back = 3 + GROUPS * (z.splits - 1) + 2 * GROUPS
    return attention, expert, back


def waiting(*moves):
    held = list(moves)

    def wait(w):
        if held[w] is not None:
            held[w].wait()
            held[w] = None

    return wait


def layer_forward(z, values, tables, weights, near, shards, parts):
    def body(k, net):
        owns, wholes = (k.attn_in.at[1], k.attn_out.at[1]), (k.next_in, k.next_out)
        gather = Gather(net, weight_pieces(z, owns, wholes), k.own)
        far = [
            FarWeights(net, k.expert_0, 0, k.near_0, k.weight_0),
            FarWeights(net, k.expert_1, 0, k.near_1, k.weight_1),
            FarWeights(net, k.expert_2, 0, k.near_2, k.weight_2),
        ]
        ahead = [
            NearWeights(net, k.expert_0, 1, k.next_0),
            NearWeights(net, k.expert_1, 1, k.next_1),
            NearWeights(net, k.expert_2, 1, k.next_2),
        ]
        at = Beside(
            start=[gather.step, far[0].start],
            sent=[gather.step, far[1].start],
            out=[gather.step],
            rows=[far[2].start, gather.step, ahead[0].start],
            side=[gather.step, ahead[1].start],
            last=[gather.step, ahead[2].start],
        )
        middle = attend(net, k, k.tokens[...].astype(F32), at)
        e = view(k, weights=(k.weight_0, k.weight_1, k.weight_2), wait_weight=waiting(*far))
        k.state[...] = experts(net, e, middle, k.logits_in[...], at)
        for move in ahead:
            move.wait()

    ins = {**in_vmem(values), **in_vmem(tables), **in_vmem(weights)}
    ins.update({**in_place(shards), **in_place(parts), **in_place(near)})
    whole = landing(z)
    outs = dict(state=struct((z.rows, z.width), F32))
    outs.update(dict(weight_0=whole, weight_1=whole, weight_2=whole))
    outs = in_vmem({**outs, **attend_kept(z), **experts_kept(z)})
    ahead = dict(
        next_in=struct(grid_of(z) + (3 * z.width,), BF),
        next_out=struct(grid_of(z) + (z.width,), BF),
        next_0=near_landing(z),
        next_1=near_landing(z),
        next_2=near_landing(z),
    )
    outs.update(in_place(ahead))
    pieces = len(weight_pieces(z, (0, 0), (0, 0)))
    own = dict(own=pltpu.SemaphoreType.DMA((pieces,)))
    scratch = {**attend_scratch(z), **experts_scratch(z), **own}
    attention, expert, _ = layer_sems(z)
    count = attention + expert + pieces_sems(z, pieces) + 3 * z.nb + 3 * GROUPS
    return launch(body, 1, z, ins, outs, scratch, count)


def back_outputs(z, more):
    outs = dict(
        grad=struct((z.rows, z.width), F32),
        grad_logits=struct((z.rows, 128), F32),
        gout=struct((z.shards, z.shard, z.width), BF),
        gsmall=struct((z.width, 128), F32),
        gw_2=landing(z),
    )
    rest = dict(
        gin=struct((z.shards, z.shard, 3 * z.width), BF),
        grad_0=grad_landing(z),
        grad_1=grad_landing(z),
    )
    return {**in_vmem({**outs, **more}), **in_place(rest)}


def layer_both(z, values, tables, weights, near, parts):
    together = z.nb <= 8

    def body(k, net):
        far = [
            FarWeights(net, k.expert_0, 1, k.near_0, k.weight_0),
            FarWeights(net, k.expert_1, 1, k.near_1, k.weight_1),
            FarWeights(net, k.expert_2, 1, k.near_2, k.weight_2),
        ]
        grads = [GradMove(net, k.gw_0, k.grad_0), GradMove(net, k.gw_1, k.grad_1)]
        at = Beside(
            start=[far[0].start],
            sent=[far[1].start],
            rows=[far[2].start],
            side_back=[grads[0].near],
            last_back=[grads[0].far],
            back_sent=[grads[1].near],
            back_out=[grads[1].far],
        )
        middle = attend(net, k, k.state[...], at)
        e = view(
            k,
            weights=(k.weight_0, k.weight_1, k.weight_2),
            gw=(k.gw_0, k.gw_1, k.gw_2),
            wait_weight=waiting(*far),
            dg=k.gate,
            du=k.up,
        )
        none = jnp.zeros((z.rows, 128), F32)
        grad = k.cotangent[...].astype(F32)
        if together:
            later = view(
                e,
                rows=k.rows_2,
                part=k.part_2,
                got=k.got_2,
                side_got=k.side_got_2,
                base=k.base_2,
                sum=k.sum_2,
                back=k.back_2,
            )
            result, dm, grad_logits = experts_both(
                net, e, later, middle, k.logits_in[...], grad, none, at
            )
        else:
            result = experts(net, e, middle, k.logits_in[...], at)
            net.settle()
            dm, grad_logits = experts_back(net, e, k.middle[...], grad, none, at)
        k.output[...] = result.astype(BF)
        k.grad_logits[...] = grad_logits
        net.settle()
        k.grad[...] = attend_back(net, view(k, dkv_out=k.kv), k.state[...], dm, at)
        for move in grads:
            move.wait()

    ins = {**in_vmem(values), **in_vmem(tables), **in_vmem(weights)}
    ins.update({**in_place(parts), **in_place(near)})
    outs = back_outputs(z, dict(output=struct((z.rows, z.width), BF)))
    scratch = {
        **scratch_of(attend_kept(z)),
        **scratch_of(experts_kept(z)),
        **attend_scratch(z),
        **attend_back_scratch(z, False),
        **experts_scratch(z),
        **experts_back_scratch(z, False),
    }
    if together:
        scratch.update({name + "_2": memory for name, memory in experts_scratch(z).items()})
    place = pltpu.VMEM(landing(z).shape, BF)
    scratch.update(dict(weight_0=place, weight_1=place, weight_2=place, gw_0=place, gw_1=place))
    attention, expert, back = layer_sems(z)
    count = attention + 2 * expert + back + 5 * z.nb
    return launch(body, 2, z, ins, outs, scratch, count)


def sum_pieces(z, k):
    wholes, sums = (k.up_in, k.up_out), (k.sum_in, k.sum_out)
    return weight_pieces(z, wholes, sums) + [(k.up_small, k.sum_small, 0, 128)]


def sum_parts(z, made):
    def grid(v):
        return v.reshape(grid_of(z) + (v.shape[-1],))

    ins = dict(up_in=grid(made.gin), up_out=grid(made.gout), up_small=grid(made.gsmall))
    outs = dict(
        sum_in=struct((z.shard, 3 * z.width), F32),
        sum_out=struct((z.shard, z.width), F32),
        sum_small=struct((z.shard, 128), F32),
    )
    columns = [(c, BF) for _, _, _, c in weight_pieces(z, (0, 0), (0, 0))] + [(128, F32)]
    buffers = reduce_buffers(z, columns)
    buffers.update(dict(mine=pltpu.SemaphoreType.DMA((len(columns),))))
    return ins, outs, buffers, len(columns)


def layer_back(z, values, tables, weights, first, upper):
    ups, sums, buffers, pieces = sum_parts(z, upper)

    def body(k, net):
        reduce = Reduce(net, sum_pieces(z, k), buffers_of(k, pieces), k.mine)
        late = GradMove(net, k.late, k.late_grad)
        own = [
            GradMove(net, k.gw_0, k.grad_0),
            GradMove(net, k.gw_1, k.grad_1),
            GradMove(net, k.gw_2, k.grad_2),
        ]
        at = Beside(
            rows_back=[reduce.step, late.near, late.far],
            side_back=[reduce.step],
            last_back=[own[0].far],
            back_sent=[reduce.step, own[1].far],
            back={1: [own[2].far]},
            back_out=[reduce.step],
        )
        pairs = ((k.far_gate, k.gate), (k.far_up, k.up), (k.far_kv, k.kv))
        loads = [
            pltpu.make_async_copy(far, near, k.load.at[n]) for n, (far, near) in enumerate(pairs)
        ]
        for load in loads:
            load.start()
        reduce.step()

        def wait(w):
            if w == 0:
                loads[0].wait()
                loads[1].wait()

        e = view(
            k,
            weights=(k.weight_0, k.weight_1, k.weight_2),
            gw=(k.gw_0, k.gw_1, k.gw_2),
            wait_weight=wait,
            dg=k.gate,
            du=k.up,
        )
        dm, grad_logits = experts_back(
            net, e, k.middle[...], k.grad_in[...], k.grad_logits_in[...], at
        )
        k.grad_logits[...] = grad_logits
        loads[2].wait()
        x = k.tokens[...].astype(F32)
        k.grad[...] = attend_back(net, view(k, dkv_out=k.kv), x, dm, at)
        reduce.step()
        late.wait()
        for move in own:
            move.wait((False, True))

    kept = {**attend_kept(z), **experts_kept(z)}
    far = dict(far_gate=kept.pop("gate"), far_up=kept.pop("up"), far_kv=kept.pop("kv"))
    loaded = {name[4:]: pltpu.VMEM(v.shape, v.dtype) for name, v in far.items()}
    ins = {**in_vmem(values), **in_vmem(tables), **in_vmem(weights)}
    ins.update(in_vmem({name: getattr(first, name) for name in kept}))
    ins.update(in_place({name: getattr(first, name[4:]) for name in far}))
    ins.update(in_place({**ups, **dict(late=upper.gw_2)}))
    outs = back_outputs(z, {**sums, **dict(gw_0=landing(z), gw_1=landing(z))})
    outs.update(in_place(dict(grad_2=grad_landing(z), late_grad=grad_landing(z))))
    scratch = {
        **attend_back_scratch(z, False),
        **experts_scratch(z),
        **experts_back_scratch(z, False),
        **loaded,
        **buffers,
        **dict(load=pltpu.SemaphoreType.DMA((3,))),
    }
    _, expert, back = layer_sems(z)
    count = expert + back + 4 * z.nb + pieces_sems(z, pieces)
    return launch(body, 3, z, ins, outs, scratch, count)


def reduce_last(z, lower):
    ups, sums, buffers, pieces = sum_parts(z, lower)

    def body(k, net):
        reduce = Reduce(net, sum_pieces(z, k), buffers_of(k, pieces), k.mine)
        reduce.step()
        own = [
            GradMove(net, k.gw_0, k.grad_0),
            GradMove(net, k.gw_1, k.grad_1),
            GradMove(net, k.gw_2, k.grad_2),
        ]
        for move in own:
            move.near()
        for _ in range(5):
            reduce.step()
        for move in own:
            move.wait((True, False))

    half = dict(half_0=lower.grad_0, half_1=lower.grad_1, half_2=lower.grad_2)
    ins = in_place({**ups, **dict(gw_0=lower.gw_0, gw_1=lower.gw_1, gw_2=lower.gw_2), **half})
    whole = grad_landing(z)
    outs = {**in_place(dict(grad_0=whole, grad_1=whole, grad_2=whole)), **in_vmem(sums)}
    same = list(zip(half, outs))
    return launch(body, 4, z, ins, outs, buffers, 3 * z.nb + pieces_sems(z, pieces), same)


def local(
    tokens,
    prev_logits,
    norm_gains,
    attn_in_weight,
    attn_out_weight,
    router_weight,
    const_mix,
    const_values,
    expert_gate,
    expert_up,
    expert_down,
    routes,
    order,
    cotangent,
):
    rows, width = tokens.shape
    z = Shape(lax.axis_size("head"), lax.axis_size("blk"), rows, width, expert_gate.shape[3])
    lane = np.arange(128) % (HD // 2)
    freqs = np.float32(10000.0) ** (-(2 * lane).astype(np.float32) / np.float32(HD))
    shards = dict(attn_in=attn_in_weight, attn_out=attn_out_weight)
    little = dict(
        router=jnp.transpose(router_weight, (2, 0, 1)),
        mix=jnp.transpose(const_mix, (0, 2, 1)),
        gains=norm_gains,
        consts=const_values,
        routes=jnp.transpose(routes, (0, 2, 1)),
        order=jnp.transpose(order, (0, 2, 1)),
        prev=jnp.transpose(prev_logits),
        freqs=jnp.asarray(freqs.astype(np.float32))[None],
    )
    parts = dict(expert_0=expert_gate, expert_1=expert_up, expert_2=expert_down)
    made = gather_first(z, {**shards, **parts}, little)
    tables = dict(cq=made.cq, sq=made.sq)

    def flat(v):
        return v.reshape(width, v.shape[-1])

    weights = dict(
        w_in=flat(made.w_in),
        w_out=flat(made.w_out),
        small=flat(made.small_0),
    )
    near = dict(near_0=made.near_0, near_1=made.near_1, near_2=made.near_2)
    values = dict(tokens=tokens, logits_in=made.logits, plan=made.plan_0)
    first = layer_forward(z, values, tables, weights, near, shards, parts)
    weights_1 = dict(
        w_in=flat(first.next_in),
        w_out=flat(first.next_out),
        small=flat(made.small_1),
    )
    near = dict(near_0=first.next_0, near_1=first.next_1, near_2=first.next_2)
    values = dict(
        state=first.state, logits_in=first.logits, plan=made.plan_1, cotangent=cotangent
    )
    upper = layer_both(z, values, tables, weights_1, near, parts)
    weights.update(
        dict(weight_0=first.weight_0, weight_1=first.weight_1, weight_2=first.weight_2)
    )
    values = dict(
        tokens=tokens, plan=made.plan_0, grad_in=upper.grad, grad_logits_in=upper.grad_logits
    )
    lower = layer_back(z, values, tables, weights, first, upper)
    final = reduce_last(z, lower)
    in_sum = jnp.stack([final.sum_in, lower.sum_in])
    out_sum = jnp.stack([final.sum_out, lower.sum_out])
    small_sum = jnp.stack([final.sum_small, lower.sum_small])
    expert_out = [
        jnp.stack(pair).astype(F32)
        for pair in (
            (final.grad_0, upper.grad_0),
            (final.grad_1, upper.grad_1),
            (final.grad_2, lower.late_grad),
        )
    ]
    return (
        upper.output,
        lower.grad,
        lower.grad_logits[:, :NE],
        jnp.transpose(small_sum[:, :, 16:18], (0, 2, 1)),
        in_sum,
        out_sum,
        small_sum[:, :, :NE],
        small_sum[:, :, NE : NE + 4],
        jnp.transpose(small_sum[:, :, 18:20], (0, 2, 1)),
        expert_out[0],
        expert_out[1],
        expert_out[2],
    )


def solution(mesh):
    placed = (
        P(("head", "blk"), None),
        P(("head", "blk"), None),
        P(None, None, ("head", "blk")),
        P(None, ("head", "blk"), None),
        P(None, ("head", "blk"), None),
        P(None, ("head", "blk"), None),
        P(None, ("head", "blk"), None),
        P(None, None, ("head", "blk")),
        P(None, "head", "blk", None),
        P(None, "head", "blk", None),
        P(None, "head", "blk", None),
        P(None, ("head", "blk"), None),
        P(None, ("head", "blk"), None),
        P(("head", "blk"), None),
    )
    return jax.shard_map(
        local,
        mesh=mesh,
        in_specs=placed,
        out_specs=(
            P(("head", "blk"), None),
            P(("head", "blk"), None),
            P(("head", "blk"), None),
            P(None, None, ("head", "blk")),
            P(None, ("head", "blk"), None),
            P(None, ("head", "blk"), None),
            P(None, ("head", "blk"), None),
            P(None, ("head", "blk"), None),
            P(None, None, ("head", "blk")),
            P(None, "head", "blk", None),
            P(None, "head", "blk", None),
            P(None, "head", "blk", None),
        ),
        check_vma=False,
    )
```

time: 2990 us -> 528 us (0.18)
  waiting for transfers between devices: 1500 us -> 0 us
  blocking collectives: 719 us -> 0 us
  Pallas kernels: 0 us -> 504 us
  local copies, waits for them, and re-layouts: 275 us -> 5.65 us
  matrix products: 251 us -> 0 us
  other arithmetic: 115 us -> 12 us
  starting transfers between devices: 65.5 us -> 0 us
    reduce_scatter x10 -> x0, waiting for transfers between devices: 1160 us -> none  [the longest x2 247 us: reduce_grads(): lax.psum_scatter(in_grad, ('head', 'blk'), scatter_dimension=1, tiled=True)]
    all_gather x12 -> x0, blocking collectives: 672 us -> none  [the longest x2 141 us: local(): lax.all_gather(router_weight[layer], ('head', 'blk'), axis=0, tiled=True)]
    pallas_call x0 -> x5, Pallas kernels: none -> 504 us  [launch(): pl.pallas_call(kernel, out_shape=[v[0] for v in outs.values()], in_specs=...]
    dot_general x202 -> x0, matrix products: 251 us -> none  [the longest x16 21.4 us: grad_block(): jnp.einsum(SCORE_FORM[grouped], own_queries, key_block, preferred_element...]
    all_gather x18 -> x0, waiting for transfers between devices: 208 us -> none  [the longest x2 94.1 us: local(): lax.all_gather(expert_gate[layer], 'blk', axis=1, tiled=True)]
    dynamic_slice x96 -> x0, local copies, waits for them, and re-layouts: 92.6 us -> none  [over_rows(): lax.scan(step, carry, (jnp.arange(blocks, dtype=jnp.int32), stacked))]
    unnamed x30 -> x0, waiting for transfers between devices: 78.6 us -> none
    all_to_all x18 -> x0, starting transfers between devices: 63.4 us -> none  [the longest x2 7.97 us: local(): lax.all_to_all(slot_low, 'head', split_axis=0, concat_axis=0, tiled=True)]
  transfers between devices with their start and end apart: 47 -> 0, of which waited for: 29 -> 0; matrix products, arithmetic and copies ran while one was open for 16% -> 0% of each run, Pallas kernels for 0% -> 0%
where the time goes in v2:
time: 528 us; the launch traced here: 522 us
  Pallas kernels  504 us (95%)
  other arithmetic  12 us (2%)
  local copies, waits for them, and re-layouts  5.65 us (1%)
    pallas_call x5, Pallas kernels, launch(): pl.pallas_call(kernel, out_shape=[v[0] for v in outs.values()], in_specs=...  504 us

profile of v2, /device:TPU:8, one launch (start us, length us, event | category | flops | bytes accessed | tf_op | source)
XLA Modules:
  0.0 522.4 jit_solution(3536344876250962152)
XLA Ops:
  0.6 43.3 %shard_map.238 = (bf16[2,2,2,2,2,24,2304]{6,5,4,3,2,1,0:T(8,128)(2,1)}, bf16[2,2,2,2,2,24,768]{6,5,4,3,2,1,0:T(8,128)(2,1)}, bf16[2,2,2,2,2,24,128]{6,5,4,3,2,1,...) custom-call(bf16[2,24,2304]{2,1,0:T(8,128)(2,1)} %refs_8_.3, ...), custom_call_target="tpu_custom_call" | custom-call | tf_op jit(solution)/shard_map/pallas_call | solution.py:219
  44.0 120.2 %shard_map.239 = (f32[128,768]{1,0:T(8,128)}, bf16[8,96,512]{2,1,0:T(8,128)(2,1)}, bf16[8,96,512]{2,1,0:T(8,128)(2,1)}, bf16[8,96,512]{2,1,0:T(8,128)(2,1)}, f32...) custom-call(bf16[128,768]{1,0:T(8,128)(2,1)} %refs_0_.5, ...), custom_call_target="tpu_custom_call" | custom-call | tf_op jit(solution)/shard_map/pallas_call | solution.py:219
  164.1 174.8 %shard_map.240 = (f32[128,768]{1,0:T(8,128)}, f32[128,128]{1,0:T(8,128)}, bf16[32,24,768]{2,1,0:T(8,128)(2,1)}, f32[768,128]{1,0:T(8,128)}, bf16[8,96,512]{2,1,0...) custom-call(f32[128,768]{1,0:T(8,128)} %get-tuple-element.85.refs_0_, ...), custom_call_target="tpu_custom_call" | custom-call | tf_op jit(solution)/shard_map/pallas_call | solution.py:219
  339.0 119.6 %shard_map.241 = (f32[128,768]{1,0:T(8,128)}, f32[128,128]{1,0:T(8,128)}, bf16[32,24,768]{2,1,0:T(8,128)(2,1)}, f32[768,128]{1,0:T(8,128)}, bf16[8,96,512]{2,1,0...) custom-call(bf16[128,768]{1,0:T(8,128)(2,1)} %refs_0_.5, ...), custom_call_target="tpu_custom_call" | custom-call | tf_op jit(solution)/shard_map/pallas_call | solution.py:219
  458.6 1.5 copy.30
  460.1 45.6 %shard_map.242 = (bf16[2,96,2048]{2,1,0:T(8,128)(2,1)}, bf16[2,96,2048]{2,1,0:T(8,128)(2,1)}, bf16[2,96,2048]{2,1,0:T(8,128)(2,1)}, f32[24,2304]{1,0:T(8,128)}, f32[24,768]{1,0:T(8,128)}, /*index=5*/f32[24,128]{1,0:T(8,128)}) custom-call(bf16[2,2,2,2,2,24,2304]{6,5,4,3,2,1,0:T(8,128)(2,1)} %bitcast.38, ...), custom_call_target="tpu_custom_call", output_to_operand_aliasing={{0}: (6, {}), {1}: (7, {}), {2}: (8, {})} | custom-call | tf_op jit(solution)/shard_map/pallas_call | solution.py:219
  505.8 0.0 copy-start.2
  505.8 0.0 copy-done.6
  505.8 1.8 pad_maximum_fusion
  507.6 0.0 copy-done.8
  507.6 0.7 fusion.3
  508.3 0.7 copy.32
  509.0 0.8 fusion
  509.7 0.7 copy.33
  510.4 0.9 fusion.4
  511.3 0.7 copy.34
  511.9 0.7 copy.31
  512.6 1.6 pad_maximum_fusion.1
  514.2 0.0 copy-done.2
  514.2 0.0 copy-start.4
  514.2 3.2 maximum_convert_fusion.2
  517.4 0.0 copy-done
  517.4 0.0 copy-done.1
  517.4 0.0 copy-done.3
  517.4 0.0 copy-done.4
  517.4 0.0 copy-start.7
  517.4 0.0 copy-start.5
  517.4 3.1 maximum_convert_fusion
  520.5 0.0 copy-done.7
  520.5 0.7 copy.40
  521.2 0.0 copy-done.5
  521.2 0.7 copy.41
  (5 shorter events, 0.0 us)
Async XLA Ops:
  460.1 45.7 %copy-start.6 = (f32[24,2304]{1,0:T(8,128)S(1)}, f32[24,2304]{1,0:T(8,128)}, u32[]{:S(2)}) copy-start(f32[24,2304]{1,0:T(8,128)} %get-tuple-element.129) | copy-start | bytes 663556
  460.1 47.5 %copy-start.8 = (f32[24,128]{1,0:T(8,128)S(1)}, f32[24,128]{1,0:T(8,128)}, u32[]{:S(2)}) copy-start(f32[24,128]{1,0:T(8,128)} %get-tuple-element.127) | copy-start | bytes 36868
  505.8 8.4 %copy-start.2 = (bf16[2,96,2048]{2,1,0:T(8,128)(2,1)S(1)}, bf16[2,96,2048]{2,1,0:T(8,128)(2,1)}, u32[]{:S(2)}) copy-start(bf16[2,96,2048]{2,1,0:T(8,128)(2,1)} %get-tuple-element.136) | copy-start | bytes 2359300
  514.2 3.2 copy-start
  514.2 3.2 copy-start.1
  514.2 3.2 copy-start.3
  514.2 3.2 copy-start.4
  517.4 3.1 copy-start.7
  517.4 3.8 copy-start.5

commit v3 on v2

--- a/solution.py
+++ b/solution.py
@@ -1369,8 +1369,9 @@
         at = Beside(
             start=[gather.step, far[0].start],
             sent=[gather.step, far[1].start],
+            mid=[gather.step],
             out=[gather.step],
-            rows=[far[2].start, gather.step, ahead[0].start],
+            rows=[far[2].start, ahead[0].start],
             side=[gather.step, ahead[1].start],
             last=[gather.step, ahead[2].start],
         )
@@ -1533,7 +1534,13 @@
             back={1: [own[2].far]},
             back_out=[reduce.step],
         )
-        pairs = ((k.far_gate, k.gate), (k.far_up, k.up), (k.far_kv, k.kv))
+        pairs = (
+            (k.far_gate, k.gate),
+            (k.far_up, k.up),
+            (k.far_kv, k.kv),
+            (k.far_in, k.w_in),
+            (k.far_out, k.w_out),
+        )
         loads = [
             pltpu.make_async_copy(far, near, k.load.at[n]) for n, (far, near) in enumerate(pairs)
         ]
@@ -1558,7 +1565,8 @@
             net, e, k.middle[...], k.grad_in[...], k.grad_logits_in[...], at
         )
         k.grad_logits[...] = grad_logits
-        loads[2].wait()
+        for load in loads[2:]:
+            load.wait()
         x = k.tokens[...].astype(F32)
         k.grad[...] = attend_back(net, view(k, dkv_out=k.kv), x, dm, at)
         reduce.step()
@@ -1569,10 +1577,17 @@
     kept = {**attend_kept(z), **experts_kept(z)}
     far = dict(far_gate=kept.pop("gate"), far_up=kept.pop("up"), far_kv=kept.pop("kv"))
     loaded = {name[4:]: pltpu.VMEM(v.shape, v.dtype) for name, v in far.items()}
+    weights = dict(weights)
+    large = dict(far_in=weights.pop("w_in"), far_out=weights.pop("w_out"))
+    loaded.update(
+        dict(
+            w_in=pltpu.VMEM(large["far_in"].shape, BF), w_out=pltpu.VMEM(large["far_out"].shape, BF)
+        )
+    )
     ins = {**in_vmem(values), **in_vmem(tables), **in_vmem(weights)}
     ins.update(in_vmem({name: getattr(first, name) for name in kept}))
     ins.update(in_place({name: getattr(first, name[4:]) for name in far}))
-    ins.update(in_place({**ups, **dict(late=upper.gw_2)}))
+    ins.update(in_place({**ups, **large, **dict(late=upper.gw_2)}))
     outs = back_outputs(z, {**sums, **dict(gw_0=landing(z), gw_1=landing(z))})
     outs.update(in_place(dict(grad_2=grad_landing(z), late_grad=grad_landing(z))))
     scratch = {
@@ -1581,7 +1596,7 @@
         **experts_back_scratch(z, False),
         **loaded,
         **buffers,
-        **dict(load=pltpu.SemaphoreType.DMA((3,))),
+        **dict(load=pltpu.SemaphoreType.DMA((5,))),
     }
     _, expert, back = layer_sems(z)
     count = expert + back + 4 * z.nb + pieces_sems(z, pieces)
@@ -1612,6 +1627,99 @@
     outs = {**in_place(dict(grad_0=whole, grad_1=whole, grad_2=whole)), **in_vmem(sums)}
     same = list(zip(half, outs))
     return launch(body, 4, z, ins, outs, buffers, 3 * z.nb + pieces_sems(z, pieces), same)
+
+
+def finish(z, upper, lower, final):
+    far = dict(
+        far_0=final.grad_0,
+        far_1=upper.grad_0,
+        far_2=final.grad_1,
+        far_3=upper.grad_1,
+        far_4=final.grad_2,
+        far_5=lower.late_grad,
+    )
+    given = dict(
+        output_in=upper.output,
+        grad_in=lower.grad,
+        logits_in=lower.grad_logits,
+        in_0=final.sum_in,
+        in_1=lower.sum_in,
+        out_0=final.sum_out,
+        out_1=lower.sum_out,
+        small_0=final.sum_small,
+        small_1=lower.sum_small,
+    )
+    wide = struct((LAYERS, 2, z.drow, z.hidden), F32)
+    made = dict(
+        output=struct((z.rows, z.width), BF),
+        grad=struct((z.rows, z.width), F32),
+        logits=struct((NE, z.rows), F32),
+        gains=struct((LAYERS, 2, z.shard), F32),
+        sum_in=struct((LAYERS, z.shard, 3 * z.width), F32),
+        sum_out=struct((LAYERS, z.shard, z.width), F32),
+        router=struct((NE, LAYERS, z.shard), F32),
+        mix=struct((LAYERS, 4, z.shard), F32),
+        consts=struct((LAYERS, 2, z.shard), F32),
+    )
+    large = dict(gate=wide, up=wide, down=wide)
+    ins = {**in_place(far), **in_vmem(given)}
+    outs = {**in_vmem(made), **in_place(large)}
+    scratch = dict(
+        low=pltpu.VMEM((6, 2, z.drow, z.hidden), BF),
+        high=pltpu.VMEM((6, 2, z.drow, z.hidden), F32),
+        come=pltpu.SemaphoreType.DMA((6,)),
+        go=pltpu.SemaphoreType.DMA((12,)),
+    )
+    names = list(ins) + list(outs) + list(scratch)
+
+    def body(*refs):
+        k = Names(**dict(zip(names, refs)))
+        parts = (k.far_0, k.far_1, k.far_2, k.far_3, k.far_4, k.far_5)
+        loads = [pltpu.make_async_copy(p, k.low.at[n], k.come.at[n]) for n, p in enumerate(parts)]
+        for load in loads:
+            load.start()
+        stores = []
+        for n, load in enumerate(loads):
+            load.wait()
+            whole = (k.gate, k.up, k.down)[n // 2]
+            for e in range(2):
+                k.high[n, e] = k.low[n, e].astype(F32)
+                place = whole.at[n % 2, e]
+                stores.append(pltpu.make_async_copy(k.high.at[n, e], place, k.go.at[2 * n + e]))
+                stores[-1].start()
+        k.output[...] = k.output_in[...]
+        k.grad[...] = k.grad_in[...]
+        same = eye(z.rows)
+        for n in range(NE):
+            column = k.logits_in[:, n : n + 1]
+            k.logits[n : n + 1] = jnp.sum(jnp.where(same, column, 0.0), axis=0, keepdims=True)
+        same = eye(z.shard)
+        sums = ((k.in_0, k.out_0, k.small_0), (k.in_1, k.out_1, k.small_1))
+        for layer, (sum_in, sum_out, small) in enumerate(sums):
+            k.sum_in[layer] = sum_in[...]
+            k.sum_out[layer] = sum_out[...]
+            for n in range(NE + 8):
+                row = jnp.sum(jnp.where(same, small[:, n : n + 1], 0.0), axis=0, keepdims=True)
+                if n < NE:
+                    k.router[n, layer : layer + 1] = row
+                elif n < NE + 4:
+                    k.mix[layer, n - NE : n - NE + 1] = row
+                elif n < NE + 6:
+                    k.gains[layer, n - NE - 4 : n - NE - 3] = row
+                else:
+                    k.consts[layer, n - NE - 6 : n - NE - 5] = row
+        for store in stores:
+            store.wait()
+
+    results = pl.pallas_call(
+        body,
+        out_shape=[v[0] for v in outs.values()],
+        in_specs=[v[1] for v in ins.values()],
+        out_specs=[v[1] for v in outs.values()],
+        scratch_shapes=list(scratch.values()),
+        compiler_params=pltpu.CompilerParams(vmem_limit_bytes=VMEM_BYTES),
+    )(*[v[0] for v in ins.values()])
+    return Names(**dict(zip(outs, results)))
 
 
 def local(
@@ -1678,30 +1786,20 @@
     )
     lower = layer_back(z, values, tables, weights, first, upper)
     final = reduce_last(z, lower)
-    in_sum = jnp.stack([final.sum_in, lower.sum_in])
-    out_sum = jnp.stack([final.sum_out, lower.sum_out])
-    small_sum = jnp.stack([final.sum_small, lower.sum_small])
-    expert_out = [
-        jnp.stack(pair).astype(F32)
-        for pair in (
-            (final.grad_0, upper.grad_0),
-            (final.grad_1, upper.grad_1),
-            (final.grad_2, lower.late_grad),
-        )
-    ]
+    done = finish(z, upper, lower, final)
     return (
-        upper.output,
-        lower.grad,
-        lower.grad_logits[:, :NE],
-        jnp.transpose(small_sum[:, :, 16:18], (0, 2, 1)),
-        in_sum,
-        out_sum,
-        small_sum[:, :, :NE],
-        small_sum[:, :, NE : NE + 4],
-        jnp.transpose(small_sum[:, :, 18:20], (0, 2, 1)),
-        expert_out[0],
-        expert_out[1],
-        expert_out[2],
+        done.output,
+        done.grad,
+        jnp.transpose(done.logits),
+        done.gains,
+        done.sum_in,
+        done.sum_out,
+        jnp.transpose(done.router, (1, 2, 0)),
+        jnp.transpose(done.mix, (0, 2, 1)),
+        done.consts,
+        done.gate,
+        done.up,
+        done.down,
     )
 
 

time: 528 us -> 513 us (0.972)
  other arithmetic: 12 us -> 0 us
  local copies, waits for them, and re-layouts: 5.65 us -> 0 us
    pallas_call x0 -> x1, Pallas kernels: none -> 7.31 us  [finish(): pl.pallas_call(body, out_shape=[v[0] for v in outs.values()], in_specs=[v...]
    convert_element_type x2 -> x0, other arithmetic: 6.26 us -> none  [local(): jnp.stack(pair).astype(F32)]
    unnamed x25 -> x0, local copies, waits for them, and re-layouts: 5.65 us -> none
where the time goes in v3:
time: 513 us; the launch traced here: 507 us
  Pallas kernels  506 us (99%)
    pallas_call x5, Pallas kernels, launch(): pl.pallas_call(kernel, out_shape=[v[0] for v in outs.values()], in_specs=...  499 us

profile of v3, /device:TPU:8, one launch (start us, length us, event | category | flops | bytes accessed | tf_op | source)
XLA Modules:
  0.0 507.3 jit_solution(6988181141924315787)
XLA Ops:
  0.6 43.3 %shard_map.238 = (bf16[2,2,2,2,2,24,2304]{6,5,4,3,2,1,0:T(8,128)(2,1)}, bf16[2,2,2,2,2,24,768]{6,5,4,3,2,1,0:T(8,128)(2,1)}, bf16[2,2,2,2,2,24,128]{6,5,4,3,2,1,...) custom-call(bf16[2,24,2304]{2,1,0:T(8,128)(2,1)} %refs_8_.3, ...), custom_call_target="tpu_custom_call" | custom-call | tf_op jit(solution)/shard_map/pallas_call | solution.py:219
  44.0 115.3 %shard_map.239 = (f32[128,768]{1,0:T(8,128)}, bf16[8,96,512]{2,1,0:T(8,128)(2,1)}, bf16[8,96,512]{2,1,0:T(8,128)(2,1)}, bf16[8,96,512]{2,1,0:T(8,128)(2,1)}, f32...) custom-call(bf16[128,768]{1,0:T(8,128)(2,1)} %refs_0_.5, ...), custom_call_target="tpu_custom_call" | custom-call | tf_op jit(solution)/shard_map/pallas_call | solution.py:219
  159.3 175.7 %shard_map.240 = (f32[128,768]{1,0:T(8,128)}, f32[128,128]{1,0:T(8,128)}, bf16[32,24,768]{2,1,0:T(8,128)(2,1)}, f32[768,128]{1,0:T(8,128)}, bf16[8,96,512]{2,1,0...) custom-call(f32[128,768]{1,0:T(8,128)} %get-tuple-element.97.refs_0_, ...), custom_call_target="tpu_custom_call" | custom-call | tf_op jit(solution)/shard_map/pallas_call | solution.py:219
  335.0 118.8 %shard_map.241 = (f32[128,768]{1,0:T(8,128)}, f32[128,128]{1,0:T(8,128)}, bf16[32,24,768]{2,1,0:T(8,128)(2,1)}, f32[768,128]{1,0:T(8,128)}, bf16[8,96,512]{2,1,0...) custom-call(bf16[128,768]{1,0:T(8,128)(2,1)} %refs_0_.5, ...), custom_call_target="tpu_custom_call" | custom-call | tf_op jit(solution)/shard_map/pallas_call | solution.py:219
  453.8 45.8 %shard_map.242 = (bf16[2,96,2048]{2,1,0:T(8,128)(2,1)}, bf16[2,96,2048]{2,1,0:T(8,128)(2,1)}, bf16[2,96,2048]{2,1,0:T(8,128)(2,1)}, f32[24,2304]{1,0:T(8,128)}, f32[24,768]{1,0:T(8,128)}, /*index=5*/f32[24,128]{1,0:T(8,128)}) custom-call(bf16[2,2,2,2,2,24,2304]{6,5,4,3,2,1,0:T(8,128)(2,1)} %bitcast.24, ...), custom_call_target="tpu_custom_call", output_to_operand_aliasing={{0}: (6, {}), {1}: (7, {}), {2}: (8, {})} | custom-call | tf_op jit(solution)/shard_map/pallas_call | solution.py:219
  499.6 7.3 %shard_map.243 = (bf16[128,768]{1,0:T(8,128)(2,1)}, f32[128,768]{1,0:T(8,128)}, f32[12,128]{1,0:T(8,128)}, f32[2,2,24]{2,1,0:T(2,128)}, f32[2,24,2304]{2,1,0:T(8...) custom-call(bf16[2,96,2048]{2,1,0:T(8,128)(2,1)} %get-tuple-element., ...), custom_call_target="tpu_custom_call" | custom-call | tf_op jit(solution)/shard_map/pallas_call | solution.py:1714

commit v4 on v3

--- a/solution.py
+++ b/solution.py
@@ -829,7 +829,7 @@
             if k == 0:
                 while_first()
 
-    def compute(self):
+    def compute(self, before_side=None):
         net, z, e = self.net, self.net.z, self.e
         block = (z.experts, SLOT, z.width)
         e.base[...] = self.chunk(net.q).reshape(block)
@@ -855,6 +855,8 @@
             net.sent = [made for made in net.sent if made is not to_core]
             to_core.wait_send()
             e.part[ds] = (kept.reshape(block) + e.got[ds].astype(F32)).astype(BF)
+            if before_side is not None and ds == 1:
+                before_side()
             for dy in reversed(range(z.hh)):
                 span = pl.ds(net.up(net.y, dy, z.hh) * GROUPS, GROUPS)
                 device = net.near(ds=z.splits - ds)
@@ -1086,8 +1088,7 @@
     back.send()
     mixing.weigh()
     run.relay(lambda: None)
-    run.compute()
-    back.relay(lambda: None)
+    run.compute(lambda: back.relay(lambda: None))
     back.compute()
     run.give_back()
     weight_grads(net, e)
@@ -1370,14 +1371,16 @@
             start=[gather.step, far[0].start],
             sent=[gather.step, far[1].start],
             mid=[gather.step],
-            out=[gather.step],
-            rows=[far[2].start, ahead[0].start],
+            out=[far[2].start],
+            rows=[ahead[0].start],
             side=[gather.step, ahead[1].start],
-            last=[gather.step, ahead[2].start],
+            last=[ahead[2].start],
         )
         middle = attend(net, k, k.tokens[...].astype(F32), at)
         e = view(k, weights=(k.weight_0, k.weight_1, k.weight_2), wait_weight=waiting(*far))
         k.state[...] = experts(net, e, middle, k.logits_in[...], at)
+        gather.step()
+        gather.step()
         for move in ahead:
             move.wait()
 
@@ -1432,7 +1435,7 @@
         at = Beside(
             start=[far[0].start],
             sent=[far[1].start],
-            rows=[far[2].start],
+            out=[far[2].start],
             side_back=[grads[0].near],
             last_back=[grads[0].far],
             back_sent=[grads[1].near],
@@ -1527,8 +1530,8 @@
             GradMove(net, k.gw_2, k.grad_2),
         ]
         at = Beside(
-            rows_back=[reduce.step, late.near, late.far],
-            side_back=[reduce.step],
+            rows_back=[reduce.step, late.near],
+            side_back=[reduce.step, late.far],
             last_back=[own[0].far],
             back_sent=[reduce.step, own[1].far],
             back={1: [own[2].far]},

time: 513 us -> 498 us (0.971)
  Pallas kernels: 506 us -> 491 us
    pallas_call x5, Pallas kernels: 499 us -> 484 us  [launch(): pl.pallas_call(kernel, out_shape=[v[0] for v in outs.values()], in_specs=...]
where the time goes in v4:
time: 498 us; the launch traced here: 492 us
  Pallas kernels  491 us (99%)
    pallas_call x5, Pallas kernels, launch(): pl.pallas_call(kernel, out_shape=[v[0] for v in outs.values()], in_specs=...  484 us

profile of v4, /device:TPU:8, one launch (start us, length us, event | category | flops | bytes accessed | tf_op | source)
XLA Modules:
  0.0 492.1 jit_solution(887617982788710574)
XLA Ops:
  0.6 43.3 %shard_map.238 = (bf16[2,2,2,2,2,24,2304]{6,5,4,3,2,1,0:T(8,128)(2,1)}, bf16[2,2,2,2,2,24,768]{6,5,4,3,2,1,0:T(8,128)(2,1)}, bf16[2,2,2,2,2,24,128]{6,5,4,3,2,1,...) custom-call(bf16[2,24,2304]{2,1,0:T(8,128)(2,1)} %refs_8_.3, ...), custom_call_target="tpu_custom_call" | custom-call | tf_op jit(solution)/shard_map/pallas_call | solution.py:219
  44.0 113.0 %shard_map.239 = (f32[128,768]{1,0:T(8,128)}, bf16[8,96,512]{2,1,0:T(8,128)(2,1)}, bf16[8,96,512]{2,1,0:T(8,128)(2,1)}, bf16[8,96,512]{2,1,0:T(8,128)(2,1)}, f32...) custom-call(bf16[128,768]{1,0:T(8,128)(2,1)} %refs_0_.5, ...), custom_call_target="tpu_custom_call" | custom-call | tf_op jit(solution)/shard_map/pallas_call | solution.py:219
  156.9 163.1 %shard_map.240 = (f32[128,768]{1,0:T(8,128)}, f32[128,128]{1,0:T(8,128)}, bf16[32,24,768]{2,1,0:T(8,128)(2,1)}, f32[768,128]{1,0:T(8,128)}, bf16[8,96,512]{2,1,0...) custom-call(f32[128,768]{1,0:T(8,128)} %get-tuple-element.97.refs_0_, ...), custom_call_target="tpu_custom_call" | custom-call | tf_op jit(solution)/shard_map/pallas_call | solution.py:219
  320.1 117.6 %shard_map.241 = (f32[128,768]{1,0:T(8,128)}, f32[128,128]{1,0:T(8,128)}, bf16[32,24,768]{2,1,0:T(8,128)(2,1)}, f32[768,128]{1,0:T(8,128)}, bf16[8,96,512]{2,1,0...) custom-call(bf16[128,768]{1,0:T(8,128)(2,1)} %refs_0_.5, ...), custom_call_target="tpu_custom_call" | custom-call | tf_op jit(solution)/shard_map/pallas_call | solution.py:219
  437.6 46.7 %shard_map.242 = (bf16[2,96,2048]{2,1,0:T(8,128)(2,1)}, bf16[2,96,2048]{2,1,0:T(8,128)(2,1)}, bf16[2,96,2048]{2,1,0:T(8,128)(2,1)}, f32[24,2304]{1,0:T(8,128)}, f32[24,768]{1,0:T(8,128)}, /*index=5*/f32[24,128]{1,0:T(8,128)}) custom-call(bf16[2,2,2,2,2,24,2304]{6,5,4,3,2,1,0:T(8,128)(2,1)} %bitcast.24, ...), custom_call_target="tpu_custom_call", output_to_operand_aliasing={{0}: (6, {}), {1}: (7, {}), {2}: (8, {})} | custom-call | tf_op jit(solution)/shard_map/pallas_call | solution.py:219
  484.3 7.3 %shard_map.243 = (bf16[128,768]{1,0:T(8,128)(2,1)}, f32[128,768]{1,0:T(8,128)}, f32[12,128]{1,0:T(8,128)}, f32[2,2,24]{2,1,0:T(2,128)}, f32[2,24,2304]{2,1,0:T(8...) custom-call(bf16[2,96,2048]{2,1,0:T(8,128)(2,1)} %get-tuple-element., ...), custom_call_target="tpu_custom_call" | custom-call | tf_op jit(solution)/shard_map/pallas_call | solution.py:1717

commit v5 on v4

--- a/solution.py
+++ b/solution.py
@@ -1207,7 +1207,7 @@
     pass
 
 
-CUT = 384
+CUT = 256
 
 
 def in_vmem(arrays):

time: 498 us -> 498 us (level)
  no operation moved by 1% of the time
where the time goes in v5:
time: 498 us; the launch traced here: 493 us
  Pallas kernels  491 us (99%)
    pallas_call x5, Pallas kernels, launch(): pl.pallas_call(kernel, out_shape=[v[0] for v in outs.values()], in_specs=...  484 us

profile of v5, /device:TPU:8, one launch (start us, length us, event | category | flops | bytes accessed | tf_op | source)
XLA Modules:
  0.0 492.5 jit_solution(8130267181715208186)
XLA Ops:
  0.6 43.9 %shard_map.238 = (bf16[2,2,2,2,2,24,2304]{6,5,4,3,2,1,0:T(8,128)(2,1)}, bf16[2,2,2,2,2,24,768]{6,5,4,3,2,1,0:T(8,128)(2,1)}, bf16[2,2,2,2,2,24,128]{6,5,4,3,2,1,...) custom-call(bf16[2,24,2304]{2,1,0:T(8,128)(2,1)} %refs_8_.3, ...), custom_call_target="tpu_custom_call" | custom-call | tf_op jit(solution)/shard_map/pallas_call | solution.py:219
  44.5 113.0 %shard_map.239 = (f32[128,768]{1,0:T(8,128)}, bf16[8,96,512]{2,1,0:T(8,128)(2,1)}, bf16[8,96,512]{2,1,0:T(8,128)(2,1)}, bf16[8,96,512]{2,1,0:T(8,128)(2,1)}, f32...) custom-call(bf16[128,768]{1,0:T(8,128)(2,1)} %refs_0_.5, ...), custom_call_target="tpu_custom_call" | custom-call | tf_op jit(solution)/shard_map/pallas_call | solution.py:219
  157.5 163.0 %shard_map.240 = (f32[128,768]{1,0:T(8,128)}, f32[128,128]{1,0:T(8,128)}, bf16[32,24,768]{2,1,0:T(8,128)(2,1)}, f32[768,128]{1,0:T(8,128)}, bf16[8,96,512]{2,1,0...) custom-call(f32[128,768]{1,0:T(8,128)} %get-tuple-element.97.refs_0_, ...), custom_call_target="tpu_custom_call" | custom-call | tf_op jit(solution)/shard_map/pallas_call | solution.py:219
  320.5 118.2 %shard_map.241 = (f32[128,768]{1,0:T(8,128)}, f32[128,128]{1,0:T(8,128)}, bf16[32,24,768]{2,1,0:T(8,128)(2,1)}, f32[768,128]{1,0:T(8,128)}, bf16[8,96,512]{2,1,0...) custom-call(bf16[128,768]{1,0:T(8,128)(2,1)} %refs_0_.5, ...), custom_call_target="tpu_custom_call" | custom-call | tf_op jit(solution)/shard_map/pallas_call | solution.py:219
  438.7 46.1 %shard_map.242 = (bf16[2,96,2048]{2,1,0:T(8,128)(2,1)}, bf16[2,96,2048]{2,1,0:T(8,128)(2,1)}, bf16[2,96,2048]{2,1,0:T(8,128)(2,1)}, f32[24,2304]{1,0:T(8,128)}, f32[24,768]{1,0:T(8,128)}, /*index=5*/f32[24,128]{1,0:T(8,128)}) custom-call(bf16[2,2,2,2,2,24,2304]{6,5,4,3,2,1,0:T(8,128)(2,1)} %bitcast.24, ...), custom_call_target="tpu_custom_call", output_to_operand_aliasing={{0}: (6, {}), {1}: (7, {}), {2}: (8, {})} | custom-call | tf_op jit(solution)/shard_map/pallas_call | solution.py:219
  484.8 7.3 %shard_map.243 = (bf16[128,768]{1,0:T(8,128)(2,1)}, f32[128,768]{1,0:T(8,128)}, f32[12,128]{1,0:T(8,128)}, f32[2,2,24]{2,1,0:T(2,128)}, f32[2,24,2304]{2,1,0:T(8...) custom-call(bf16[2,96,2048]{2,1,0:T(8,128)(2,1)} %get-tuple-element., ...), custom_call_target="tpu_custom_call" | custom-call | tf_op jit(solution)/shard_map/pallas_call | solution.py:1717
